TPU v7x, 256 devices: a whole 4x4x8 slice. The times are simulated.
256 devices in a mesh: row: 16 (over y, z_hi, core), col: 16 (over x, z_lo).
Axes of the slice: x: 4, y: 4, z: 8 (z_hi: 2, z_lo: 4; z = z_hi * 4 + z_lo), core: 2. Of those that a mesh axis runs over, the one named last changes fastest.
Arguments:
- vectors: float32 [16, 393216], P(None, ('row', 'col')), may hold values from -6 to 6
- tiles: float32 [16, 16, 48, 256, 256], P('row', 'col'), may hold values from -0.375 to 0.375
- tile_rows: int32 [16, 16, 48], P('row', 'col'), may hold values from 0 to 95, as said below
- tile_cols: int32 [16, 16, 48], P('row', 'col'), may hold values from 0 to 95, as said below
- counts: int32 [16, 16], P('row', 'col'), may hold values from 6 to 48, as said below
Outputs:
- residual: float32 [16, 393216], P(None, ('row', 'col'))
- image: float32 [16, 393216], P(None, ('row', 'col'))
- gram: float32 [16, 16], replicated
Inputs may be any that keep to these rules, and one draw needn't show every extreme that they name: Within one cell the slots name distinct tile positions. The live slots of one cell name at most 3 distinct block rows within any one segment (tile_rows // 6 equal), and every cell has a segment with exactly 3. The live slots of one cell name at most 3 distinct block columns within any one segment (tile_cols // 6 equal), and every cell has a segment with exactly 3. `counts`: some cell holds all 48 slots live in every draw; slots at or above a cell's count hold unused tiles.
All inputs are finite; a program needn't handle non-finite values.
Results may differ from a plain program's by a relative error of at most 0.0001.
Values sent between devices are 32-bit elements; how exact they have to be, the bound alone decides.
No kernel may reach another device: no remote copies, remote signals or barrier semaphores. Data moves between devices by JAX's collectives and lax.ppermute only.
A program may use at most 64 MiB of HBM per device.

v0:
```python
import jax
import jax.numpy as jnp
from jax import lax
from jax.sharding import PartitionSpec as P

TILE = 256


def local_products(cell_tiles, row_pick, col_pick, row_group, col_group):
    width = row_group.shape[0]
    row_blocks = row_group.reshape(width, row_pick.shape[1], TILE)
    col_blocks = col_group.reshape(width, col_pick.shape[1], TILE)
    from_rows = jnp.einsum("kg,vgj->vkj", row_pick, row_blocks, precision=lax.Precision.HIGHEST)
    from_cols = jnp.einsum("kg,vgj->vkj", col_pick, col_blocks, precision=lax.Precision.HIGHEST)
    to_rows = jnp.einsum("kij,vkj->vki", cell_tiles, from_cols, precision=lax.Precision.HIGHEST)
    to_cols = jnp.einsum("kij,vki->vkj", cell_tiles, from_rows, precision=lax.Precision.HIGHEST)
    row_terms = jnp.einsum("kg,vki->vgi", row_pick, to_rows, precision=lax.Precision.HIGHEST)
    col_terms = jnp.einsum("kg,vkj->vgj", col_pick, to_cols, precision=lax.Precision.HIGHEST)
    return (row_terms, col_terms)


def reduce_rows(row_terms):
    width = row_terms.shape[0]
    return lax.psum_scatter(row_terms.reshape(width, -1), "col", scatter_dimension=1, tiled=True)


def reduce_columns(col_terms):
    width = col_terms.shape[0]
    return lax.psum_scatter(col_terms.reshape(width, -1), "row", scatter_dimension=1, tiled=True)


def apply_whole(block, cell_tiles, row_pick, col_pick):
    row_group = lax.all_gather(block, "col", axis=1, tiled=True)
    col_group = lax.all_gather(block, "row", axis=1, tiled=True)
    row_terms, col_terms = local_products(cell_tiles, row_pick, col_pick, row_group, col_group)
    return reduce_rows(row_terms) + reduce_columns(col_terms)


def apply_hamiltonian(block, cell_tiles, row_pick, col_pick):
    return apply_whole(block, cell_tiles, row_pick, col_pick)


def per_device(vectors, tiles, tile_rows, tile_cols, counts):
    cell_tiles = tiles[0, 0]
    rows = tile_rows[0, 0]
    cols = tile_cols[0, 0]
    segment_blocks = vectors.shape[1] // TILE
    row_span = lax.axis_size("col") * segment_blocks
    col_span = lax.axis_size("row") * segment_blocks
    order_total = vectors.shape[1] * lax.axis_size("row") * lax.axis_size("col")
    alive = (jnp.arange(rows.shape[0], dtype=jnp.int32) < counts[0, 0]).astype(jnp.float32)
    row_pick = (rows[:, None] == jnp.arange(row_span, dtype=jnp.int32)[None, :]).astype(
        jnp.float32
    ) * alive[:, None]
    col_pick = (cols[:, None] == jnp.arange(col_span, dtype=jnp.int32)[None, :]).astype(
        jnp.float32
    ) * alive[:, None]
    product = apply_hamiltonian(vectors, cell_tiles, row_pick, col_pick)
    local_correlation = jnp.einsum("vn,wn->vw", vectors, vectors, precision=lax.Precision.HIGHEST)
    local_projection = jnp.einsum("vn,wn->vw", vectors, product, precision=lax.Precision.HIGHEST)
    correlation, projection = lax.psum((local_correlation, local_projection), ("row", "col"))
    factor = jnp.linalg.cholesky(correlation)
    coeffs = jax.scipy.linalg.cho_solve((factor, True), projection)
    residual = product - jnp.einsum("wv,wn->vn", coeffs, vectors, precision=lax.Precision.HIGHEST)
    image = apply_hamiltonian(residual, cell_tiles, row_pick, col_pick)
    local_gram = jnp.einsum("vn,wn->vw", residual, image, precision=lax.Precision.HIGHEST)
    gram = lax.psum(local_gram, ("row", "col")) / order_total
    return (residual, image, gram)


def solution(mesh):
    in_specs = (
        P(None, ("row", "col")),
        P("row", "col", None, None, None),
        P("row", "col", None),
        P("row", "col", None),
        P("row", "col"),
    )
    out_specs = (P(None, ("row", "col")), P(None, ("row", "col")), P())
    return jax.shard_map(
        per_device, mesh=mesh, in_specs=in_specs, out_specs=out_specs, check_vma=False
    )
```

profile of v0, /device:TPU:1, one launch (start us, length us, event | category | flops | bytes accessed | tf_op | source)
XLA Modules:
  0.0 809.2 jit_solution(5120501601112097085)
XLA Ops:
  9.4 79.7 %all-gather.7.cloned.1.call-done = f32[16,24576]{1,0:T(8,128)} async-done(((f32[16,1536]{1,0:T(8,128)}), f32[16,24576]{1,0:T(8,128)}) %all-gather.7.cloned.1.call-update) | async-done | bytes 1572880 | tf_op jit(solution)/shard_map/all_gather | solution.py:33
  89.0 1.9 copy.25
  91.9 9.3 %fusion.11 = f32[16,48,256]{2,0,1:T(8,128)S(1)} fusion(f32[1,1,48,256,256]{4,3,2,1,0:T(8,128)} %param.6, f32[16,48,256]{2,1,0:T(8,128)S(1)} %convolution_bitcast_fusion.2), kind=kOutput, calls=%fused_computation.10 | convolution fusion | flops 603979776 | bytes 14155776 | tf_op jit(solution)/shard_map/kij,vki->vkj/dot_general | solution.py:16
  101.2 1.9 fusion.26
  103.2 2.1 copy.26
  105.5 54.4 %all-gather.5.cloned.1.call-done = f32[16,24576]{1,0:T(8,128)} async-done(((f32[16,1536]{1,0:T(8,128)}), f32[16,24576]{1,0:T(8,128)}) %all-gather.5.cloned.1.call-update) | async-done | bytes 1572880 | tf_op jit(solution)/shard_map/all_gather | solution.py:34
  159.9 1.9 copy.23
  162.7 13.6 %fusion.8 = f32[16,48,256]{2,0,1:T(8,128)S(1)} fusion(f32[1,1,48,256,256]{4,3,2,1,0:T(8,128)} %param.6, f32[16,48,256]{2,1,0:T(8,128)S(1)} %convolution_bitcast_fusion.3), kind=kOutput, calls=%fused_computation.9 | convolution fusion | flops 603979776 | bytes 14155776 | tf_op jit(solution)/shard_map/kij,vkj->vki/dot_general | solution.py:15
  176.3 1.9 fusion.29
  178.2 2.1 copy.24
  181.4 60.3 %reduce-scatter.7.cloned.1.call-done = f32[16,1536]{1,0:T(8,128)} async-done(((f32[16,24576]{1,0:T(8,128)}), f32[16,1536]{1,0:T(8,128)}) %reduce-scatter.7.cloned.1.call-update) | async-done | bytes 98320 | tf_op jit(solution)/shard_map/reduce_scatter | solution.py:29
  241.6 78.6 %reduce-scatter.5.cloned.1.call-done = f32[16,1536]{1,0:T(8,128)} async-done(((f32[16,24576]{1,0:T(8,128)}), f32[16,1536]{1,0:T(8,128)}) %reduce-scatter.5.cloned.1.call-update) | async-done | bytes 98320 | tf_op jit(solution)/shard_map/reduce_scatter | solution.py:24
  320.2 1.0 add.35
  321.4 84.7 %all-reduce = (f32[16,16]{0,1:T(8,128)S(1)}, f32[16,16]{0,1:T(8,128)S(1)}) all-reduce(f32[16,16]{0,1:T(8,128)S(1)} %convolution_bitcast_fusion.4, f32[16,16]{0,1:T(8,128)S(1)} %fusion.86), channel_id=1, replica_groups=mesh['row'=16,'col'=16] {'row','col'}, use_global_device_ids=true, to_apply=%region_5.6 | all-reduce | flops 512 | bytes 4096 | tf_op jit(solution)/shard_map/psum | solution.py:61
  406.2 1.5 cholesky.16
  409.0 1.2 custom-call.10
  412.3 70.5 %all-gather.11.cloned.1.call-done = f32[16,24576]{1,0:T(8,128)} async-done(((f32[16,1536]{1,0:T(8,128)}), f32[16,24576]{1,0:T(8,128)}) %all-gather.11.cloned.1.call-update) | async-done | bytes 1572880 | tf_op jit(solution)/shard_map/all_gather | solution.py:33
  482.9 1.9 copy.29
  484.8 1.0 convolution_bitcast_fusion
  485.8 9.3 %fusion.17 = f32[16,48,256]{2,0,1:T(8,128)S(1)} fusion(f32[1,1,48,256,256]{4,3,2,1,0:T(8,128)} %param.6, f32[16,48,256]{2,1,0:T(8,128)S(1)} %convolution_bitcast_fusion), kind=kOutput, calls=%fused_computation.12 | convolution fusion | flops 603979776 | bytes 14155776 | tf_op jit(solution)/shard_map/kij,vki->vkj/dot_general | solution.py:16
  495.2 1.9 fusion.20
  497.1 2.1 copy.30
  499.5 55.1 %all-gather.9.cloned.1.call-done = f32[16,24576]{1,0:T(8,128)} async-done(((f32[16,1536]{1,0:T(8,128)}), f32[16,24576]{1,0:T(8,128)}) %all-gather.9.cloned.1.call-update) | async-done | bytes 1572880 | tf_op jit(solution)/shard_map/all_gather | solution.py:34
  554.6 1.9 copy.27
  556.4 1.0 convolution_bitcast_fusion.1
  557.5 13.6 %fusion.14 = f32[16,48,256]{2,0,1:T(8,128)S(1)} fusion(f32[1,1,48,256,256]{4,3,2,1,0:T(8,128)} %param.6, f32[16,48,256]{2,1,0:T(8,128)S(1)} %convolution_bitcast_fusion.1), kind=kOutput, calls=%fused_computation.11 | convolution fusion | flops 603979776 | bytes 14155776 | tf_op jit(solution)/shard_map/kij,vkj->vki/dot_general | solution.py:15
  571.1 1.9 fusion.23
  573.0 2.1 copy.28
  575.1 61.8 %reduce-scatter.11.cloned.1.call-done = f32[16,1536]{1,0:T(8,128)} async-done(((f32[16,24576]{1,0:T(8,128)}), f32[16,1536]{1,0:T(8,128)}) %reduce-scatter.11.cloned.1.call-update) | async-done | bytes 98320 | tf_op jit(solution)/shard_map/reduce_scatter | solution.py:29
  636.9 79.0 %reduce-scatter.9.cloned.1.call-done = f32[16,1536]{1,0:T(8,128)} async-done(((f32[16,24576]{1,0:T(8,128)}), f32[16,1536]{1,0:T(8,128)}) %reduce-scatter.9.cloned.1.call-update) | async-done | bytes 98320 | tf_op jit(solution)/shard_map/reduce_scatter | solution.py:24
  715.8 1.0 add.37
  717.0 84.3 %psum.23 = f32[16,16]{1,0:T(8,128)S(1)} all-reduce(f32[16,16]{1,0:T(8,128)S(1)} %fusion.87), channel_id=1, replica_groups=mesh['row'=16,'col'=16] {'row','col'}, use_global_device_ids=true, to_apply=%region_8.9 | all-reduce | flops 256 | bytes 2048 | tf_op jit(solution)/shard_map/psum | solution.py:67
  (41 shorter events, 9.5 us)
Async XLA Ops:
  7.2 81.9 %all-gather.7.cloned.1.call-start = ((), (), s32[]{:S(2)}) async-start(), calls=%async_computation.6 | async-start | bytes 1671168 | tf_op jit(solution)/shard_map/all_gather | solution.py:33
  7.9 152.0 %all-gather.5.cloned.1.call-start = ((), (), s32[]{:S(2)}) async-start(), calls=%async_computation.4 | async-start | bytes 1671168 | tf_op jit(solution)/shard_map/all_gather | solution.py:34
  8.7 233.0 %reduce-scatter.7.cloned.1.call-start = ((), (), s32[]{:S(2)}) async-start(), calls=%async_computation.7 | async-start | bytes 1671168 | tf_op jit(solution)/shard_map/reduce_scatter | solution.py:29
  89.0 1.9 copy-start.4
  91.9 9.4 %copy-start.3 = (s32[1,1,48]{2,1,0:T(1,128)S(1)}, s32[1,1,48]{2,1,0:T(1,128)}, u32[]{:S(2)}) copy-start(s32[1,1,48]{2,1,0:T(1,128)} %param.8) | copy-start | bytes 580
  105.2 215.0 %reduce-scatter.5.cloned.1.call-start = ((), (), s32[]{:S(2)}) async-start(), calls=%async_computation.5 | async-start | bytes 1671168 | tf_op jit(solution)/shard_map/reduce_scatter | solution.py:24
  180.3 0.9 copy-start
  180.3 302.6 %all-gather.11.cloned.1.call-start = ((), (), s32[]{:S(2)}) async-start(), calls=%async_computation.10 | async-start | bytes 1671168 | tf_op jit(solution)/shard_map/all_gather | solution.py:33
  411.5 143.1 %all-gather.9.cloned.1.call-start = ((), (), s32[]{:S(2)}) async-start(), calls=%async_computation.8 | async-start | bytes 1671168 | tf_op jit(solution)/shard_map/all_gather | solution.py:34
  412.1 224.8 %reduce-scatter.11.cloned.1.call-start = ((), (), s32[]{:S(2)}) async-start(), calls=%async_computation.11 | async-start | bytes 1671168 | tf_op jit(solution)/shard_map/reduce_scatter | solution.py:29
  499.2 216.7 %reduce-scatter.9.cloned.1.call-start = ((), (), s32[]{:S(2)}) async-start(), calls=%async_computation.9 | async-start | bytes 1671168 | tf_op jit(solution)/shard_map/reduce_scatter | solution.py:24
  575.1 141.7 %copy-start.1 = (f32[16,1536]{1,0:T(8,128)S(1)}, f32[16,1536]{1,0:T(8,128)}, u32[]{:S(2)}) copy-start(f32[16,1536]{1,0:T(8,128)} %convolution_subtract_fusion) | copy-start | bytes 294916
  716.8 85.1 %copy-start.2 = (f32[16,1536]{1,0:T(8,128)}, f32[16,1536]{1,0:T(8,128)S(1)}, u32[]{:S(2)}) copy-start(f32[16,1536]{1,0:T(8,128)S(1)} %add.37) | copy-start | bytes 294916
Sparse Core Ops, SparseCore 0:
  9.8 79.2 all-gather.6
  91.8 68.0 all-gather.4
  164.1 77.5 reduce-scatter.6
  244.0 76.1 reduce-scatter.4
  411.6 71.2 all-gather.10
  486.5 68.0 all-gather.8
  559.3 77.5 reduce-scatter.10
  639.6 76.2 reduce-scatter.8
where the time goes:
time: 815 us; the launch traced here: 809 us
  waiting for transfers between devices  541 us (66%)
  blocking collectives  169 us (21%)
  matrix products  59.3 us (7%)
  local copies, waits for them, and re-layouts  16.7 us (2%)
  between operations  15.4 us (2%)
    reduce_scatter x2, waiting for transfers between devices, reduce_rows(): lax.psum_scatter(row_terms.reshape(width, -1), 'col', scatter_dimension=1...  158 us
    all_gather x2, waiting for transfers between devices, apply_whole(): row_group = lax.all_gather(block, 'col', axis=1, tiled=True)  150 us
    reduce_scatter x2, waiting for transfers between devices, reduce_columns(): lax.psum_scatter(col_terms.reshape(width, -1), 'row', scatter_dimension=1...  122 us
    all_gather x2, waiting for transfers between devices, apply_whole(): col_group = lax.all_gather(block, 'row', axis=1, tiled=True)  110 us
    psum x1, blocking collectives, per_device(): lax.psum((local_correlation, local_projection), ('row', 'col'))  84.7 us
    psum x1, blocking collectives, per_device(): gram = lax.psum(local_gram, ('row', 'col')) / order_total  84.3 us
    dot_general x2, matrix products, local_products(): jnp.einsum('kij,vkj->vki', cell_tiles, from_cols, precision=lax.Precision...  27.2 us
    dot_general x2, matrix products, local_products(): jnp.einsum('kij,vki->vkj', cell_tiles, from_rows, precision=lax.Precision...  18.7 us
  transfers between devices with their start and end apart: 8, of which 8 were waited for; matrix products, arithmetic and copies ran while one was open for 9% of the time, Pallas kernels for 0%

commit v1 on v0

v1 whole, which is shorter than its diff:
```python
import jax
import jax.numpy as jnp
from jax import lax
from jax.experimental import pallas as pl
from jax.experimental.pallas import tpu as pltpu
from jax.sharding import PartitionSpec as P


NV = 16
TILE = 256
SEGB = 6
CAP = 3
SEG = SEGB * NV
RID = 8
F32 = jnp.float32
BF16 = jnp.bfloat16
HIGH = lax.Precision.HIGHEST
VMEM_LIMIT = 48 * 1024 * 1024


def vspec():
    return pl.BlockSpec(memory_space=pltpu.VMEM)


def sspec():
    return pl.BlockSpec(memory_space=pltpu.SMEM)


def params():
    return pltpu.CompilerParams(vmem_limit_bytes=VMEM_LIMIT)


def row_shift(step):
    return [(i, (i // 4 + step) % 4 * 4 + i % 4) for i in range(16)]


OTHER_HALF = [(i, i ^ 2) for i in range(16)]
OTHER_CORE = [(i, i ^ 1) for i in range(16)]


def prep_kernel(place, rows, cols, counts, vectors, seg, table, slots, mark, used):
    n_segs = table.shape[0]

    def clear(b, _):
        mark[b] = -1
        return 0

    lax.fori_loop(0, n_segs * SEGB, clear, 0)

    def clear_table(s, _):
        used[s] = 0
        for q in range(CAP):
            table[s, q] = 0
        return 0

    lax.fori_loop(0, n_segs, clear_table, 0)
    my_y, my_half, my_core = place[0] // 4, place[0] // 2 % 2, place[0] % 2

    def slot(k, _):
        b = rows[0, 0, k]
        s = b // SEGB
        old = mark[b]
        rank = jnp.where(old < 0, used[s], old)
        mark[b] = rank
        used[s] = jnp.where(old < 0, rank + 1, used[s])
        table[s, rank] = b - s * SEGB
        slots[0, k] = s * CAP + rank
        g = cols[0, 0, k]
        t = g // SEGB
        step = (t // 4 + 4 - my_y) % 4
        half = (t // 2 % 2 + my_half) % 2
        core = (t % 2 + my_core) % 2
        slots[1, k] = ((core * 4 + step) * 2 + half) * SEGB + g - t * SEGB
        return 0

    lax.fori_loop(0, counts[0, 0], slot, 0)
    for b in range(SEGB):
        seg[b * NV : (b + 1) * NV, :] = vectors[:, b * TILE : (b + 1) * TILE]


def prep(vectors, rows, cols, counts, place):
    n_segs = lax.axis_size("col")
    slots = rows.shape[-1]
    return pl.pallas_call(
        prep_kernel,
        out_shape=(
            jax.ShapeDtypeStruct((SEG, TILE), F32),
            jax.ShapeDtypeStruct((n_segs, 128), jnp.int32),
            jax.ShapeDtypeStruct((2, slots), jnp.int32),
        ),
        in_specs=[sspec()] * 4 + [vspec()],
        out_specs=(vspec(), sspec(), sspec()),
        scratch_shapes=[pltpu.SMEM((n_segs * SEGB,), jnp.int32), pltpu.SMEM((n_segs,), jnp.int32)],
        compiler_params=params(),
        name="prep",
    )(place, rows, cols, counts, vectors)


def pack_into(wanted, seg, message):
    for d in range(message.shape[0]):
        for q in range(CAP):
            b = wanted[d, q]
            message[d, q * NV : (q + 1) * NV, :] = seg[pl.ds(pl.multiple_of(b * NV, NV), NV), :]


def pack_kernel(wanted, seg, message):
    pack_into(wanted, seg, message)


def pack(wanted, seg):
    return pl.pallas_call(
        pack_kernel,
        out_shape=jax.ShapeDtypeStruct((wanted.shape[0], CAP * NV, TILE), F32),
        in_specs=[sspec(), vspec()],
        out_specs=vspec(),
        compiler_params=params(),
        name="pack",
    )(wanted, seg)


def split(x):
    high = x.astype(BF16)
    return high, (x - high.astype(F32)).astype(BF16)


def product_kernel(rider, *refs):
    counts, slots, tiles, from_x = refs[:4]
    from_y = refs[4:12]
    to_x = refs[12]
    to_y = refs[13:21]
    held, sems, row_vecs, col_vecs, row_sum, col_sum = refs[21:]
    count = counts[0, 0]

    def copy(k):
        return pltpu.make_async_copy(tiles.at[k], held.at[k], sems.at[k])

    def start(k, _):
        copy(k).start()
        return 0

    lax.fori_loop(0, count, start, 0)
    n_segs = from_x.shape[0]
    for s in range(n_segs):
        for q in range(CAP):
            high, low = split(from_x[s, q * NV : (q + 1) * NV, :])
            row_vecs[s * CAP + q, 0:NV, :] = high
            row_vecs[s * CAP + q, NV : 2 * NV, :] = low
            row_sum[s * CAP + q] = jnp.zeros((NV, TILE), F32)
    for p in range(8):
        for b in range(2 * SEGB):
            high, low = split(from_y[p][b * NV : (b + 1) * NV, :])
            col_vecs[p * 2 * SEGB + b, 0:NV, :] = high
            col_vecs[p * 2 * SEGB + b, NV : 2 * NV, :] = low
            col_sum[p * 2 * SEGB + b] = jnp.zeros((NV, TILE), F32)

    def slot(k, _):
        copy(k).wait()
        i = slots[0, k]
        j = slots[1, k]
        high, low = split(held[k])
        v_row = row_vecs[i]
        v_col = col_vecs[j]
        across = (((1,), (1,)), ((), ()))
        a = lax.dot_general(v_col, high, across, preferred_element_type=F32)
        b = lax.dot_general(v_col[:NV], low, across, preferred_element_type=F32)
        row_sum[i] += a[:NV] + a[NV:] + b
        c = jnp.dot(v_row, high, preferred_element_type=F32)
        d = jnp.dot(v_row[:NV], low, preferred_element_type=F32)
        col_sum[j] += c[:NV] + c[NV:] + d
        return 0

    lax.fori_loop(0, count, slot, 0)
    if rider:
        carried = from_y[0][2 * SEG : 2 * SEG + RID, :]
        for p in range(1, 8):
            carried = carried + from_y[p][2 * SEG : 2 * SEG + RID, :]
    for s in range(n_segs):
        for q in range(CAP):
            to_x[s, q * NV : (q + 1) * NV, :] = row_sum[s * CAP + q]
        if rider:
            to_x[s, CAP * NV : CAP * NV + RID, :] = carried
    for p in range(8):
        for b in range(2 * SEGB):
            to_y[p][b * NV : (b + 1) * NV, :] = col_sum[p * 2 * SEGB + b]


def cell_product(counts, slots, tiles, from_x, from_y, rider):
    n_segs = from_x.shape[0]
    maxt = tiles.shape[0]
    rows = CAP * NV + (RID if rider else 0)

    def kernel(*refs):
        product_kernel(rider, *refs)

    return pl.pallas_call(
        kernel,
        out_shape=(jax.ShapeDtypeStruct((n_segs, rows, TILE), F32),)
        + (jax.ShapeDtypeStruct((2 * SEG, TILE), F32),) * 8,
        in_specs=[sspec(), sspec(), pl.BlockSpec(memory_space=pl.ANY)] + [vspec()] * 9,
        out_specs=(vspec(),) * 9,
        scratch_shapes=[
            pltpu.VMEM((maxt, TILE, TILE), F32),
            pltpu.SemaphoreType.DMA((maxt,)),
            pltpu.VMEM((n_segs * CAP, 2 * NV, TILE), BF16),
            pltpu.VMEM((16 * SEGB, 2 * NV, TILE), BF16),
            pltpu.VMEM((n_segs * CAP, NV, TILE), F32),
            pltpu.VMEM((16 * SEGB, NV, TILE), F32),
        ],
        compiler_params=params(),
        cost_estimate=pl.CostEstimate(flops=48 * 2 * 3 * 2 * 256 * 256 * 256, bytes_accessed=16_000_000, transcendentals=0),
        name="cell_product",
    )(counts, slots, tiles, from_x, *from_y)


def add_parts(wanted, from_x, mine, theirs, total):
    total[...] = mine[0:SEG, :] + theirs[...]
    for d in range(from_x.shape[0]):
        for q in range(CAP):
            at = pl.ds(pl.multiple_of(wanted[d, q] * NV, NV), NV)
            total[at, :] += from_x[d, q * NV : (q + 1) * NV, :]


def gram_of(a, b):
    out = jnp.zeros((NV, NV), F32)
    for k in range(SEGB):
        out += lax.dot_general(
            a[k * NV : (k + 1) * NV, :],
            b[k * NV : (k + 1) * NV, :],
            (((1,), (1,)), ((), ())),
            precision=HIGH,
            preferred_element_type=F32,
        )
    return out


def turn_kernel(wanted, from_x, mine, theirs, seg, ride, message, total):
    add_parts(wanted, from_x, mine, theirs, total)
    pack_into(wanted, total, message)
    ride[0:SEG, :] = total[...]
    correlation = gram_of(seg, seg)
    projection = gram_of(seg, total)
    ride[SEG : SEG + RID, :] = jnp.zeros((RID, TILE), F32)
    for at, matrix in ((0, correlation), (2, projection)):
        for h in range(2):
            ride[SEG : SEG + RID, (at + h) * NV : (at + h + 1) * NV] = matrix[h * RID : (h + 1) * RID, :]


def turn(wanted, from_x, mine, theirs, seg):
    return pl.pallas_call(
        turn_kernel,
        out_shape=(
            jax.ShapeDtypeStruct((SEG + RID, TILE), F32),
            jax.ShapeDtypeStruct((from_x.shape[0], CAP * NV, TILE), F32),
        ),
        in_specs=[sspec()] + [vspec()] * 4,
        out_specs=(vspec(), vspec()),
        scratch_shapes=[pltpu.VMEM((SEG, TILE), F32)],
        compiler_params=params(),
        name="turn",
    )(wanted, from_x, mine, theirs, seg)


def solve(correlation, projection):
    m = jnp.concatenate([correlation, projection], axis=1)
    row_id = lax.broadcasted_iota(jnp.int32, m.shape, 0)
    for j in range(NV):
        row = m[j : j + 1, :] / m[j : j + 1, j : j + 1]
        m = jnp.where(row_id == j, row, m - m[:, j : j + 1] * row)
    return m[:, NV:]


def finish_kernel(wanted, from_x, mine, theirs, seg, product, residual, image, gram, total, rest):
    add_parts(wanted, from_x, mine, theirs, total)
    carried = from_x[0, CAP * NV : CAP * NV + RID, :]
    for d in range(1, from_x.shape[0]):
        carried = carried + from_x[d, CAP * NV : CAP * NV + RID, :]
    correlation, projection = (
        jnp.concatenate([carried[:, (at + h) * NV : (at + h + 1) * NV] for h in range(2)], axis=0) for at in (0, 2)
    )
    coeffs = solve(correlation, projection)
    back = coeffs.T
    for k in range(SEGB):
        at = slice(k * NV, (k + 1) * NV)
        p = product[at, :]
        r = p - jnp.dot(back, seg[at, :], precision=HIGH, preferred_element_type=F32)
        m = total[at, :] - jnp.dot(back, p, precision=HIGH, preferred_element_type=F32)
        rest[at, :] = r
        total[at, :] = m
        residual[:, k * TILE : (k + 1) * TILE] = r
        image[:, k * TILE : (k + 1) * TILE] = m
    local = gram_of(rest, total)
    for d in range(gram.shape[0]):
        gram[d] = jnp.zeros(gram.shape[1:], F32)
        for h in range(2):
            gram[d, :, h * NV : (h + 1) * NV] = local[h * RID : (h + 1) * RID, :]


def finish(wanted, from_x, mine, theirs, seg, product):
    n_segs = from_x.shape[0]
    return pl.pallas_call(
        finish_kernel,
        out_shape=(
            jax.ShapeDtypeStruct((NV, SEGB * TILE), F32),
            jax.ShapeDtypeStruct((NV, SEGB * TILE), F32),
            jax.ShapeDtypeStruct((n_segs, RID, 128), F32),
        ),
        in_specs=[sspec()] + [vspec()] * 5,
        out_specs=(vspec(),) * 3,
        scratch_shapes=[pltpu.VMEM((SEG, TILE), F32)] * 2,
        compiler_params=params(),
        name="finish",
    )(wanted, from_x, mine, theirs, seg, product)


def swap(x, axis):
    return lax.all_to_all(x, axis, 0, 0, tiled=True)


def spread(seg):
    other = lax.ppermute(seg, "row", OTHER_HALF)
    parts = [seg[:SEG], other[:SEG]]
    if seg.shape[0] > SEG:
        parts.append(seg[SEG:] + other[SEG:])
    mine = jnp.concatenate(parts, axis=0)
    near = [mine] + [lax.ppermute(mine, "row", row_shift(-step)) for step in (1, 2, 3)]
    return near + [lax.ppermute(x, "row", OTHER_CORE) for x in near]


def collect(pieces):
    met = [a + lax.ppermute(b, "row", OTHER_CORE) for a, b in zip(pieces[:4], pieces[4:])]
    both = met[0]
    for step in (1, 2, 3):
        both = both + lax.ppermute(met[step], "row", row_shift(step))
    return both, lax.ppermute(both[SEG:], "row", OTHER_HALF)


def per_device(vectors, tiles, tile_rows, tile_cols, counts):
    cell_tiles = tiles[0, 0]
    order_total = vectors.shape[1] * lax.axis_size("row") * lax.axis_size("col")
    place = lax.axis_index("row").astype(jnp.int32).reshape(1)
    seg, table, slots = prep(vectors, tile_rows, tile_cols, counts, place)
    wanted = swap(table, "col")

    from_y = spread(seg)
    from_x = swap(pack(wanted, seg), "col")
    to_x, *to_y = cell_product(counts, slots, cell_tiles, from_x, from_y, False)
    from_x = swap(to_x, "col")
    mine, theirs = collect(to_y)
    product, message = turn(wanted, from_x, mine, theirs, seg)

    from_y = spread(product)
    from_x = swap(message, "col")
    to_x, *to_y = cell_product(counts, slots, cell_tiles, from_x, from_y, True)
    from_x = swap(to_x, "col")
    mine, theirs = collect(to_y)
    residual, image, local = finish(wanted, from_x, mine, theirs, seg, product)

    part = jnp.sum(swap(local, "col"), axis=0)
    total = jnp.sum(swap(jnp.broadcast_to(part, local.shape), "row"), axis=0)
    gram = jnp.concatenate([total[:, :NV], total[:, NV : 2 * NV]], axis=0) / order_total
    return (residual, image, gram)


def solution(mesh):
    in_specs = (
        P(None, ("row", "col")),
        P("row", "col", None, None, None),
        P("row", "col", None),
        P("row", "col", None),
        P("row", "col"),
    )
    out_specs = (P(None, ("row", "col")), P(None, ("row", "col")), P())
    return jax.shard_map(
        per_device, mesh=mesh, in_specs=in_specs, out_specs=out_specs, check_vma=False
    )
```

time: 815 us -> 241 us (0.30)
  waiting for transfers between devices: 541 us -> 57.5 us
  blocking collectives: 169 us -> 49.8 us
  starting transfers between devices: 0.96 us -> 97 us
  matrix products: 59.3 us -> 0 us
  Pallas kernels: 0 us -> 24.1 us
  between operations: 15.4 us -> 1.52 us
    reduce_scatter x4 -> x0, waiting for transfers between devices: 280 us -> none  [the longest x2 158 us: reduce_rows(): lax.psum_scatter(row_terms.reshape(width, -1), 'col', scatter_dimension=1...]
    all_gather x4 -> x0, waiting for transfers between devices: 260 us -> none  [the longest x2 150 us: apply_whole(): row_group = lax.all_gather(block, 'col', axis=1, tiled=True)]
    psum x2 -> x0, blocking collectives: 169 us -> none  [the longest x1 84.7 us: per_device(): lax.psum((local_correlation, local_projection), ('row', 'col'))]
    ppermute x0 -> x32, starting transfers between devices: none -> 63.6 us  [the longest x8 20.4 us: spread(): return near + [lax.ppermute(x, 'row', OTHER_CORE) for x in near]]
    dot_general x16 -> x0, matrix products: 58.9 us -> none  [the longest x2 27.2 us: local_products(): jnp.einsum('kij,vkj->vki', cell_tiles, from_cols, precision=lax.Precision...]
    ppermute x0 -> x32, waiting for transfers between devices: none -> 57.5 us  [the longest x2 30.8 us: spread(): other = lax.ppermute(seg, 'row', OTHER_HALF)]
    all_to_all x0 -> x3, blocking collectives: none -> 49.8 us  [swap(): return lax.all_to_all(x, axis, 0, 0, tiled=True)]
    all_to_all x0 -> x4, starting transfers between devices: none -> 33.4 us  [swap(): return lax.all_to_all(x, axis, 0, 0, tiled=True)]
  transfers between devices with their start and end apart: 8 -> 36, of which waited for: 8 -> 15; matrix products, arithmetic and copies ran while one was open for 9% -> 0% of each run, Pallas kernels for 0% -> 0%
where the time goes in v1:
time: 241 us
  starting transfers between devices  97 us (40%)
  waiting for transfers between devices  57.5 us (24%)
  blocking collectives  49.8 us (21%)
  Pallas kernels  24.1 us (10%)
  local copies, waits for them, and re-layouts  9.59 us (4%)
    all_to_all x3, blocking collectives, swap(): return lax.all_to_all(x, axis, 0, 0, tiled=True)  49.8 us
    all_to_all x4, starting transfers between devices, swap(): return lax.all_to_all(x, axis, 0, 0, tiled=True)  33.4 us
    ppermute x2, waiting for transfers between devices, spread(): other = lax.ppermute(seg, 'row', OTHER_HALF)  30.8 us
    ppermute x8, starting transfers between devices, spread(): return near + [lax.ppermute(x, 'row', OTHER_CORE) for x in near]  20.4 us
    ppermute x6, starting transfers between devices, collect(): both = both + lax.ppermute(met[step], 'row', row_shift(step))  14.6 us
    ppermute x6, waiting for transfers between devices, collect(): both = both + lax.ppermute(met[step], 'row', row_shift(step))  14.3 us
    pallas_call x2, Pallas kernels, cell_product(): pl.pallas_call(kernel, out_shape=(jax.ShapeDtypeStruct((n_segs, rows, TIL...  14 us
    ppermute x6, starting transfers between devices, spread(): lax.ppermute(mine, 'row', row_shift(-step))  10.9 us
  transfers between devices with their start and end apart: 36, of which 15 were waited for; matrix products, arithmetic and copies ran while one was open for 0% of the time, Pallas kernels for 0%

profile of v1, /device:TPU:1, one launch (start us, length us, event | category | flops | bytes accessed | tf_op | source)
XLA Modules:
  0.0 240.5 jit_solution(11787260839975964979)
XLA Ops:
  3.5 2.8 %prep.1 = (f32[96,256]{1,0:T(8,128)S(1)}, s32[16,128]{1,0:T(8,128)S(1)}, s32[2,48]{1,0:T(2,128)S(1)}) custom-call(s32[1]{0:T(128)} %bitcast.place, s32[1,1,48]{2,1,0:T(1,128)S(1)} %copy-done.1, s32[1,1,48]{2,1,0:T(1,128)S(1)} %copy-done.2, s32[1,1]{1,0:T(1,128)S(6)} %copy.11.counts.refs_0_, f32[16,1536]{1,0:T(8,128)S(1)} %copy-done), custom_call_target="tpu_custom_call" | custom-call | tf_op jit(solution)/shard_map/prep/pallas_call | solution.py:84
  6.3 15.2 %all_to_all.41 = s32[16,1,128]{2,1,0:T(1,128)S(1)} all-to-all(s32[16,1,128]{2,1,0:T(1,128)S(1)} %bitcast.9), channel_id=1, replica_groups=mesh['row'=16,'col'=16] {'col'}, dimensions={0} | all-to-all | bytes 16384 | tf_op jit(solution)/shard_map/all_to_all | solution.py:316
  23.2 3.6 %all-to-all-start.1 = ((f32[16,48,256]{2,1,0:T(8,128)}), f32[16,48,256]{2,1,0:T(8,128)S(1)}, u32[]{:S(2)}, u32[]{:S(2)}) async-start(f32[16,48,256]{2,1,0:T(8,128)} %pack.1), calls=%async_computation.1 | async-start | bytes 1572864 | tf_op jit(solution)/shard_map/all_to_all | solution.py:316
  26.8 4.4 %collective-permute-start = (f32[96,256]{1,0:T(8,128)S(1)}, f32[96,256]{1,0:T(8,128)S(1)}, u32[]{:S(2)}, u32[]{:S(2)}) collective-permute-start(f32[96,256]{1,0:T(8,128)S(1)} %get-tuple-element.31.seg), channel_id=1, source_target_pairs={{0,32},{16,48},{32,0},{48,16},{64,96},{80,112},{96,64},{112,80},{1... | collective-permute-start | bytes 294920 | tf_op jit(solution)/shard_map/ppermute | solution.py:320
  31.2 14.4 %collective-permute-done = f32[96,256]{1,0:T(8,128)S(1)} collective-permute-done((f32[96,256]{1,0:T(8,128)S(1)}, f32[96,256]{1,0:T(8,128)S(1)}, u32[]{:S(2)}, u32[]{:S(2)}) %collective-permute-start) | collective-permute-done | bytes 98336 | tf_op jit(solution)/shard_map/ppermute | solution.py:320
  46.2 6.7 %collective-permute-start.2 = (f32[192,256]{1,0:T(8,128)S(1)}, f32[192,256]{1,0:T(8,128)S(1)}, u32[]{:S(2)}, u32[]{:S(2)}) collective-permute-start(f32[192,256]{1,0:T(8,128)S(1)} %constant_dynamic-update-slice_fusion.refs_4_), channel_id=1, source_target_pairs={{0,128},{16,144},{32,160},{48,176},{64,192},{80,208},{96,224},{112... | collective-permute-start | bytes 589832 | tf_op jit(solution)/shard_map/ppermute | solution.py:325
  52.9 3.1 %collective-permute-start.4 = (f32[192,256]{1,0:T(8,128)S(1)}, f32[192,256]{1,0:T(8,128)S(1)}, u32[]{:S(2)}, u32[]{:S(2)}) collective-permute-start(f32[192,256]{1,0:T(8,128)S(1)} %constant_dynamic-update-slice_fusion.refs_4_), channel_id=1, source_target_pairs={{0,16},{16,0},{32,48},{48,32},{64,80},{80,64},{96,112},{112,96},{1... | collective-permute-start | bytes 589832 | tf_op jit(solution)/shard_map/ppermute | solution.py:326
  56.1 4.3 %collective-permute-start.7 = (f32[192,256]{1,0:T(8,128)S(1)}, f32[192,256]{1,0:T(8,128)S(1)}, u32[]{:S(2)}, u32[]{:S(2)}) collective-permute-start(f32[192,256]{1,0:T(8,128)S(1)} %collective-permute-done.3.refs_7_), channel_id=1, source_target_pairs={{0,16},{16,0},{32,48},{48,32},{64,80},{80,64},{96,112},{112,96},{1... | collective-permute-start | bytes 589832 | tf_op jit(solution)/shard_map/ppermute | solution.py:326
  60.4 2.7 %collective-permute-start.6 = (f32[192,256]{1,0:T(8,128)S(1)}, f32[192,256]{1,0:T(8,128)S(1)}, u32[]{:S(2)}, u32[]{:S(2)}) collective-permute-start(f32[192,256]{1,0:T(8,128)S(1)} %collective-permute-done.2.refs_6_), channel_id=1, source_target_pairs={{0,16},{16,0},{32,48},{48,32},{64,80},{80,64},{96,112},{112,96},{1... | collective-permute-start | bytes 589832 | tf_op jit(solution)/shard_map/ppermute | solution.py:326
  67.3 6.9 %cell_product.2 = (f32[16,48,256]{2,1,0:T(8,128)}, f32[192,256]{1,0:T(8,128)S(1)}, f32[192,256]{1,0:T(8,128)S(1)}, f32[192,256]{1,0:T(8,128)S(1)}, f32[192,256]{...) custom-call(s32[1,1]{1,0:T(1,128)S(6)} %copy.11.counts.refs_0_, ...), custom_call_target="tpu_custom_call" | custom-call | flops 9663676416 | bytes 16000000 | tf_op jit(solution)/shard_map/cell_product/pallas_call | solution.py:195
  75.6 10.3 %all-to-all-start.2 = ((f32[16,48,256]{2,1,0:T(8,128)}), f32[16,48,256]{2,1,0:T(8,128)S(1)}, u32[]{:S(2)}, u32[]{:S(2)}) async-start(f32[16,48,256]{2,1,0:T(8,128)} %get-tuple-element.32), calls=%async_computation.2 | async-start | bytes 1572864 | tf_op jit(solution)/shard_map/all_to_all | solution.py:316
  87.7 4.4 %collective-permute-start.10 = (f32[192,256]{1,0:T(8,128)S(1)}, f32[192,256]{1,0:T(8,128)S(1)}, u32[]{:S(2)}, u32[]{:S(2)}) collective-permute-start(f32[192,256]{1,0:T(8,128)S(1)} %add.46), channel_id=1, source_target_pairs={{0,64},{16,80},{32,96},{48,112},{64,128},{80,144},{96,160},{112,17... | collective-permute-start | bytes 589832 | tf_op jit(solution)/shard_map/ppermute | solution.py:333
  96.3 5.2 %collective-permute-done.12 = f32[192,256]{1,0:T(8,128)S(1)} collective-permute-done((f32[192,256]{1,0:T(8,128)S(1)}, f32[192,256]{1,0:T(8,128)S(1)}, u32[]{:S(2)}, u32[]{:S(2)}) %collective-permute-start.12) | collective-permute-done | bytes 196640 | tf_op jit(solution)/shard_map/ppermute | solution.py:333
  101.8 3.5 %collective-permute-start.15 = (f32[96,256]{1,0:T(8,128)S(1)}, f32[96,256]{1,0:T(8,128)S(1)}, u32[]{:S(2)}, u32[]{:S(2)}) collective-permute-start(f32[96,256]{1,0:T(8,128)S(1)} %slice.32), channel_id=1, source_target_pairs={{0,32},{16,48},{32,0},{48,16},{64,96},{80,112},{96,64},{112,80},{1... | collective-permute-start | bytes 294920 | tf_op jit(solution)/shard_map/ppermute | solution.py:334
  105.3 4.2 %collective-permute-done.15.theirs = f32[96,256]{1,0:T(8,128)S(1)} collective-permute-done((f32[96,256]{1,0:T(8,128)S(1)}, f32[96,256]{1,0:T(8,128)S(1)}, u32[]{:S(2)}, u32[]{:S(2)}) %collective-permute-start.15) | collective-permute-done | bytes 98336 | tf_op jit(solution)/shard_map/ppermute | solution.py:334
  109.5 2.4 turn.1
  111.9 9.2 %all-to-all-start.3 = ((f32[16,48,256]{2,1,0:T(8,128)}), f32[16,48,256]{2,1,0:T(8,128)S(1)}, u32[]{:S(2)}, u32[]{:S(2)}) async-start(f32[16,48,256]{2,1,0:T(8,128)} %get-tuple-element.41), calls=%async_computation.3 | async-start | bytes 1572864 | tf_op jit(solution)/shard_map/all_to_all | solution.py:316
  121.1 4.2 %collective-permute-start.16 = (f32[104,256]{1,0:T(8,128)S(1)}, f32[104,256]{1,0:T(8,128)S(1)}, u32[]{:S(2)}, u32[]{:S(2)}) collective-permute-start(f32[104,256]{1,0:T(8,128)S(1)} %get-tuple-element.42.product), channel_id=1, source_target_pairs={{0,32},{16,48},{32,0},{48,16},{64,96},{80,112},{96,64},{112,80},{1... | collective-permute-start | bytes 319496 | tf_op jit(solution)/shard_map/ppermute | solution.py:320
  125.4 16.4 %collective-permute-done.16 = f32[104,256]{1,0:T(8,128)S(1)} collective-permute-done((f32[104,256]{1,0:T(8,128)S(1)}, f32[104,256]{1,0:T(8,128)S(1)}, u32[]{:S(2)}, u32[]{:S(2)}) %collective-permute-start.16) | collective-permute-done | bytes 106528 | tf_op jit(solution)/shard_map/ppermute | solution.py:320
  141.9 3.5 %collective-permute-start.18 = (f32[200,256]{1,0:T(8,128)S(1)}, f32[200,256]{1,0:T(8,128)S(1)}, u32[]{:S(2)}, u32[]{:S(2)}) collective-permute-start(f32[200,256]{1,0:T(8,128)S(1)} %pad_maximum_fusion.refs_4_), channel_id=1, source_target_pairs={{0,128},{16,144},{32,160},{48,176},{64,192},{80,208},{96,224},{112... | collective-permute-start | bytes 614408 | tf_op jit(solution)/shard_map/ppermute | solution.py:325
  145.4 2.5 %collective-permute-start.20 = (f32[200,256]{1,0:T(8,128)S(1)}, f32[200,256]{1,0:T(8,128)S(1)}, u32[]{:S(2)}, u32[]{:S(2)}) collective-permute-start(f32[200,256]{1,0:T(8,128)S(1)} %pad_maximum_fusion.refs_4_), channel_id=1, source_target_pairs={{0,16},{16,0},{32,48},{48,32},{64,80},{80,64},{96,112},{112,96},{1... | collective-permute-start | bytes 614408 | tf_op jit(solution)/shard_map/ppermute | solution.py:326
  148.0 4.5 %collective-permute-start.23 = (f32[200,256]{1,0:T(8,128)S(1)}, f32[200,256]{1,0:T(8,128)S(1)}, u32[]{:S(2)}, u32[]{:S(2)}) collective-permute-start(f32[200,256]{1,0:T(8,128)S(1)} %collective-permute-done.19.refs_7_), channel_id=1, source_target_pairs={{0,16},{16,0},{32,48},{48,32},{64,80},{80,64},{96,112},{112,96},{1... | collective-permute-start | bytes 614408 | tf_op jit(solution)/shard_map/ppermute | solution.py:326
  152.6 3.2 %collective-permute-start.22 = (f32[200,256]{1,0:T(8,128)S(1)}, f32[200,256]{1,0:T(8,128)S(1)}, u32[]{:S(2)}, u32[]{:S(2)}) collective-permute-start(f32[200,256]{1,0:T(8,128)S(1)} %collective-permute-done.18.refs_6_), channel_id=1, source_target_pairs={{0,16},{16,0},{32,48},{48,32},{64,80},{80,64},{96,112},{112,96},{1... | collective-permute-start | bytes 614408 | tf_op jit(solution)/shard_map/ppermute | solution.py:326
  157.3 7.0 %cell_product.3 = (f32[16,56,256]{2,1,0:T(8,128)}, f32[192,256]{1,0:T(8,128)S(1)}, f32[192,256]{1,0:T(8,128)S(1)}, f32[192,256]{1,0:T(8,128)S(1)}, f32[192,256]{...) custom-call(s32[1,1]{1,0:T(1,128)S(6)} %copy.11.counts.refs_0_, ...), custom_call_target="tpu_custom_call" | custom-call | flops 9663676416 | bytes 16000000 | tf_op jit(solution)/shard_map/cell_product/pallas_call | solution.py:195
  167.0 10.3 %all-to-all-start.4 = ((f32[16,56,256]{2,1,0:T(8,128)}), f32[16,56,256]{2,1,0:T(8,128)S(1)}, u32[]{:S(2)}, u32[]{:S(2)}) async-start(f32[16,56,256]{2,1,0:T(8,128)} %get-tuple-element.43), calls=%async_computation.4 | async-start | bytes 1835008 | tf_op jit(solution)/shard_map/all_to_all | solution.py:316
  179.1 4.8 %collective-permute-start.26 = (f32[192,256]{1,0:T(8,128)S(1)}, f32[192,256]{1,0:T(8,128)S(1)}, u32[]{:S(2)}, u32[]{:S(2)}) collective-permute-start(f32[192,256]{1,0:T(8,128)S(1)} %add.54), channel_id=1, source_target_pairs={{0,64},{16,80},{32,96},{48,112},{64,128},{80,144},{96,160},{112,17... | collective-permute-start | bytes 589832 | tf_op jit(solution)/shard_map/ppermute | solution.py:333
  189.0 5.2 %collective-permute-done.28 = f32[192,256]{1,0:T(8,128)S(1)} collective-permute-done((f32[192,256]{1,0:T(8,128)S(1)}, f32[192,256]{1,0:T(8,128)S(1)}, u32[]{:S(2)}, u32[]{:S(2)}) %collective-permute-start.28) | collective-permute-done | bytes 196640 | tf_op jit(solution)/shard_map/ppermute | solution.py:333
  194.3 3.4 %collective-permute-start.31 = (f32[96,256]{1,0:T(8,128)S(1)}, f32[96,256]{1,0:T(8,128)S(1)}, u32[]{:S(2)}, u32[]{:S(2)}) collective-permute-start(f32[96,256]{1,0:T(8,128)S(1)} %slice.35), channel_id=1, source_target_pairs={{0,32},{16,48},{32,0},{48,16},{64,96},{80,112},{96,64},{112,80},{1... | collective-permute-start | bytes 294920 | tf_op jit(solution)/shard_map/ppermute | solution.py:334
  197.7 4.2 %collective-permute-done.31.theirs = f32[96,256]{1,0:T(8,128)S(1)} collective-permute-done((f32[96,256]{1,0:T(8,128)S(1)}, f32[96,256]{1,0:T(8,128)S(1)}, u32[]{:S(2)}, u32[]{:S(2)}) %collective-permute-start.31) | collective-permute-done | bytes 98336 | tf_op jit(solution)/shard_map/ppermute | solution.py:334
  201.8 3.4 %finish.1 = (f32[16,1536]{1,0:T(8,128)}, f32[16,1536]{1,0:T(8,128)}, f32[16,8,128]{2,1,0:T(8,128)S(1)}) custom-call(s32[16,128]{1,0:T(8,128)S(1)} %bitcast.8, f32[16,56,256]{2,1,0:T(8,128)S(1)} %all-to-all-done.4.from_x, f32[192,256]{1,0:T(8,128)S(1)} %add_add_fusion.mine, f32[96,256]{1,0:T(8,128)S(1)} %collective-permute-done.31.theirs, ...), custom_call_target="tpu_custom_call" | custom-call | tf_op jit(solution)/shard_map/finish/pallas_call | solution.py:300
  205.2 15.7 %all_to_all.42 = f32[16,8,128]{2,1,0:T(8,128)S(1)} all-to-all(f32[16,8,128]{2,1,0:T(8,128)S(1)} %get-tuple-element.54), channel_id=1, replica_groups=mesh['row'=16,'col'=16] {'col'}, dimensions={0} | all-to-all | bytes 131072 | tf_op jit(solution)/shard_map/all_to_all | solution.py:316
  220.9 18.9 %all_to_all.43 = f32[16,8,128]{2,1,0:T(8,128)S(1)} all-to-all(f32[16,8,128]{2,1,0:T(8,128)S(1)} %broadcast_in_dim.3), channel_id=1, replica_groups=mesh['row'=16,'col'=16] {'row'}, dimensions={0} | all-to-all | bytes 131072 | tf_op jit(solution)/shard_map/all_to_all | solution.py:316
  (96 shorter events, 28.4 us)
Async XLA Ops:
  23.2 42.3 %all-to-all-start.1 = ((f32[16,48,256]{2,1,0:T(8,128)}), f32[16,48,256]{2,1,0:T(8,128)S(1)}, u32[]{:S(2)}, u32[]{:S(2)}) async-start(f32[16,48,256]{2,1,0:T(8,128)} %pack.1), calls=%async_computation.1 | async-start | bytes 1572864 | tf_op jit(solution)/shard_map/all_to_all | solution.py:316
  26.8 18.8 %collective-permute-start = (f32[96,256]{1,0:T(8,128)S(1)}, f32[96,256]{1,0:T(8,128)S(1)}, u32[]{:S(2)}, u32[]{:S(2)}) collective-permute-start(f32[96,256]{1,0:T(8,128)S(1)} %get-tuple-element.31.seg), channel_id=1, source_target_pairs={{0,32},{16,48},{32,0},{48,16},{64,96},{80,112},{96,64},{112,80},{1... | collective-permute-start | bytes 294920 | tf_op jit(solution)/shard_map/ppermute | solution.py:320
  45.7 10.4 %collective-permute-start.3 = (f32[192,256]{1,0:T(8,128)S(1)}, f32[192,256]{1,0:T(8,128)S(1)}, u32[]{:S(2)}, u32[]{:S(2)}) collective-permute-start(f32[192,256]{1,0:T(8,128)S(1)} %constant_dynamic-update-slice_fusion.refs_4_), channel_id=1, source_target_pairs={{0,64},{16,80},{32,96},{48,112},{64,128},{80,144},{96,160},{112,17... | collective-permute-start | bytes 589832 | tf_op jit(solution)/shard_map/ppermute | solution.py:325
  46.2 14.2 %collective-permute-start.2 = (f32[192,256]{1,0:T(8,128)S(1)}, f32[192,256]{1,0:T(8,128)S(1)}, u32[]{:S(2)}, u32[]{:S(2)}) collective-permute-start(f32[192,256]{1,0:T(8,128)S(1)} %constant_dynamic-update-slice_fusion.refs_4_), channel_id=1, source_target_pairs={{0,128},{16,144},{32,160},{48,176},{64,192},{80,208},{96,224},{112... | collective-permute-start | bytes 589832 | tf_op jit(solution)/shard_map/ppermute | solution.py:325
  52.9 10.1 %collective-permute-start.1 = (f32[192,256]{1,0:T(8,128)S(1)}, f32[192,256]{1,0:T(8,128)S(1)}, u32[]{:S(2)}, u32[]{:S(2)}) collective-permute-start(f32[192,256]{1,0:T(8,128)S(1)} %constant_dynamic-update-slice_fusion.refs_4_), channel_id=1, source_target_pairs={{0,192},{16,208},{32,224},{48,240},{64,0},{80,16},{96,32},{112,48}... | collective-permute-start | bytes 589832 | tf_op jit(solution)/shard_map/ppermute | solution.py:325
  52.9 10.1 %collective-permute-start.4 = (f32[192,256]{1,0:T(8,128)S(1)}, f32[192,256]{1,0:T(8,128)S(1)}, u32[]{:S(2)}, u32[]{:S(2)}) collective-permute-start(f32[192,256]{1,0:T(8,128)S(1)} %constant_dynamic-update-slice_fusion.refs_4_), channel_id=1, source_target_pairs={{0,16},{16,0},{32,48},{48,32},{64,80},{80,64},{96,112},{112,96},{1... | collective-permute-start | bytes 589832 | tf_op jit(solution)/shard_map/ppermute | solution.py:326
  56.1 7.0 %collective-permute-start.7 = (f32[192,256]{1,0:T(8,128)S(1)}, f32[192,256]{1,0:T(8,128)S(1)}, u32[]{:S(2)}, u32[]{:S(2)}) collective-permute-start(f32[192,256]{1,0:T(8,128)S(1)} %collective-permute-done.3.refs_7_), channel_id=1, source_target_pairs={{0,16},{16,0},{32,48},{48,32},{64,80},{80,64},{96,112},{112,96},{1... | collective-permute-start | bytes 589832 | tf_op jit(solution)/shard_map/ppermute | solution.py:326
  60.4 3.7 %collective-permute-start.6 = (f32[192,256]{1,0:T(8,128)S(1)}, f32[192,256]{1,0:T(8,128)S(1)}, u32[]{:S(2)}, u32[]{:S(2)}) collective-permute-start(f32[192,256]{1,0:T(8,128)S(1)} %collective-permute-done.2.refs_6_), channel_id=1, source_target_pairs={{0,16},{16,0},{32,48},{48,32},{64,80},{80,64},{96,112},{112,96},{1... | collective-permute-start | bytes 589832 | tf_op jit(solution)/shard_map/ppermute | solution.py:326
  75.6 33.9 %all-to-all-start.2 = ((f32[16,48,256]{2,1,0:T(8,128)}), f32[16,48,256]{2,1,0:T(8,128)S(1)}, u32[]{:S(2)}, u32[]{:S(2)}) async-start(f32[16,48,256]{2,1,0:T(8,128)} %get-tuple-element.32), calls=%async_computation.2 | async-start | bytes 1572864 | tf_op jit(solution)/shard_map/all_to_all | solution.py:316
  86.0 6.1 %collective-permute-start.11 = (f32[192,256]{1,0:T(8,128)}, f32[192,256]{1,0:T(8,128)S(1)}, u32[]{:S(2)}, u32[]{:S(2)}) collective-permute-start(f32[192,256]{1,0:T(8,128)} %copy-done.6), channel_id=1, source_target_pairs={{0,16},{16,0},{32,48},{48,32},{64,80},{80,64},{96,112},{112,96},{1... | collective-permute-start | bytes 589832 | tf_op jit(solution)/shard_map/ppermute | solution.py:330
  86.5 6.0 %collective-permute-start.13 = (f32[192,256]{1,0:T(8,128)S(1)}, f32[192,256]{1,0:T(8,128)S(1)}, u32[]{:S(2)}, u32[]{:S(2)}) collective-permute-start(f32[192,256]{1,0:T(8,128)S(1)} %get-tuple-element.40), channel_id=1, source_target_pairs={{0,16},{16,0},{32,48},{48,32},{64,80},{80,64},{96,112},{112,96},{1... | collective-permute-start | bytes 589832 | tf_op jit(solution)/shard_map/ppermute | solution.py:330
  86.6 8.3 %collective-permute-start.8 = (f32[192,256]{1,0:T(8,128)S(1)}, f32[192,256]{1,0:T(8,128)S(1)}, u32[]{:S(2)}, u32[]{:S(2)}) collective-permute-start(f32[192,256]{1,0:T(8,128)S(1)} %get-tuple-element.34), channel_id=1, source_target_pairs={{0,16},{16,0},{32,48},{48,32},{64,80},{80,64},{96,112},{112,96},{1... | collective-permute-start | bytes 589832 | tf_op jit(solution)/shard_map/ppermute | solution.py:330
  87.7 8.6 %collective-permute-start.10 = (f32[192,256]{1,0:T(8,128)S(1)}, f32[192,256]{1,0:T(8,128)S(1)}, u32[]{:S(2)}, u32[]{:S(2)}) collective-permute-start(f32[192,256]{1,0:T(8,128)S(1)} %add.46), channel_id=1, source_target_pairs={{0,64},{16,80},{32,96},{48,112},{64,128},{80,144},{96,160},{112,17... | collective-permute-start | bytes 589832 | tf_op jit(solution)/shard_map/ppermute | solution.py:333
  92.1 9.3 %collective-permute-start.12 = (f32[192,256]{1,0:T(8,128)S(1)}, f32[192,256]{1,0:T(8,128)S(1)}, u32[]{:S(2)}, u32[]{:S(2)}) collective-permute-start(f32[192,256]{1,0:T(8,128)S(1)} %add.48), channel_id=1, source_target_pairs={{0,128},{16,144},{32,160},{48,176},{64,192},{80,208},{96,224},{112... | collective-permute-start | bytes 589832 | tf_op jit(solution)/shard_map/ppermute | solution.py:333
  92.5 9.2 %collective-permute-start.14 = (f32[192,256]{1,0:T(8,128)S(1)}, f32[192,256]{1,0:T(8,128)S(1)}, u32[]{:S(2)}, u32[]{:S(2)}) collective-permute-start(f32[192,256]{1,0:T(8,128)S(1)} %add.50), channel_id=1, source_target_pairs={{0,192},{16,208},{32,224},{48,240},{64,0},{80,16},{96,32},{112,48}... | collective-permute-start | bytes 589832 | tf_op jit(solution)/shard_map/ppermute | solution.py:333
  101.8 7.7 %collective-permute-start.15 = (f32[96,256]{1,0:T(8,128)S(1)}, f32[96,256]{1,0:T(8,128)S(1)}, u32[]{:S(2)}, u32[]{:S(2)}) collective-permute-start(f32[96,256]{1,0:T(8,128)S(1)} %slice.32), channel_id=1, source_target_pairs={{0,32},{16,48},{32,0},{48,16},{64,96},{80,112},{96,64},{112,80},{1... | collective-permute-start | bytes 294920 | tf_op jit(solution)/shard_map/ppermute | solution.py:334
  111.9 45.4 %all-to-all-start.3 = ((f32[16,48,256]{2,1,0:T(8,128)}), f32[16,48,256]{2,1,0:T(8,128)S(1)}, u32[]{:S(2)}, u32[]{:S(2)}) async-start(f32[16,48,256]{2,1,0:T(8,128)} %get-tuple-element.41), calls=%async_computation.3 | async-start | bytes 1572864 | tf_op jit(solution)/shard_map/all_to_all | solution.py:316
  121.1 20.6 %collective-permute-start.16 = (f32[104,256]{1,0:T(8,128)S(1)}, f32[104,256]{1,0:T(8,128)S(1)}, u32[]{:S(2)}, u32[]{:S(2)}) collective-permute-start(f32[104,256]{1,0:T(8,128)S(1)} %get-tuple-element.42.product), channel_id=1, source_target_pairs={{0,32},{16,48},{32,0},{48,16},{64,96},{80,112},{96,64},{112,80},{1... | collective-permute-start | bytes 319496 | tf_op jit(solution)/shard_map/ppermute | solution.py:320
  141.8 6.2 %collective-permute-start.19 = (f32[200,256]{1,0:T(8,128)S(1)}, f32[200,256]{1,0:T(8,128)S(1)}, u32[]{:S(2)}, u32[]{:S(2)}) collective-permute-start(f32[200,256]{1,0:T(8,128)S(1)} %pad_maximum_fusion.refs_4_), channel_id=1, source_target_pairs={{0,64},{16,80},{32,96},{48,112},{64,128},{80,144},{96,160},{112,17... | collective-permute-start | bytes 614408 | tf_op jit(solution)/shard_map/ppermute | solution.py:325
  141.9 10.8 %collective-permute-start.18 = (f32[200,256]{1,0:T(8,128)S(1)}, f32[200,256]{1,0:T(8,128)S(1)}, u32[]{:S(2)}, u32[]{:S(2)}) collective-permute-start(f32[200,256]{1,0:T(8,128)S(1)} %pad_maximum_fusion.refs_4_), channel_id=1, source_target_pairs={{0,128},{16,144},{32,160},{48,176},{64,192},{80,208},{96,224},{112... | collective-permute-start | bytes 614408 | tf_op jit(solution)/shard_map/ppermute | solution.py:325
  145.4 10.4 %collective-permute-start.17 = (f32[200,256]{1,0:T(8,128)S(1)}, f32[200,256]{1,0:T(8,128)S(1)}, u32[]{:S(2)}, u32[]{:S(2)}) collective-permute-start(f32[200,256]{1,0:T(8,128)S(1)} %pad_maximum_fusion.refs_4_), channel_id=1, source_target_pairs={{0,192},{16,208},{32,224},{48,240},{64,0},{80,16},{96,32},{112,48}... | collective-permute-start | bytes 614408 | tf_op jit(solution)/shard_map/ppermute | solution.py:325
  145.4 10.4 %collective-permute-start.20 = (f32[200,256]{1,0:T(8,128)S(1)}, f32[200,256]{1,0:T(8,128)S(1)}, u32[]{:S(2)}, u32[]{:S(2)}) collective-permute-start(f32[200,256]{1,0:T(8,128)S(1)} %pad_maximum_fusion.refs_4_), channel_id=1, source_target_pairs={{0,16},{16,0},{32,48},{48,32},{64,80},{80,64},{96,112},{112,96},{1... | collective-permute-start | bytes 614408 | tf_op jit(solution)/shard_map/ppermute | solution.py:326
  148.0 7.9 %collective-permute-start.23 = (f32[200,256]{1,0:T(8,128)S(1)}, f32[200,256]{1,0:T(8,128)S(1)}, u32[]{:S(2)}, u32[]{:S(2)}) collective-permute-start(f32[200,256]{1,0:T(8,128)S(1)} %collective-permute-done.19.refs_7_), channel_id=1, source_target_pairs={{0,16},{16,0},{32,48},{48,32},{64,80},{80,64},{96,112},{112,96},{1... | collective-permute-start | bytes 614408 | tf_op jit(solution)/shard_map/ppermute | solution.py:326
  152.6 4.3 %collective-permute-start.22 = (f32[200,256]{1,0:T(8,128)S(1)}, f32[200,256]{1,0:T(8,128)S(1)}, u32[]{:S(2)}, u32[]{:S(2)}) collective-permute-start(f32[200,256]{1,0:T(8,128)S(1)} %collective-permute-done.18.refs_6_), channel_id=1, source_target_pairs={{0,16},{16,0},{32,48},{48,32},{64,80},{80,64},{96,112},{112,96},{1... | collective-permute-start | bytes 614408 | tf_op jit(solution)/shard_map/ppermute | solution.py:326
  167.0 34.8 %all-to-all-start.4 = ((f32[16,56,256]{2,1,0:T(8,128)}), f32[16,56,256]{2,1,0:T(8,128)S(1)}, u32[]{:S(2)}, u32[]{:S(2)}) async-start(f32[16,56,256]{2,1,0:T(8,128)} %get-tuple-element.43), calls=%async_computation.4 | async-start | bytes 1835008 | tf_op jit(solution)/shard_map/all_to_all | solution.py:316
  177.4 6.5 %collective-permute-start.27 = (f32[192,256]{1,0:T(8,128)}, f32[192,256]{1,0:T(8,128)S(1)}, u32[]{:S(2)}, u32[]{:S(2)}) collective-permute-start(f32[192,256]{1,0:T(8,128)} %copy-done.5), channel_id=1, source_target_pairs={{0,16},{16,0},{32,48},{48,32},{64,80},{80,64},{96,112},{112,96},{1... | collective-permute-start | bytes 589832 | tf_op jit(solution)/shard_map/ppermute | solution.py:330
  177.9 7.3 %collective-permute-start.29 = (f32[192,256]{1,0:T(8,128)}, f32[192,256]{1,0:T(8,128)S(1)}, u32[]{:S(2)}, u32[]{:S(2)}) collective-permute-start(f32[192,256]{1,0:T(8,128)} %copy-done.4), channel_id=1, source_target_pairs={{0,16},{16,0},{32,48},{48,32},{64,80},{80,64},{96,112},{112,96},{1... | collective-permute-start | bytes 589832 | tf_op jit(solution)/shard_map/ppermute | solution.py:330
  178.0 8.7 %collective-permute-start.24 = (f32[192,256]{1,0:T(8,128)}, f32[192,256]{1,0:T(8,128)S(1)}, u32[]{:S(2)}, u32[]{:S(2)}) collective-permute-start(f32[192,256]{1,0:T(8,128)} %copy-done.3), channel_id=1, source_target_pairs={{0,16},{16,0},{32,48},{48,32},{64,80},{80,64},{96,112},{112,96},{1... | collective-permute-start | bytes 589832 | tf_op jit(solution)/shard_map/ppermute | solution.py:330
  179.1 9.9 %collective-permute-start.26 = (f32[192,256]{1,0:T(8,128)S(1)}, f32[192,256]{1,0:T(8,128)S(1)}, u32[]{:S(2)}, u32[]{:S(2)}) collective-permute-start(f32[192,256]{1,0:T(8,128)S(1)} %add.54), channel_id=1, source_target_pairs={{0,64},{16,80},{32,96},{48,112},{64,128},{80,144},{96,160},{112,17... | collective-permute-start | bytes 589832 | tf_op jit(solution)/shard_map/ppermute | solution.py:333
  183.9 10.2 %collective-permute-start.28 = (f32[192,256]{1,0:T(8,128)S(1)}, f32[192,256]{1,0:T(8,128)S(1)}, u32[]{:S(2)}, u32[]{:S(2)}) collective-permute-start(f32[192,256]{1,0:T(8,128)S(1)} %add.56), channel_id=1, source_target_pairs={{0,128},{16,144},{32,160},{48,176},{64,192},{80,208},{96,224},{112... | collective-permute-start | bytes 589832 | tf_op jit(solution)/shard_map/ppermute | solution.py:333
  185.2 9.0 %collective-permute-start.30 = (f32[192,256]{1,0:T(8,128)S(1)}, f32[192,256]{1,0:T(8,128)S(1)}, u32[]{:S(2)}, u32[]{:S(2)}) collective-permute-start(f32[192,256]{1,0:T(8,128)S(1)} %add.58), channel_id=1, source_target_pairs={{0,192},{16,208},{32,224},{48,240},{64,0},{80,16},{96,32},{112,48}... | collective-permute-start | bytes 589832 | tf_op jit(solution)/shard_map/ppermute | solution.py:333
  194.3 7.6 %collective-permute-start.31 = (f32[96,256]{1,0:T(8,128)S(1)}, f32[96,256]{1,0:T(8,128)S(1)}, u32[]{:S(2)}, u32[]{:S(2)}) collective-permute-start(f32[96,256]{1,0:T(8,128)S(1)} %slice.35), channel_id=1, source_target_pairs={{0,32},{16,48},{32,0},{48,16},{64,96},{80,112},{96,64},{112,80},{1... | collective-permute-start | bytes 294920 | tf_op jit(solution)/shard_map/ppermute | solution.py:334
  (17 other events, 16.2 us)

commit v2 on v0

v2 whole, which is shorter than its diff:
```python
import jax
import jax.numpy as jnp
from jax import lax
from jax.experimental import pallas as pl
from jax.experimental.pallas import tpu as pltpu
from jax.sharding import Mesh
from jax.sharding import PartitionSpec as P


ROW = ("y", "zh", "core")
COL = ("x", "zl")
ROW_SIZES = (4, 2, 2)
COL_SIZES = (4, 4)
NV = 16
TILE = 256
SEGB = 6
CAP = 3
SEG = SEGB * NV
RID = 8
UNROLL = 4
F32 = jnp.float32
BF16 = jnp.bfloat16
HIGH = lax.Precision.HIGHEST
ACROSS = (((1,), (1,)), ((), ()))
MIB = 1024 * 1024


def vspec():
    return pl.BlockSpec(memory_space=pltpu.VMEM)


def sspec():
    return pl.BlockSpec(memory_space=pltpu.SMEM)


def hint(us):
    return pl.CostEstimate(flops=int(us * 1e9), bytes_accessed=0, transcendentals=0)


def params(mib):
    return pltpu.CompilerParams(vmem_limit_bytes=mib * MIB)


def turned(n, step):
    return [(i, (i + step) % n) for i in range(n)]


def prep_kernel(place, rows, cols, counts, table, slots, mark, used):
    n_segs = used.shape[0]

    def clear(b, _):
        mark[b] = -1
        return 0

    lax.fori_loop(0, n_segs * SEGB, clear, 0)

    def clear_table(s, _):
        used[s] = 0
        for q in range(CAP):
            table[s * CAP + q] = 0
        return 0

    lax.fori_loop(0, n_segs, clear_table, 0)
    my_y, my_half, my_core = place[0], place[1], place[2]

    def slot(k, _):
        b = rows[0, 0, k]
        s = b // SEGB
        old = mark[b]
        rank = jnp.where(old < 0, used[s], old)
        mark[b] = rank
        used[s] = jnp.where(old < 0, rank + 1, used[s])
        table[s * CAP + rank] = b - s * SEGB
        slots[0, k] = b
        slots[1, k] = s * CAP + rank
        g = cols[0, 0, k]
        t = g // SEGB
        step = (t // 4 + 4 - my_y) % 4
        half = (t // 2 % 2 + my_half) % 2
        core = (t % 2 + my_core) % 2
        slots[2, k] = ((core * 4 + step) * 2 + half) * SEGB + g - t * SEGB
        return 0

    lax.fori_loop(0, counts[0, 0], slot, 0)


def prep(rows, cols, counts, place):
    n_segs = 16
    return pl.pallas_call(
        prep_kernel,
        out_shape=(
            jax.ShapeDtypeStruct((n_segs * CAP,), jnp.int32),
            jax.ShapeDtypeStruct((3, rows.shape[-1]), jnp.int32),
        ),
        in_specs=[sspec()] * 4,
        out_specs=(sspec(), sspec()),
        scratch_shapes=[pltpu.SMEM((n_segs * SEGB,), jnp.int32), pltpu.SMEM((n_segs,), jnp.int32)],
        name="prep",
    )(place, rows, cols, counts)


def split(x):
    high = x.astype(BF16)
    return high, (x - high.astype(F32)).astype(BF16)


def tile_loop(count, tiles, held, sems, slot):
    def copy(k):
        return pltpu.make_async_copy(tiles.at[k], held.at[k], sems.at[k])

    def start(k, _):
        copy(k).start()
        return 0

    def one(k):
        slot(k, *split(held[k]))

    def group(g, _):
        for u in range(UNROLL):
            copy(g * UNROLL + u).wait()
        for u in range(UNROLL):
            one(g * UNROLL + u)
        return 0

    def single(k, _):
        copy(k).wait()
        one(k)
        return 0

    def run():
        whole = count // UNROLL
        lax.fori_loop(0, whole, group, 0)
        lax.fori_loop(whole * UNROLL, count, single, 0)

    lax.fori_loop(0, count, start, 0)
    return run


def put(vecs, at, block):
    high, low = split(block)
    vecs[at, 0:NV, :] = high
    vecs[at, NV : 2 * NV, :] = low


def rows_kernel(first, *refs):
    counts, slots, table, tiles = refs[:4]
    from_y = refs[4:12]
    to_x, held, sems, vecs, total = refs[12:]

    def slot(k, high, low):
        i = slots[1, k]
        v = vecs[slots[2, k]]
        a = lax.dot_general(v, high, ACROSS, preferred_element_type=F32)
        b = lax.dot_general(v[:NV], low, ACROSS, preferred_element_type=F32)
        total[i] += a[:NV] + a[NV:] + b

    run = tile_loop(counts[0, 0], tiles, held, sems, slot)
    n_segs = to_x.shape[0]
    for p in range(8):
        for h in range(2):
            for b in range(SEGB):
                at = (p * 2 + h) * SEGB + b
                if first:
                    put(vecs, at, from_y[p][h, :, b * TILE : (b + 1) * TILE])
                else:
                    put(vecs, at, from_y[p][(h * SEGB + b) * NV : (h * SEGB + b + 1) * NV, :])
    total[...] = jnp.zeros(total.shape, F32)
    run()
    if not first:
        carried = from_y[0][2 * SEG : 2 * SEG + RID, :]
        for p in range(1, 8):
            carried = carried + from_y[p][2 * SEG : 2 * SEG + RID, :]
    for s in range(n_segs):
        for q in range(CAP):
            to_x[s, q * NV : (q + 1) * NV, :] = total[s * CAP + q]
        if first:
            row_id = lax.broadcasted_iota(jnp.int32, (RID, TILE), 0)
            carried = jnp.zeros((RID, TILE), jnp.int32)
            for q in range(CAP):
                carried = jnp.where(row_id == q, table[s * CAP + q], carried)
            carried = carried.astype(F32)
        to_x[s, CAP * NV : CAP * NV + RID, :] = carried


def cols_kernel(first, *refs):
    counts, slots, tiles, from_x = refs[:4]
    to_y = refs[4:12]
    held, sems, vecs, total = refs[12:]

    def slot(k, high, low):
        j = slots[2, k]
        v = vecs[slots[0 if first else 1, k]]
        a = jnp.dot(v, high, preferred_element_type=F32)
        b = jnp.dot(v[:NV], low, preferred_element_type=F32)
        total[j] += a[:NV] + a[NV:] + b

    run = tile_loop(counts[0, 0], tiles, held, sems, slot)
    in_seg = SEGB if first else CAP
    for s in range(from_x.shape[0]):
        for q in range(in_seg):
            if first:
                put(vecs, s * in_seg + q, from_x[s, :, q * TILE : (q + 1) * TILE])
            else:
                put(vecs, s * in_seg + q, from_x[s, q * NV : (q + 1) * NV, :])
    total[...] = jnp.zeros(total.shape, F32)
    run()
    for p in range(8):
        for b in range(2 * SEGB):
            to_y[p][b * NV : (b + 1) * NV, :] = total[p * 2 * SEGB + b]


def tile_scratch(tiles):
    return [pltpu.VMEM(tiles.shape, F32), pltpu.SemaphoreType.DMA(tiles.shape[:1])]


def rows_product(counts, slots, table, tiles, from_y, first):
    def kernel(*refs):
        rows_kernel(first, *refs)

    return pl.pallas_call(
        kernel,
        out_shape=jax.ShapeDtypeStruct((16, CAP * NV + RID, TILE), F32),
        in_specs=[sspec()] * 3 + [pl.BlockSpec(memory_space=pltpu.HBM)] + [vspec()] * 8,
        out_specs=vspec(),
        scratch_shapes=tile_scratch(tiles)
        + [pltpu.VMEM((16 * SEGB, 2 * NV, TILE), BF16), pltpu.VMEM((16 * CAP, NV, TILE), F32)],
        compiler_params=params(24),
        cost_estimate=hint(10 if first else 5),
        name="rows_product",
    )(counts, slots, table, tiles, *from_y)


def cols_product(counts, slots, tiles, from_x, first):
    def kernel(*refs):
        cols_kernel(first, *refs)

    return pl.pallas_call(
        kernel,
        out_shape=(jax.ShapeDtypeStruct((2 * SEG, TILE), F32),) * 8,
        in_specs=[sspec()] * 2 + [pl.BlockSpec(memory_space=pltpu.HBM), vspec()],
        out_specs=(vspec(),) * 8,
        scratch_shapes=tile_scratch(tiles)
        + [
            pltpu.VMEM((16 * (SEGB if first else CAP), 2 * NV, TILE), BF16),
            pltpu.VMEM((16 * SEGB, NV, TILE), F32),
        ],
        compiler_params=params(24),
        cost_estimate=hint(5),
        name="cols_product",
    )(counts, slots, tiles, from_x)


def add_terms(wanted, from_x, total):
    for b in range(SEGB):
        at = slice(b * NV, (b + 1) * NV)
        block = total[at, :]
        for d in range(from_x.shape[0]):
            for q in range(CAP):
                term = from_x[d, q * NV : (q + 1) * NV, :]
                block = block + jnp.where(wanted[d, q : q + 1, :] == b, term, 0.0)
        total[at, :] = block


def near_kernel(from_x, wanted, total):
    total[...] = jnp.zeros(total.shape, F32)
    wanted[...] = from_x[:, CAP * NV : CAP * NV + RID, :]
    add_terms(wanted, from_x, total)


def near(from_x):
    return pl.pallas_call(
        near_kernel,
        out_shape=(
            jax.ShapeDtypeStruct((from_x.shape[0], RID, TILE), F32),
            jax.ShapeDtypeStruct((SEG, TILE), F32),
        ),
        in_specs=[vspec()],
        out_specs=(vspec(), vspec()),
        compiler_params=params(8),
        name="near",
    )(from_x)


def turn_kernel(wanted, near_mine, far_mine, far_theirs, product, message):
    for b in range(SEGB):
        at = slice(b * NV, (b + 1) * NV)
        product[at, :] = near_mine[at, :] + (far_mine[at, :] + far_theirs[at, :])
    for d in range(message.shape[0]):
        for q in range(CAP):
            want = wanted[d, q : q + 1, :]
            block = jnp.zeros((NV, TILE), F32)
            for b in range(SEGB):
                block = jnp.where(want == b, product[b * NV : (b + 1) * NV, :], block)
            message[d, q * NV : (q + 1) * NV, :] = block


def turn(wanted, near_mine, far_mine, far_theirs):
    return pl.pallas_call(
        turn_kernel,
        out_shape=(
            jax.ShapeDtypeStruct((SEG, TILE), F32),
            jax.ShapeDtypeStruct((wanted.shape[0], CAP * NV, TILE), F32),
        ),
        in_specs=[vspec()] * 4,
        out_specs=(vspec(), vspec()),
        compiler_params=params(8),
        name="turn",
    )(wanted, near_mine, far_mine, far_theirs)


def cross(a, b):
    return lax.dot_general(a, b, ACROSS, precision=HIGH, preferred_element_type=F32)


def fan_kernel(table, slots, mine, theirs, pair, correlation):
    pair[0] = mine[...]
    pair[1] = theirs[...]
    correlation[...] = cross(mine[...], mine[...]) + cross(theirs[...], theirs[...])


def fan(table, slots, mine, theirs):
    return pl.pallas_call(
        fan_kernel,
        out_shape=(
            jax.ShapeDtypeStruct((2,) + mine.shape, F32),
            jax.ShapeDtypeStruct((NV, NV), F32),
        ),
        in_specs=[sspec()] * 2 + [vspec()] * 2,
        out_specs=(vspec(),) * 2,
        compiler_params=params(8),
        cost_estimate=hint(20),
        name="fan",
    )(table, slots, mine, theirs)


def load_kernel(product, other, mine, theirs, correlation, ride):
    ride[0:SEG, :] = product[...]
    ride[SEG : 2 * SEG, :] = other[...]
    projection = jnp.zeros((NV, NV), F32)
    for h, vectors in enumerate((mine, theirs)):
        for b in range(SEGB):
            at = (h * SEGB + b) * NV
            projection += cross(vectors[:, b * TILE : (b + 1) * TILE], ride[at : at + NV, :])
    ride[2 * SEG : 2 * SEG + RID, :] = jnp.zeros((RID, TILE), F32)
    for at, matrix in ((0, correlation[...]), (2, projection)):
        for h in range(2):
            ride[2 * SEG : 2 * SEG + RID, (at + h) * NV : (at + h + 1) * NV] = matrix[h * RID : (h + 1) * RID, :]


def load(product, other, mine, theirs, correlation):
    return pl.pallas_call(
        load_kernel,
        out_shape=jax.ShapeDtypeStruct((2 * SEG + RID, TILE), F32),
        in_specs=[vspec()] * 5,
        out_specs=vspec(),
        compiler_params=params(4),
        cost_estimate=hint(50),
        name="load",
    )(product, other, mine, theirs, correlation)


def solve(correlation, projection):
    m = jnp.concatenate([correlation, projection], axis=1)
    row_id = lax.broadcasted_iota(jnp.int32, m.shape, 0)
    for j in range(NV):
        row = m[j : j + 1, :] / m[j : j + 1, j : j + 1]
        m = jnp.where(row_id == j, row, m - m[:, j : j + 1] * row)
    return m[:, NV:]


def finish_kernel(wanted, from_x, both, mine, theirs, pair, residual, image, gram, total):
    total[...] = both[0:SEG, :]
    add_terms(wanted, from_x, total)
    carried = from_x[0, CAP * NV : CAP * NV + RID, :]
    for d in range(1, from_x.shape[0]):
        carried = carried + from_x[d, CAP * NV : CAP * NV + RID, :]
    correlation, projection = (
        jnp.concatenate([carried[:, (at + h) * NV : (at + h + 1) * NV] for h in range(2)], axis=0) for at in (0, 2)
    )
    coeffs = solve(correlation, projection)
    back = coeffs.T
    local = jnp.zeros((NV, NV), F32)
    for b in range(SEGB):
        at = slice(b * NV, (b + 1) * NV)
        other = slice(SEG + b * NV, SEG + (b + 1) * NV)
        cols = slice(b * TILE, (b + 1) * TILE)
        p = pair[at, :]
        r = p - jnp.dot(back, mine[:, cols], precision=HIGH, preferred_element_type=F32)
        m = total[at, :] - jnp.dot(back, p, precision=HIGH, preferred_element_type=F32)
        residual[:, cols] = r
        image[:, cols] = m
        r_other = pair[other, :] - jnp.dot(back, theirs[:, cols], precision=HIGH, preferred_element_type=F32)
        local += cross(r, m) + cross(r_other, both[other, :])
    for d in range(gram.shape[0]):
        gram[d] = jnp.zeros(gram.shape[1:], F32)
        for h in range(2):
            gram[d, :, h * NV : (h + 1) * NV] = local[h * RID : (h + 1) * RID, :]


def finish(wanted, from_x, both, mine, theirs, pair):
    return pl.pallas_call(
        finish_kernel,
        out_shape=(
            jax.ShapeDtypeStruct(mine.shape, F32),
            jax.ShapeDtypeStruct(mine.shape, F32),
            jax.ShapeDtypeStruct((16, RID, 128), F32),
        ),
        in_specs=[vspec()] * 6,
        out_specs=(vspec(),) * 3,
        scratch_shapes=[pltpu.VMEM((SEG, TILE), F32)],
        compiler_params=params(8),
        name="finish",
    )(wanted, from_x, both, mine, theirs, pair)


def last_kernel(part, far, image):
    for b in range(SEGB):
        cols = slice(b * TILE, (b + 1) * TILE)
        image[:, cols] = part[:, cols] + far[b * NV : (b + 1) * NV, :]


def last(part, far):
    return pl.pallas_call(
        last_kernel,
        out_shape=jax.ShapeDtypeStruct(part.shape, F32),
        in_specs=[vspec()] * 2,
        out_specs=vspec(),
        compiler_params=params(4),
        name="last",
    )(part, far)


def swap(x, axis):
    return lax.all_to_all(x, axis, 0, 0, tiled=True)


def other_half(x):
    return lax.ppermute(x, "zh", turned(2, 1))


def other_core(x):
    return lax.ppermute(x, "core", turned(2, 1))


def spread(mine):
    pieces = [mine] + [lax.ppermute(mine, "y", turned(4, -step)) for step in (1, 2, 3)]
    return pieces + [other_core(x) for x in pieces]


def collect(pieces):
    met = [a + other_core(b) for a, b in zip(pieces[:4], pieces[4:])]
    both = met[0]
    for step in (1, 2, 3):
        both = both + lax.ppermute(met[step], "y", turned(4, step))
    return both


def per_device(vectors, tiles, tile_rows, tile_cols, counts):
    cell_tiles = pltpu.with_memory_space_constraint(tiles[0, 0], pltpu.HBM)
    order_total = vectors.shape[1] * lax.axis_size(ROW) * lax.axis_size(COL)
    place = jnp.stack([lax.axis_index(name).astype(jnp.int32) for name in ROW])
    table, slots = prep(tile_rows, tile_cols, counts, place)

    theirs = other_half(vectors)
    both, correlation = fan(table, slots, vectors, theirs)
    from_y = spread(both)
    line = swap(jnp.broadcast_to(vectors, (4,) + vectors.shape), "zl")
    from_x = swap(jnp.broadcast_to(line, (4,) + line.shape), "x").reshape((16,) + vectors.shape)
    to_x = rows_product(counts, slots, table, cell_tiles, from_y, True)
    to_y = cols_product(counts, slots, cell_tiles, from_x, True)
    from_x = swap(to_x, COL)
    both = collect(to_y)
    far = other_half(both[SEG:])
    wanted, mine = near(from_x)
    product, message = turn(wanted, mine, both, far)

    from_x = swap(message, COL)
    pair = load(product, other_half(product), vectors, theirs, correlation)
    from_y = spread(pair)
    to_x = rows_product(counts, slots, table, cell_tiles, from_y, False)
    to_y = cols_product(counts, slots, cell_tiles, from_x, False)
    from_x = swap(to_x, COL)
    both = collect(to_y)
    residual, part, local = finish(wanted, from_x, both, vectors, theirs, pair)
    image = last(part, other_half(both[SEG:]))

    some = jnp.sum(swap(local, ("zh", "zl", "core")), axis=0)
    total = jnp.sum(swap(jnp.broadcast_to(some, local.shape), ("x", "y")), axis=0)
    gram = jnp.concatenate([total[:, :NV], total[:, NV : 2 * NV]], axis=0) / order_total
    return (residual, image, gram)


def solution(mesh):
    fine = Mesh(mesh.devices.reshape(ROW_SIZES + COL_SIZES), ROW + COL)
    in_specs = (
        P(None, ROW + COL),
        P(ROW, COL, None, None, None),
        P(ROW, COL, None),
        P(ROW, COL, None),
        P(ROW, COL),
    )
    out_specs = (P(None, ROW + COL), P(None, ROW + COL), P())
    return jax.shard_map(
        per_device, mesh=fine, in_specs=in_specs, out_specs=out_specs, check_vma=False
    )
```

time: 815 us -> 181 us (0.22)
  waiting for transfers between devices: 541 us -> 52.1 us
  blocking collectives: 169 us -> 0 us
  starting transfers between devices: 0.96 us -> 95.6 us
  matrix products: 59.3 us -> 0 us
  Pallas kernels: 0 us -> 24.6 us
  between operations: 15.4 us -> 1.55 us
  local copies, waits for them, and re-layouts: 16.7 us -> 6.02 us
    reduce_scatter x4 -> x0, waiting for transfers between devices: 280 us -> none  [the longest x2 158 us: reduce_rows(): lax.psum_scatter(row_terms.reshape(width, -1), 'col', scatter_dimension=1...]
    all_gather x4 -> x0, waiting for transfers between devices: 260 us -> none  [the longest x2 150 us: apply_whole(): row_group = lax.all_gather(block, 'col', axis=1, tiled=True)]
    psum x2 -> x0, blocking collectives: 169 us -> none  [the longest x1 84.7 us: per_device(): lax.psum((local_correlation, local_projection), ('row', 'col'))]
    dot_general x16 -> x0, matrix products: 58.9 us -> none  [the longest x2 27.2 us: local_products(): jnp.einsum('kij,vkj->vki', cell_tiles, from_cols, precision=lax.Precision...]
    ppermute x0 -> x32, starting transfers between devices: none -> 51.9 us  [the longest x16 21.3 us: other_core(): return lax.ppermute(x, 'core', turned(2, 1))]
    all_to_all x0 -> x7, starting transfers between devices: none -> 43.7 us  [swap(): return lax.all_to_all(x, axis, 0, 0, tiled=True)]
    ppermute x0 -> x32, waiting for transfers between devices: none -> 26.6 us  [the longest x6 17.2 us: collect(): both = both + lax.ppermute(met[step], 'y', turned(4, step))]
    all_to_all x0 -> x7, waiting for transfers between devices: none -> 25.5 us  [swap(): return lax.all_to_all(x, axis, 0, 0, tiled=True)]
  transfers between devices with their start and end apart: 8 -> 39, of which waited for: 8 -> 20; matrix products, arithmetic and copies ran while one was open for 9% -> 3% of each run, Pallas kernels for 0% -> 11%
where the time goes in v2:
time: 181 us
  starting transfers between devices  95.6 us (53%)
  waiting for transfers between devices  52.1 us (29%)
  Pallas kernels  24.6 us (14%)
  local copies, waits for them, and re-layouts  6.02 us (3%)
    all_to_all x7, starting transfers between devices, swap(): return lax.all_to_all(x, axis, 0, 0, tiled=True)  43.7 us
    all_to_all x7, waiting for transfers between devices, swap(): return lax.all_to_all(x, axis, 0, 0, tiled=True)  25.5 us
    ppermute x16, starting transfers between devices, other_core(): return lax.ppermute(x, 'core', turned(2, 1))  21.3 us
    ppermute x6, waiting for transfers between devices, collect(): both = both + lax.ppermute(met[step], 'y', turned(4, step))  17.2 us
    ppermute x4, starting transfers between devices, other_half(): return lax.ppermute(x, 'zh', turned(2, 1))  14.8 us
    ppermute x6, starting transfers between devices, spread(): lax.ppermute(mine, 'y', turned(4, -step))  8.56 us
    pallas_call x2, Pallas kernels, rows_product(): pl.pallas_call(kernel, out_shape=jax.ShapeDtypeStruct((16, CAP * NV + RID...  8.39 us
    ppermute x6, starting transfers between devices, collect(): both = both + lax.ppermute(met[step], 'y', turned(4, step))  7.25 us
  transfers between devices with their start and end apart: 39, of which 20 were waited for; matrix products, arithmetic and copies ran while one was open for 3% of the time, Pallas kernels for 11%

profile of v2, /device:TPU:1, one launch (start us, length us, event | category | flops | bytes accessed | tf_op | source)
XLA Modules:
  0.0 181.4 jit_solution(5322623229427356369)
XLA Ops:
  0.6 7.8 %collective-permute-start = (f32[16,1536]{1,0:T(8,128)}, f32[16,1536]{1,0:T(8,128)S(1)}, u32[]{:S(2)}, u32[]{:S(2)}) collective-permute-start(f32[16,1536]{1,0:T(8,128)} %mine.5), channel_id=1, source_target_pairs={{0,32},{32,0},{1,33},{33,1},{2,34},{34,2},{3,35},{35,3},{4,36},{36... | collective-permute-start | bytes 294920 | tf_op jit(solution)/shard_map/ppermute | solution.py:438
  10.2 3.5 %all-to-all-start.1 = ((f32[4,16,1536]{2,1,0:T(8,128)}), f32[4,16,1536]{2,1,0:T(8,128)S(1)}, u32[]{:S(2)}, u32[]{:S(2)}) async-start(f32[4,16,1536]{2,1,0:T(8,128)} %broadcast_in_dim.9), calls=%async_computation.1 | async-start | bytes 786432 | tf_op jit(solution)/shard_map/all_to_all | solution.py:434
  15.0 2.3 %prep.1 = (s32[48]{0:T(128)}, s32[3,48]{1,0:T(4,128)}) custom-call(s32[3]{0:T(128)} %pad_add_fusion.place, s32[1,1,48]{2,1,0:T(1,128)} %rows.1, s32[1,1,48]{2,1,0:T(1,128)} %cols.1, s32[1,1]{1,0:T(1,128)S(6)} %copy.8.counts.refs_0_), custom_call_target="tpu_custom_call" | custom-call | tf_op jit(solution)/shard_map/prep/pallas_call | solution.py:89
  20.5 3.0 %collective-permute-start.1 = (f32[2,16,1536]{2,1,0:T(8,128)S(1)}, f32[2,16,1536]{2,1,0:T(8,128)S(1)}, u32[]{:S(2)}, u32[]{:S(2)}) collective-permute-start(f32[2,16,1536]{2,1,0:T(8,128)S(1)} %get-tuple-element.32.refs_4_), channel_id=1, source_target_pairs={{0,192},{64,0},{128,64},{192,128},{1,193},{65,1},{129,65},{193,129... | collective-permute-start | bytes 589832 | tf_op jit(solution)/shard_map/ppermute | solution.py:446
  25.8 4.1 %all-to-all-start.2 = ((f32[4,4,16,1536]{3,2,1,0:T(8,128)}), f32[4,4,16,1536]{3,2,1,0:T(8,128)S(1)}, u32[]{:S(2)}, u32[]{:S(2)}) async-start(f32[4,4,16,1536]{3,2,1,0:T(8,128)} %broadcast_in_dim.10), calls=%async_computation.2 | async-start | bytes 3145728 | tf_op jit(solution)/shard_map/all_to_all | solution.py:434
  37.5 4.2 %rows_product.2 = f32[16,56,256]{2,1,0:T(8,128)} custom-call(s32[1,1]{1,0:T(1,128)S(6)} %copy.8.counts.refs_0_, s32[3,48]{1,0:T(4,128)S(1)} %copy-done.3, s32[48]{0:T(128)S(1)} %copy-done.5, f32[48,256,256]{2,1,0:T(8,128)} %bitcast.6, f32[2,16,1536]{2,1,0:T(8,128)S(1)} %get-tuple-element.32.refs_4_, f32[2,16,1536]{2,1,0:T(8,128)S(1)} %collective-permute-done.1.refs_5_, ...), custom_call_target="tpu_custom_call" | custom-call | flops 10000000000 | tf_op jit(solution)/shard_map/rows_product/pallas_call | solution.py:220
  41.6 7.1 %all-to-all-done.2 = f32[4,4,16,1536]{3,2,1,0:T(8,128)S(1)} async-done(((f32[4,4,16,1536]{3,2,1,0:T(8,128)}), f32[4,4,16,1536]{3,2,1,0:T(8,128)S(1)}, u32[]{:S(2)}, u32[]{:S(2)}) %all-to-all-start.2) | async-done | bytes 1572896 | tf_op jit(solution)/shard_map/all_to_all | solution.py:434
  48.7 6.1 %all-to-all-start = ((f32[16,56,256]{2,1,0:T(8,128)}), f32[16,56,256]{2,1,0:T(8,128)S(1)}, u32[]{:S(2)}, u32[]{:S(2)}) async-start(f32[16,56,256]{2,1,0:T(8,128)} %rows_product.2), calls=%async_computation | async-start | bytes 1835008 | tf_op jit(solution)/shard_map/all_to_all | solution.py:434
  54.8 3.0 %cols_product.2 = (f32[192,256]{1,0:T(8,128)S(1)}, f32[192,256]{1,0:T(8,128)S(1)}, f32[192,256]{1,0:T(8,128)S(1)}, f32[192,256]{1,0:T(8,128)S(1)}, f32[192,256]{...) custom-call(s32[1,1]{1,0:T(1,128)S(6)} %copy.8.counts.refs_0_, ...), custom_call_target="tpu_custom_call" | custom-call | flops 5000000000 | tf_op jit(solution)/shard_map/cols_product/pallas_call | solution.py:237
  57.9 3.3 %collective-permute-start.9 = (f32[192,256]{1,0:T(8,128)S(1)}, f32[192,256]{1,0:T(8,128)S(1)}, u32[]{:S(2)}, u32[]{:S(2)}) collective-permute-start(f32[192,256]{1,0:T(8,128)S(1)} %get-tuple-element.38), channel_id=1, source_target_pairs={{0,16},{16,0},{1,17},{17,1},{2,18},{18,2},{3,19},{19,3},{4,20},{20... | collective-permute-start | bytes 589832 | tf_op jit(solution)/shard_map/ppermute | solution.py:442
  62.9 3.4 %collective-permute-start.12 = (f32[192,256]{1,0:T(8,128)S(1)}, f32[192,256]{1,0:T(8,128)S(1)}, u32[]{:S(2)}, u32[]{:S(2)}) collective-permute-start(f32[192,256]{1,0:T(8,128)S(1)} %add.45), channel_id=1, source_target_pairs={{0,128},{64,192},{128,0},{192,64},{1,129},{65,193},{129,1},{193,65... | collective-permute-start | bytes 589832 | tf_op jit(solution)/shard_map/ppermute | solution.py:454
  66.5 3.2 %collective-permute-done.10 = f32[192,256]{1,0:T(8,128)S(1)} collective-permute-done((f32[192,256]{1,0:T(8,128)S(1)}, f32[192,256]{1,0:T(8,128)S(1)}, u32[]{:S(2)}, u32[]{:S(2)}) %collective-permute-start.10) | collective-permute-done | bytes 196640 | tf_op jit(solution)/shard_map/ppermute | solution.py:454
  69.7 5.4 %collective-permute-done.12 = f32[192,256]{1,0:T(8,128)S(1)} collective-permute-done((f32[192,256]{1,0:T(8,128)S(1)}, f32[192,256]{1,0:T(8,128)S(1)}, u32[]{:S(2)}, u32[]{:S(2)}) %collective-permute-start.12) | collective-permute-done | bytes 196640 | tf_op jit(solution)/shard_map/ppermute | solution.py:454
  76.1 2.5 %all-to-all-done.from_x = f32[16,56,256]{2,1,0:T(8,128)S(1)} async-done(((f32[16,56,256]{2,1,0:T(8,128)}), f32[16,56,256]{2,1,0:T(8,128)S(1)}, u32[]{:S(2)}, u32[]{:S(2)}) %all-to-all-start) | async-done | bytes 917536 | tf_op jit(solution)/shard_map/all_to_all | solution.py:434
  79.1 3.7 %collective-permute-done.15.far_theirs = f32[96,256]{1,0:T(8,128)S(1)} collective-permute-done((f32[96,256]{1,0:T(8,128)S(1)}, f32[96,256]{1,0:T(8,128)S(1)}, u32[]{:S(2)}, u32[]{:S(2)}) %collective-permute-start.15) | collective-permute-done | bytes 98336 | tf_op jit(solution)/shard_map/ppermute | solution.py:438
  84.7 9.1 %all-to-all-start.4 = ((f32[16,48,256]{2,1,0:T(8,128)}), f32[16,48,256]{2,1,0:T(8,128)S(1)}, u32[]{:S(2)}, u32[]{:S(2)}) async-start(f32[16,48,256]{2,1,0:T(8,128)} %get-tuple-element.45), calls=%async_computation.4 | async-start | bytes 1572864 | tf_op jit(solution)/shard_map/all_to_all | solution.py:434
  94.3 3.5 %collective-permute-start.17 = (f32[200,256]{1,0:T(8,128)S(1)}, f32[200,256]{1,0:T(8,128)S(1)}, u32[]{:S(2)}, u32[]{:S(2)}) collective-permute-start(f32[200,256]{1,0:T(8,128)S(1)} %load.1.refs_4_.pair), channel_id=1, source_target_pairs={{0,192},{64,0},{128,64},{192,128},{1,193},{65,1},{129,65},{193,129... | collective-permute-start | bytes 614408 | tf_op jit(solution)/shard_map/ppermute | solution.py:446
  98.9 3.8 %collective-permute-start.20 = (f32[200,256]{1,0:T(8,128)S(1)}, f32[200,256]{1,0:T(8,128)S(1)}, u32[]{:S(2)}, u32[]{:S(2)}) collective-permute-start(f32[200,256]{1,0:T(8,128)S(1)} %load.1.refs_4_.pair), channel_id=1, source_target_pairs={{0,16},{16,0},{1,17},{17,1},{2,18},{18,2},{3,19},{19,3},{4,20},{20... | collective-permute-start | bytes 614408 | tf_op jit(solution)/shard_map/ppermute | solution.py:442
  103.2 4.4 %collective-permute-start.21 = (f32[200,256]{1,0:T(8,128)S(1)}, f32[200,256]{1,0:T(8,128)S(1)}, u32[]{:S(2)}, u32[]{:S(2)}) collective-permute-start(f32[200,256]{1,0:T(8,128)S(1)} %collective-permute-done.17.refs_5_), channel_id=1, source_target_pairs={{0,16},{16,0},{1,17},{17,1},{2,18},{18,2},{3,19},{19,3},{4,20},{20... | collective-permute-start | bytes 614408 | tf_op jit(solution)/shard_map/ppermute | solution.py:442
  112.2 4.2 %rows_product.3 = f32[16,56,256]{2,1,0:T(8,128)} custom-call(s32[1,1]{1,0:T(1,128)S(6)} %copy.8.counts.refs_0_, s32[3,48]{1,0:T(4,128)S(1)} %copy-done.3, s32[48]{0:T(128)S(1)} %copy-done.5, f32[48,256,256]{2,1,0:T(8,128)} %bitcast.8, f32[200,256]{1,0:T(8,128)S(1)} %load.1.refs_4_.pair, f32[200,256]{1,0:T(8,128)S(1)} %collective-permute-done.17.refs_5_, ...), custom_call_target="tpu_custom_call" | custom-call | flops 5000000000 | tf_op jit(solution)/shard_map/rows_product/pallas_call | solution.py:220
  116.5 10.7 %all-to-all-start.3 = ((f32[16,56,256]{2,1,0:T(8,128)}), f32[16,56,256]{2,1,0:T(8,128)S(1)}, u32[]{:S(2)}, u32[]{:S(2)}) async-start(f32[16,56,256]{2,1,0:T(8,128)} %rows_product.3), calls=%async_computation.3 | async-start | bytes 1835008 | tf_op jit(solution)/shard_map/all_to_all | solution.py:434
  127.2 3.0 %cols_product.3 = (f32[192,256]{1,0:T(8,128)S(1)}, f32[192,256]{1,0:T(8,128)S(1)}, f32[192,256]{1,0:T(8,128)S(1)}, f32[192,256]{1,0:T(8,128)S(1)}, f32[192,256]{...) custom-call(s32[1,1]{1,0:T(1,128)S(6)} %copy.8.counts.refs_0_, ...), custom_call_target="tpu_custom_call" | custom-call | flops 5000000000 | tf_op jit(solution)/shard_map/cols_product/pallas_call | solution.py:237
  132.3 2.7 %collective-permute-start.28 = (f32[192,256]{1,0:T(8,128)S(1)}, f32[192,256]{1,0:T(8,128)S(1)}, u32[]{:S(2)}, u32[]{:S(2)}) collective-permute-start(f32[192,256]{1,0:T(8,128)S(1)} %add.52), channel_id=1, source_target_pairs={{0,128},{64,192},{128,0},{192,64},{1,129},{65,193},{129,1},{193,65... | collective-permute-start | bytes 589832 | tf_op jit(solution)/shard_map/ppermute | solution.py:454
  135.4 3.9 %collective-permute-done.26 = f32[192,256]{1,0:T(8,128)S(1)} collective-permute-done((f32[192,256]{1,0:T(8,128)S(1)}, f32[192,256]{1,0:T(8,128)S(1)}, u32[]{:S(2)}, u32[]{:S(2)}) %collective-permute-start.26) | collective-permute-done | bytes 196640 | tf_op jit(solution)/shard_map/ppermute | solution.py:454
  139.3 4.4 %collective-permute-done.28 = f32[192,256]{1,0:T(8,128)S(1)} collective-permute-done((f32[192,256]{1,0:T(8,128)S(1)}, f32[192,256]{1,0:T(8,128)S(1)}, u32[]{:S(2)}, u32[]{:S(2)}) %collective-permute-start.28) | collective-permute-done | bytes 196640 | tf_op jit(solution)/shard_map/ppermute | solution.py:454
  144.0 7.4 %all-to-all-done.3.from_x = f32[16,56,256]{2,1,0:T(8,128)S(1)} async-done(((f32[16,56,256]{2,1,0:T(8,128)}), f32[16,56,256]{2,1,0:T(8,128)S(1)}, u32[]{:S(2)}, u32[]{:S(2)}) %all-to-all-start.3) | async-done | bytes 917536 | tf_op jit(solution)/shard_map/all_to_all | solution.py:434
  151.4 4.0 %finish.1 = (f32[16,1536]{1,0:T(8,128)}, f32[16,1536]{1,0:T(8,128)S(1)}, f32[16,8,128]{2,1,0:T(8,128)}) custom-call(f32[16,8,256]{2,1,0:T(8,128)S(1)} %get-tuple-element.33.wanted, f32[16,56,256]{2,1,0:T(8,128)S(1)} %all-to-all-done.3.from_x, f32[192,256]{1,0:T(8,128)S(1)} %add_add_fusion.both, f32[16,1536]{1,0:T(8,128)S(1)} %copy-done.1, ...), custom_call_target="tpu_custom_call" | custom-call | tf_op jit(solution)/shard_map/finish/pallas_call | solution.py:401
  155.4 5.0 %all-to-all-start.5 = ((f32[16,8,128]{2,1,0:T(8,128)}), f32[16,8,128]{2,1,0:T(8,128)S(1)}, u32[]{:S(2)}, u32[]{:S(2)}) async-start(f32[16,8,128]{2,1,0:T(8,128)} %get-tuple-element.56), calls=%async_computation.5 | async-start | bytes 131072 | tf_op jit(solution)/shard_map/all_to_all | solution.py:434
  160.4 5.4 %collective-permute-start.31 = (f32[96,256]{1,0:T(8,128)S(1)}, f32[96,256]{1,0:T(8,128)S(1)}, u32[]{:S(2)}, u32[]{:S(2)}) collective-permute-start(f32[96,256]{1,0:T(8,128)S(1)} %slice.17), channel_id=1, source_target_pairs={{0,32},{32,0},{1,33},{33,1},{2,34},{34,2},{3,35},{35,3},{4,36},{36... | collective-permute-start | bytes 294920 | tf_op jit(solution)/shard_map/ppermute | solution.py:438
  165.8 2.6 %all-to-all-done.5 = f32[16,8,128]{2,1,0:T(8,128)S(1)} async-done(((f32[16,8,128]{2,1,0:T(8,128)}), f32[16,8,128]{2,1,0:T(8,128)S(1)}, u32[]{:S(2)}, u32[]{:S(2)}) %all-to-all-start.5) | async-done | bytes 65568 | tf_op jit(solution)/shard_map/all_to_all | solution.py:434
  169.1 5.1 %all-to-all-start.6 = ((f32[16,8,128]{2,1,0:T(8,128)}), f32[16,8,128]{2,1,0:T(8,128)S(1)}, u32[]{:S(2)}, u32[]{:S(2)}) async-start(f32[16,8,128]{2,1,0:T(8,128)} %broadcast_in_dim.11), calls=%async_computation.6 | async-start | bytes 131072 | tf_op jit(solution)/shard_map/all_to_all | solution.py:434
  174.9 5.8 %all-to-all-done.6 = f32[16,8,128]{2,1,0:T(8,128)S(1)} async-done(((f32[16,8,128]{2,1,0:T(8,128)}), f32[16,8,128]{2,1,0:T(8,128)S(1)}, u32[]{:S(2)}, u32[]{:S(2)}) %all-to-all-start.6) | async-done | bytes 65568 | tf_op jit(solution)/shard_map/all_to_all | solution.py:434
  (87 shorter events, 31.9 us)
Async XLA Ops:
  0.6 16.6 %collective-permute-start = (f32[16,1536]{1,0:T(8,128)}, f32[16,1536]{1,0:T(8,128)S(1)}, u32[]{:S(2)}, u32[]{:S(2)}) collective-permute-start(f32[16,1536]{1,0:T(8,128)} %mine.5), channel_id=1, source_target_pairs={{0,32},{32,0},{1,33},{33,1},{2,34},{34,2},{3,35},{35,3},{4,36},{36... | collective-permute-start | bytes 294920 | tf_op jit(solution)/shard_map/ppermute | solution.py:438
  10.2 14.3 %all-to-all-start.1 = ((f32[4,16,1536]{2,1,0:T(8,128)}), f32[4,16,1536]{2,1,0:T(8,128)S(1)}, u32[]{:S(2)}, u32[]{:S(2)}) async-start(f32[4,16,1536]{2,1,0:T(8,128)} %broadcast_in_dim.9), calls=%async_computation.1 | async-start | bytes 786432 | tf_op jit(solution)/shard_map/all_to_all | solution.py:434
  20.5 11.6 %collective-permute-start.1 = (f32[2,16,1536]{2,1,0:T(8,128)S(1)}, f32[2,16,1536]{2,1,0:T(8,128)S(1)}, u32[]{:S(2)}, u32[]{:S(2)}) collective-permute-start(f32[2,16,1536]{2,1,0:T(8,128)S(1)} %get-tuple-element.32.refs_4_), channel_id=1, source_target_pairs={{0,192},{64,0},{128,64},{192,128},{1,193},{65,1},{129,65},{193,129... | collective-permute-start | bytes 589832 | tf_op jit(solution)/shard_map/ppermute | solution.py:446
  23.5 9.3 %collective-permute-start.2 = (f32[2,16,1536]{2,1,0:T(8,128)S(1)}, f32[2,16,1536]{2,1,0:T(8,128)S(1)}, u32[]{:S(2)}, u32[]{:S(2)}) collective-permute-start(f32[2,16,1536]{2,1,0:T(8,128)S(1)} %get-tuple-element.32.refs_4_), channel_id=1, source_target_pairs={{0,128},{64,192},{128,0},{192,64},{1,129},{65,193},{129,1},{193,65... | collective-permute-start | bytes 589832 | tf_op jit(solution)/shard_map/ppermute | solution.py:446
  23.6 12.1 %collective-permute-start.3 = (f32[2,16,1536]{2,1,0:T(8,128)S(1)}, f32[2,16,1536]{2,1,0:T(8,128)S(1)}, u32[]{:S(2)}, u32[]{:S(2)}) collective-permute-start(f32[2,16,1536]{2,1,0:T(8,128)S(1)} %get-tuple-element.32.refs_4_), channel_id=1, source_target_pairs={{0,64},{64,128},{128,192},{192,0},{1,65},{65,129},{129,193},{193,1... | collective-permute-start | bytes 589832 | tf_op jit(solution)/shard_map/ppermute | solution.py:446
  25.8 22.9 %all-to-all-start.2 = ((f32[4,4,16,1536]{3,2,1,0:T(8,128)}), f32[4,4,16,1536]{3,2,1,0:T(8,128)S(1)}, u32[]{:S(2)}, u32[]{:S(2)}) async-start(f32[4,4,16,1536]{3,2,1,0:T(8,128)} %broadcast_in_dim.10), calls=%async_computation.2 | async-start | bytes 3145728 | tf_op jit(solution)/shard_map/all_to_all | solution.py:434
  30.0 6.4 %collective-permute-start.4 = (f32[2,16,1536]{2,1,0:T(8,128)S(1)}, f32[2,16,1536]{2,1,0:T(8,128)S(1)}, u32[]{:S(2)}, u32[]{:S(2)}) collective-permute-start(f32[2,16,1536]{2,1,0:T(8,128)S(1)} %get-tuple-element.32.refs_4_), channel_id=1, source_target_pairs={{0,16},{16,0},{1,17},{17,1},{2,18},{18,2},{3,19},{19,3},{4,20},{20... | collective-permute-start | bytes 589832 | tf_op jit(solution)/shard_map/ppermute | solution.py:442
  32.0 4.4 %collective-permute-start.5 = (f32[2,16,1536]{2,1,0:T(8,128)S(1)}, f32[2,16,1536]{2,1,0:T(8,128)S(1)}, u32[]{:S(2)}, u32[]{:S(2)}) collective-permute-start(f32[2,16,1536]{2,1,0:T(8,128)S(1)} %collective-permute-done.1.refs_5_), channel_id=1, source_target_pairs={{0,16},{16,0},{1,17},{17,1},{2,18},{18,2},{3,19},{19,3},{4,20},{20... | collective-permute-start | bytes 589832 | tf_op jit(solution)/shard_map/ppermute | solution.py:442
  48.7 29.9 %all-to-all-start = ((f32[16,56,256]{2,1,0:T(8,128)}), f32[16,56,256]{2,1,0:T(8,128)S(1)}, u32[]{:S(2)}, u32[]{:S(2)}) async-start(f32[16,56,256]{2,1,0:T(8,128)} %rows_product.2), calls=%async_computation | async-start | bytes 1835008 | tf_op jit(solution)/shard_map/all_to_all | solution.py:434
  57.9 4.4 %collective-permute-start.9 = (f32[192,256]{1,0:T(8,128)S(1)}, f32[192,256]{1,0:T(8,128)S(1)}, u32[]{:S(2)}, u32[]{:S(2)}) collective-permute-start(f32[192,256]{1,0:T(8,128)S(1)} %get-tuple-element.38), channel_id=1, source_target_pairs={{0,16},{16,0},{1,17},{17,1},{2,18},{18,2},{3,19},{19,3},{4,20},{20... | collective-permute-start | bytes 589832 | tf_op jit(solution)/shard_map/ppermute | solution.py:442
  61.3 5.1 %collective-permute-start.13 = (f32[192,256]{1,0:T(8,128)S(1)}, f32[192,256]{1,0:T(8,128)S(1)}, u32[]{:S(2)}, u32[]{:S(2)}) collective-permute-start(f32[192,256]{1,0:T(8,128)S(1)} %get-tuple-element.42), channel_id=1, source_target_pairs={{0,16},{16,0},{1,17},{17,1},{2,18},{18,2},{3,19},{19,3},{4,20},{20... | collective-permute-start | bytes 589832 | tf_op jit(solution)/shard_map/ppermute | solution.py:442
  61.7 4.8 %collective-permute-start.8 = (f32[192,256]{1,0:T(8,128)S(1)}, f32[192,256]{1,0:T(8,128)S(1)}, u32[]{:S(2)}, u32[]{:S(2)}) collective-permute-start(f32[192,256]{1,0:T(8,128)S(1)} %get-tuple-element.36), channel_id=1, source_target_pairs={{0,16},{16,0},{1,17},{17,1},{2,18},{18,2},{3,19},{19,3},{4,20},{20... | collective-permute-start | bytes 589832 | tf_op jit(solution)/shard_map/ppermute | solution.py:442
  62.3 7.4 %collective-permute-start.10 = (f32[192,256]{1,0:T(8,128)S(1)}, f32[192,256]{1,0:T(8,128)S(1)}, u32[]{:S(2)}, u32[]{:S(2)}) collective-permute-start(f32[192,256]{1,0:T(8,128)S(1)} %add.43), channel_id=1, source_target_pairs={{0,64},{64,128},{128,192},{192,0},{1,65},{65,129},{129,193},{193,1... | collective-permute-start | bytes 589832 | tf_op jit(solution)/shard_map/ppermute | solution.py:454
  62.9 12.1 %collective-permute-start.12 = (f32[192,256]{1,0:T(8,128)S(1)}, f32[192,256]{1,0:T(8,128)S(1)}, u32[]{:S(2)}, u32[]{:S(2)}) collective-permute-start(f32[192,256]{1,0:T(8,128)S(1)} %add.45), channel_id=1, source_target_pairs={{0,128},{64,192},{128,0},{192,64},{1,129},{65,193},{129,1},{193,65... | collective-permute-start | bytes 589832 | tf_op jit(solution)/shard_map/ppermute | solution.py:454
  66.4 8.7 %collective-permute-start.14 = (f32[192,256]{1,0:T(8,128)S(1)}, f32[192,256]{1,0:T(8,128)S(1)}, u32[]{:S(2)}, u32[]{:S(2)}) collective-permute-start(f32[192,256]{1,0:T(8,128)S(1)} %add.47), channel_id=1, source_target_pairs={{0,192},{64,0},{128,64},{192,128},{1,193},{65,1},{129,65},{193,129... | collective-permute-start | bytes 589832 | tf_op jit(solution)/shard_map/ppermute | solution.py:454
  75.2 7.6 %collective-permute-start.15 = (f32[96,256]{1,0:T(8,128)S(1)}, f32[96,256]{1,0:T(8,128)S(1)}, u32[]{:S(2)}, u32[]{:S(2)}) collective-permute-start(f32[96,256]{1,0:T(8,128)S(1)} %slice.16), channel_id=1, source_target_pairs={{0,32},{32,0},{1,33},{33,1},{2,34},{34,2},{3,35},{35,3},{4,36},{36... | collective-permute-start | bytes 294920 | tf_op jit(solution)/shard_map/ppermute | solution.py:438
  84.1 9.8 %collective-permute-start.16 = (f32[96,256]{1,0:T(8,128)S(1)}, f32[96,256]{1,0:T(8,128)S(1)}, u32[]{:S(2)}, u32[]{:S(2)}) collective-permute-start(f32[96,256]{1,0:T(8,128)S(1)} %get-tuple-element.43.product), channel_id=1, source_target_pairs={{0,32},{32,0},{1,33},{33,1},{2,34},{34,2},{3,35},{35,3},{4,36},{36... | collective-permute-start | bytes 294920 | tf_op jit(solution)/shard_map/ppermute | solution.py:438
  84.7 31.7 %all-to-all-start.4 = ((f32[16,48,256]{2,1,0:T(8,128)}), f32[16,48,256]{2,1,0:T(8,128)S(1)}, u32[]{:S(2)}, u32[]{:S(2)}) async-start(f32[16,48,256]{2,1,0:T(8,128)} %get-tuple-element.45), calls=%async_computation.4 | async-start | bytes 1572864 | tf_op jit(solution)/shard_map/all_to_all | solution.py:434
  94.3 8.9 %collective-permute-start.17 = (f32[200,256]{1,0:T(8,128)S(1)}, f32[200,256]{1,0:T(8,128)S(1)}, u32[]{:S(2)}, u32[]{:S(2)}) collective-permute-start(f32[200,256]{1,0:T(8,128)S(1)} %load.1.refs_4_.pair), channel_id=1, source_target_pairs={{0,192},{64,0},{128,64},{192,128},{1,193},{65,1},{129,65},{193,129... | collective-permute-start | bytes 614408 | tf_op jit(solution)/shard_map/ppermute | solution.py:446
  97.9 9.7 %collective-permute-start.18 = (f32[200,256]{1,0:T(8,128)S(1)}, f32[200,256]{1,0:T(8,128)S(1)}, u32[]{:S(2)}, u32[]{:S(2)}) collective-permute-start(f32[200,256]{1,0:T(8,128)S(1)} %load.1.refs_4_.pair), channel_id=1, source_target_pairs={{0,128},{64,192},{128,0},{192,64},{1,129},{65,193},{129,1},{193,65... | collective-permute-start | bytes 614408 | tf_op jit(solution)/shard_map/ppermute | solution.py:446
  98.0 11.4 %collective-permute-start.19 = (f32[200,256]{1,0:T(8,128)S(1)}, f32[200,256]{1,0:T(8,128)S(1)}, u32[]{:S(2)}, u32[]{:S(2)}) collective-permute-start(f32[200,256]{1,0:T(8,128)S(1)} %load.1.refs_4_.pair), channel_id=1, source_target_pairs={{0,64},{64,128},{128,192},{192,0},{1,65},{65,129},{129,193},{193,1... | collective-permute-start | bytes 614408 | tf_op jit(solution)/shard_map/ppermute | solution.py:446
  98.9 12.2 %collective-permute-start.20 = (f32[200,256]{1,0:T(8,128)S(1)}, f32[200,256]{1,0:T(8,128)S(1)}, u32[]{:S(2)}, u32[]{:S(2)}) collective-permute-start(f32[200,256]{1,0:T(8,128)S(1)} %load.1.refs_4_.pair), channel_id=1, source_target_pairs={{0,16},{16,0},{1,17},{17,1},{2,18},{18,2},{3,19},{19,3},{4,20},{20... | collective-permute-start | bytes 614408 | tf_op jit(solution)/shard_map/ppermute | solution.py:442
  103.2 8.0 %collective-permute-start.21 = (f32[200,256]{1,0:T(8,128)S(1)}, f32[200,256]{1,0:T(8,128)S(1)}, u32[]{:S(2)}, u32[]{:S(2)}) collective-permute-start(f32[200,256]{1,0:T(8,128)S(1)} %collective-permute-done.17.refs_5_), channel_id=1, source_target_pairs={{0,16},{16,0},{1,17},{17,1},{2,18},{18,2},{3,19},{19,3},{4,20},{20... | collective-permute-start | bytes 614408 | tf_op jit(solution)/shard_map/ppermute | solution.py:442
  116.5 35.0 %all-to-all-start.3 = ((f32[16,56,256]{2,1,0:T(8,128)}), f32[16,56,256]{2,1,0:T(8,128)S(1)}, u32[]{:S(2)}, u32[]{:S(2)}) async-start(f32[16,56,256]{2,1,0:T(8,128)} %rows_product.3), calls=%async_computation.3 | async-start | bytes 1835008 | tf_op jit(solution)/shard_map/all_to_all | solution.py:434
  130.9 4.1 %collective-permute-start.29 = (f32[192,256]{1,0:T(8,128)S(1)}, f32[192,256]{1,0:T(8,128)S(1)}, u32[]{:S(2)}, u32[]{:S(2)}) collective-permute-start(f32[192,256]{1,0:T(8,128)S(1)} %get-tuple-element.53), channel_id=1, source_target_pairs={{0,16},{16,0},{1,17},{17,1},{2,18},{18,2},{3,19},{19,3},{4,20},{20... | collective-permute-start | bytes 589832 | tf_op jit(solution)/shard_map/ppermute | solution.py:442
  131.3 4.1 %collective-permute-start.24 = (f32[192,256]{1,0:T(8,128)S(1)}, f32[192,256]{1,0:T(8,128)S(1)}, u32[]{:S(2)}, u32[]{:S(2)}) collective-permute-start(f32[192,256]{1,0:T(8,128)S(1)} %get-tuple-element.47), channel_id=1, source_target_pairs={{0,16},{16,0},{1,17},{17,1},{2,18},{18,2},{3,19},{19,3},{4,20},{20... | collective-permute-start | bytes 589832 | tf_op jit(solution)/shard_map/ppermute | solution.py:442
  131.9 7.4 %collective-permute-start.26 = (f32[192,256]{1,0:T(8,128)S(1)}, f32[192,256]{1,0:T(8,128)S(1)}, u32[]{:S(2)}, u32[]{:S(2)}) collective-permute-start(f32[192,256]{1,0:T(8,128)S(1)} %add.50), channel_id=1, source_target_pairs={{0,64},{64,128},{128,192},{192,0},{1,65},{65,129},{129,193},{193,1... | collective-permute-start | bytes 589832 | tf_op jit(solution)/shard_map/ppermute | solution.py:454
  132.3 11.5 %collective-permute-start.28 = (f32[192,256]{1,0:T(8,128)S(1)}, f32[192,256]{1,0:T(8,128)S(1)}, u32[]{:S(2)}, u32[]{:S(2)}) collective-permute-start(f32[192,256]{1,0:T(8,128)S(1)} %add.52), channel_id=1, source_target_pairs={{0,128},{64,192},{128,0},{192,64},{1,129},{65,193},{129,1},{193,65... | collective-permute-start | bytes 589832 | tf_op jit(solution)/shard_map/ppermute | solution.py:454
  135.1 8.9 %collective-permute-start.30 = (f32[192,256]{1,0:T(8,128)S(1)}, f32[192,256]{1,0:T(8,128)S(1)}, u32[]{:S(2)}, u32[]{:S(2)}) collective-permute-start(f32[192,256]{1,0:T(8,128)S(1)} %add.54), channel_id=1, source_target_pairs={{0,192},{64,0},{128,64},{192,128},{1,193},{65,1},{129,65},{193,129... | collective-permute-start | bytes 589832 | tf_op jit(solution)/shard_map/ppermute | solution.py:454
  155.4 13.1 %all-to-all-start.5 = ((f32[16,8,128]{2,1,0:T(8,128)}), f32[16,8,128]{2,1,0:T(8,128)S(1)}, u32[]{:S(2)}, u32[]{:S(2)}) async-start(f32[16,8,128]{2,1,0:T(8,128)} %get-tuple-element.56), calls=%async_computation.5 | async-start | bytes 131072 | tf_op jit(solution)/shard_map/all_to_all | solution.py:434
  160.4 13.8 %collective-permute-start.31 = (f32[96,256]{1,0:T(8,128)S(1)}, f32[96,256]{1,0:T(8,128)S(1)}, u32[]{:S(2)}, u32[]{:S(2)}) collective-permute-start(f32[96,256]{1,0:T(8,128)S(1)} %slice.17), channel_id=1, source_target_pairs={{0,32},{32,0},{1,33},{33,1},{2,34},{34,2},{3,35},{35,3},{4,36},{36... | collective-permute-start | bytes 294920 | tf_op jit(solution)/shard_map/ppermute | solution.py:438
  169.1 11.6 %all-to-all-start.6 = ((f32[16,8,128]{2,1,0:T(8,128)}), f32[16,8,128]{2,1,0:T(8,128)S(1)}, u32[]{:S(2)}, u32[]{:S(2)}) async-start(f32[16,8,128]{2,1,0:T(8,128)} %broadcast_in_dim.11), calls=%async_computation.6 | async-start | bytes 131072 | tf_op jit(solution)/shard_map/all_to_all | solution.py:434
  (13 other events, 60.7 us)

commit v3 on v2

--- a/solution.py
+++ b/solution.py
@@ -17,6 +17,9 @@
 CAP = 3
 SEG = SEGB * NV
 RID = 8
+MAXT = 48
+COUNT = 2 * MAXT
+PLACE = COUNT + 1
 UNROLL = 4
 F32 = jnp.float32
 BF16 = jnp.bfloat16
@@ -45,7 +48,7 @@
     return [(i, (i + step) % n) for i in range(n)]
 
 
-def prep_kernel(place, rows, cols, counts, table, slots, mark, used):
+def prep_kernel(facts, slots, ids, table, mark, used):
     n_segs = used.shape[0]
 
     def clear(b, _):
@@ -61,42 +64,79 @@
         return 0
 
     lax.fori_loop(0, n_segs, clear_table, 0)
-    my_y, my_half, my_core = place[0], place[1], place[2]
+    count, my_y, my_half, my_core = facts[COUNT], facts[PLACE], facts[PLACE + 1], facts[PLACE + 2]
 
     def slot(k, _):
-        b = rows[0, 0, k]
+        b = facts[k]
         s = b // SEGB
         old = mark[b]
         rank = jnp.where(old < 0, used[s], old)
         mark[b] = rank
         used[s] = jnp.where(old < 0, rank + 1, used[s])
         table[s * CAP + rank] = b - s * SEGB
-        slots[0, k] = b
-        slots[1, k] = s * CAP + rank
-        g = cols[0, 0, k]
+        slots[0, k] = s * CAP + rank
+        g = facts[MAXT + k]
         t = g // SEGB
         step = (t // 4 + 4 - my_y) % 4
         half = (t // 2 % 2 + my_half) % 2
         core = (t % 2 + my_core) % 2
-        slots[2, k] = ((core * 4 + step) * 2 + half) * SEGB + g - t * SEGB
+        slots[1, k] = ((core * 4 + step) * 2 + half) * SEGB + g - t * SEGB
         return 0
 
-    lax.fori_loop(0, counts[0, 0], slot, 0)
-
-
-def prep(rows, cols, counts, place):
+    lax.fori_loop(0, count, slot, 0)
+    row_id = lax.broadcasted_iota(jnp.int32, (RID, TILE), 0)
+
+    for s in range(n_segs):
+        out = jnp.zeros((RID, TILE), jnp.int32)
+        for q in range(CAP):
+            out = jnp.where(row_id == q, table[s * CAP + q], out)
+        ids[s] = out.astype(F32)
+
+
+def prep(facts):
     n_segs = 16
     return pl.pallas_call(
         prep_kernel,
         out_shape=(
-            jax.ShapeDtypeStruct((n_segs * CAP,), jnp.int32),
-            jax.ShapeDtypeStruct((3, rows.shape[-1]), jnp.int32),
+            jax.ShapeDtypeStruct((2, MAXT), jnp.int32),
+            jax.ShapeDtypeStruct((n_segs, RID, TILE), F32),
         ),
-        in_specs=[sspec()] * 4,
-        out_specs=(sspec(), sspec()),
-        scratch_shapes=[pltpu.SMEM((n_segs * SEGB,), jnp.int32), pltpu.SMEM((n_segs,), jnp.int32)],
+        in_specs=[sspec()],
+        out_specs=(sspec(), vspec()),
+        scratch_shapes=[
+            pltpu.SMEM((n_segs * CAP,), jnp.int32),
+            pltpu.SMEM((n_segs * SEGB,), jnp.int32),
+            pltpu.SMEM((n_segs,), jnp.int32),
+        ],
+        compiler_params=params(4),
+        cost_estimate=hint(2),
         name="prep",
-    )(place, rows, cols, counts)
+    )(facts)
+
+
+def pack_kernel(facts, line, *refs):
+    asked, message = refs[:4], refs[4]
+    for k in range(4):
+        to = (facts[PLACE + 3] + 4 - k) % 4
+        for z in range(4):
+            for q in range(CAP):
+                want = asked[k][facts[PLACE + 3] * 4 + z, q : q + 1, :]
+                block = jnp.zeros((NV, TILE), F32)
+                for b in range(SEGB):
+                    block = jnp.where(want == b, line[z, :, b * TILE : (b + 1) * TILE], block)
+                message[to, z, q * NV : (q + 1) * NV, :] = block
+
+
+def pack(facts, line, asked):
+    return pl.pallas_call(
+        pack_kernel,
+        out_shape=jax.ShapeDtypeStruct((4, 4, CAP * NV, TILE), F32),
+        in_specs=[sspec()] + [vspec()] * 5,
+        out_specs=vspec(),
+        compiler_params=params(8),
+        cost_estimate=hint(1),
+        name="pack",
+    )(facts, line, *asked)
 
 
 def split(x):
@@ -143,18 +183,18 @@
 
 
 def rows_kernel(first, *refs):
-    counts, slots, table, tiles = refs[:4]
+    facts, slots, ids, tiles = refs[:4]
     from_y = refs[4:12]
     to_x, held, sems, vecs, total = refs[12:]
 
     def slot(k, high, low):
-        i = slots[1, k]
-        v = vecs[slots[2, k]]
+        i = slots[0, k]
+        v = vecs[slots[1, k]]
         a = lax.dot_general(v, high, ACROSS, preferred_element_type=F32)
         b = lax.dot_general(v[:NV], low, ACROSS, preferred_element_type=F32)
         total[i] += a[:NV] + a[NV:] + b
 
-    run = tile_loop(counts[0, 0], tiles, held, sems, slot)
+    run = tile_loop(facts[COUNT], tiles, held, sems, slot)
     n_segs = to_x.shape[0]
     for p in range(8):
         for h in range(2):
@@ -174,34 +214,26 @@
         for q in range(CAP):
             to_x[s, q * NV : (q + 1) * NV, :] = total[s * CAP + q]
         if first:
-            row_id = lax.broadcasted_iota(jnp.int32, (RID, TILE), 0)
-            carried = jnp.zeros((RID, TILE), jnp.int32)
-            for q in range(CAP):
-                carried = jnp.where(row_id == q, table[s * CAP + q], carried)
-            carried = carried.astype(F32)
+            carried = ids[s]
         to_x[s, CAP * NV : CAP * NV + RID, :] = carried
 
 
-def cols_kernel(first, *refs):
-    counts, slots, tiles, from_x = refs[:4]
+def cols_kernel(*refs):
+    facts, slots, tiles, from_x = refs[:4]
     to_y = refs[4:12]
     held, sems, vecs, total = refs[12:]
 
     def slot(k, high, low):
-        j = slots[2, k]
-        v = vecs[slots[0 if first else 1, k]]
+        j = slots[1, k]
+        v = vecs[slots[0, k]]
         a = jnp.dot(v, high, preferred_element_type=F32)
         b = jnp.dot(v[:NV], low, preferred_element_type=F32)
         total[j] += a[:NV] + a[NV:] + b
 
-    run = tile_loop(counts[0, 0], tiles, held, sems, slot)
-    in_seg = SEGB if first else CAP
+    run = tile_loop(facts[COUNT], tiles, held, sems, slot)
     for s in range(from_x.shape[0]):
-        for q in range(in_seg):
-            if first:
-                put(vecs, s * in_seg + q, from_x[s, :, q * TILE : (q + 1) * TILE])
-            else:
-                put(vecs, s * in_seg + q, from_x[s, q * NV : (q + 1) * NV, :])
+        for q in range(CAP):
+            put(vecs, s * CAP + q, from_x[s, q * NV : (q + 1) * NV, :])
     total[...] = jnp.zeros(total.shape, F32)
     run()
     for p in range(8):
@@ -213,41 +245,38 @@
     return [pltpu.VMEM(tiles.shape, F32), pltpu.SemaphoreType.DMA(tiles.shape[:1])]
 
 
-def rows_product(counts, slots, table, tiles, from_y, first):
+def rows_product(facts, slots, ids, tiles, from_y, first):
     def kernel(*refs):
         rows_kernel(first, *refs)
 
     return pl.pallas_call(
         kernel,
         out_shape=jax.ShapeDtypeStruct((16, CAP * NV + RID, TILE), F32),
-        in_specs=[sspec()] * 3 + [pl.BlockSpec(memory_space=pltpu.HBM)] + [vspec()] * 8,
+        in_specs=[sspec()] * 2 + [vspec(), pl.BlockSpec(memory_space=pltpu.HBM)] + [vspec()] * 8,
         out_specs=vspec(),
         scratch_shapes=tile_scratch(tiles)
         + [pltpu.VMEM((16 * SEGB, 2 * NV, TILE), BF16), pltpu.VMEM((16 * CAP, NV, TILE), F32)],
         compiler_params=params(24),
-        cost_estimate=hint(10 if first else 5),
+        cost_estimate=hint(4 if first else 5),
         name="rows_product",
-    )(counts, slots, table, tiles, *from_y)
-
-
-def cols_product(counts, slots, tiles, from_x, first):
-    def kernel(*refs):
-        cols_kernel(first, *refs)
-
-    return pl.pallas_call(
-        kernel,
+    )(facts, slots, ids, tiles, *from_y)
+
+
+def cols_product(facts, slots, tiles, from_x):
+    return pl.pallas_call(
+        cols_kernel,
         out_shape=(jax.ShapeDtypeStruct((2 * SEG, TILE), F32),) * 8,
         in_specs=[sspec()] * 2 + [pl.BlockSpec(memory_space=pltpu.HBM), vspec()],
         out_specs=(vspec(),) * 8,
         scratch_shapes=tile_scratch(tiles)
         + [
-            pltpu.VMEM((16 * (SEGB if first else CAP), 2 * NV, TILE), BF16),
+            pltpu.VMEM((16 * CAP, 2 * NV, TILE), BF16),
             pltpu.VMEM((16 * SEGB, NV, TILE), F32),
         ],
         compiler_params=params(24),
         cost_estimate=hint(5),
         name="cols_product",
-    )(counts, slots, tiles, from_x)
+    )(facts, slots, tiles, from_x)
 
 
 def add_terms(wanted, from_x, total):
@@ -312,25 +341,25 @@
     return lax.dot_general(a, b, ACROSS, precision=HIGH, preferred_element_type=F32)
 
 
-def fan_kernel(table, slots, mine, theirs, pair, correlation):
+def fan_kernel(mine, theirs, pair, correlation):
     pair[0] = mine[...]
     pair[1] = theirs[...]
     correlation[...] = cross(mine[...], mine[...]) + cross(theirs[...], theirs[...])
 
 
-def fan(table, slots, mine, theirs):
+def fan(mine, theirs):
     return pl.pallas_call(
         fan_kernel,
         out_shape=(
             jax.ShapeDtypeStruct((2,) + mine.shape, F32),
             jax.ShapeDtypeStruct((NV, NV), F32),
         ),
-        in_specs=[sspec()] * 2 + [vspec()] * 2,
+        in_specs=[vspec()] * 2,
         out_specs=(vspec(),) * 2,
         compiler_params=params(8),
-        cost_estimate=hint(20),
+        cost_estimate=hint(5),
         name="fan",
-    )(table, slots, mine, theirs)
+    )(mine, theirs)
 
 
 def load_kernel(product, other, mine, theirs, correlation, ride):
@@ -368,6 +397,24 @@
     return m[:, NV:]
 
 
+def thirds(x):
+    high = x.astype(BF16)
+    rest = x - high.astype(F32)
+    middle = rest.astype(BF16)
+    return high, middle, (rest - middle.astype(F32)).astype(BF16)
+
+
+def stack_left(x):
+    a, b, c = thirds(x)
+    return jnp.concatenate([a, a, b, a, b, c], axis=1)
+
+
+def times(left, x):
+    a, b, c = thirds(x)
+    right = jnp.concatenate([a, b, a, c, b, a], axis=0)
+    return jnp.dot(left, right, preferred_element_type=F32)
+
+
 def finish_kernel(wanted, from_x, both, mine, theirs, pair, residual, image, gram, total):
     total[...] = both[0:SEG, :]
     add_terms(wanted, from_x, total)
@@ -378,18 +425,18 @@
         jnp.concatenate([carried[:, (at + h) * NV : (at + h + 1) * NV] for h in range(2)], axis=0) for at in (0, 2)
     )
     coeffs = solve(correlation, projection)
-    back = coeffs.T
+    back = stack_left(coeffs.T)
     local = jnp.zeros((NV, NV), F32)
     for b in range(SEGB):
         at = slice(b * NV, (b + 1) * NV)
         other = slice(SEG + b * NV, SEG + (b + 1) * NV)
         cols = slice(b * TILE, (b + 1) * TILE)
         p = pair[at, :]
-        r = p - jnp.dot(back, mine[:, cols], precision=HIGH, preferred_element_type=F32)
-        m = total[at, :] - jnp.dot(back, p, precision=HIGH, preferred_element_type=F32)
+        r = p - times(back, mine[:, cols])
+        m = total[at, :] - times(back, p)
         residual[:, cols] = r
         image[:, cols] = m
-        r_other = pair[other, :] - jnp.dot(back, theirs[:, cols], precision=HIGH, preferred_element_type=F32)
+        r_other = pair[other, :] - times(back, theirs[:, cols])
         local += cross(r, m) + cross(r_other, both[other, :])
     for d in range(gram.shape[0]):
         gram[d] = jnp.zeros(gram.shape[1:], F32)
@@ -430,6 +477,10 @@
     )(part, far)
 
 
+def in_hbm(x):
+    return pltpu.with_memory_space_constraint(x, pltpu.HBM)
+
+
 def swap(x, axis):
     return lax.all_to_all(x, axis, 0, 0, tiled=True)
 
@@ -456,18 +507,20 @@
 
 
 def per_device(vectors, tiles, tile_rows, tile_cols, counts):
-    cell_tiles = pltpu.with_memory_space_constraint(tiles[0, 0], pltpu.HBM)
+    cell_tiles = in_hbm(tiles[0, 0])
     order_total = vectors.shape[1] * lax.axis_size(ROW) * lax.axis_size(COL)
-    place = jnp.stack([lax.axis_index(name).astype(jnp.int32) for name in ROW])
-    table, slots = prep(tile_rows, tile_cols, counts, place)
+    place = jnp.stack([lax.axis_index(name).astype(jnp.int32) for name in ROW + ("x",)])
+    facts = jnp.concatenate([tile_rows.reshape(MAXT), tile_cols.reshape(MAXT), counts.reshape(1), place])
+    slots, ids = prep(facts)
+    asked = [ids] + [lax.ppermute(ids, "x", turned(4, k)) for k in (1, 2, 3)]
 
     theirs = other_half(vectors)
-    both, correlation = fan(table, slots, vectors, theirs)
+    both, correlation = fan(in_hbm(vectors), theirs)
     from_y = spread(both)
     line = swap(jnp.broadcast_to(vectors, (4,) + vectors.shape), "zl")
-    from_x = swap(jnp.broadcast_to(line, (4,) + line.shape), "x").reshape((16,) + vectors.shape)
-    to_x = rows_product(counts, slots, table, cell_tiles, from_y, True)
-    to_y = cols_product(counts, slots, cell_tiles, from_x, True)
+    from_x = swap(pack(facts, line, asked), "x").reshape(16, CAP * NV, TILE)
+    to_x = rows_product(facts, slots, ids, cell_tiles, from_y, True)
+    to_y = cols_product(facts, slots, cell_tiles, from_x)
     from_x = swap(to_x, COL)
     both = collect(to_y)
     far = other_half(both[SEG:])
@@ -477,8 +530,8 @@
     from_x = swap(message, COL)
     pair = load(product, other_half(product), vectors, theirs, correlation)
     from_y = spread(pair)
-    to_x = rows_product(counts, slots, table, cell_tiles, from_y, False)
-    to_y = cols_product(counts, slots, cell_tiles, from_x, False)
+    to_x = rows_product(facts, slots, ids, cell_tiles, from_y, False)
+    to_y = cols_product(facts, slots, cell_tiles, from_x)
     from_x = swap(to_x, COL)
     both = collect(to_y)
     residual, part, local = finish(wanted, from_x, both, vectors, theirs, pair)

time: 181 us -> 176 us (0.972); the launches traced: 181 us -> 174 us
  Pallas kernels: 24.6 us -> 41.8 us
  starting transfers between devices: 95.6 us -> 83.7 us
  waiting for transfers between devices: 52.1 us -> 43.1 us
  local copies, waits for them, and re-layouts: 6.02 us -> 3.19 us
    all_to_all x7, starting transfers between devices: 43.7 us -> 34 us  [swap(): return lax.all_to_all(x, axis, 0, 0, tiled=True)]
    pallas_call x3 -> x4, Pallas kernels: 8.39 us -> 17.8 us  [the longest x2 12 us: cols_product(): pl.pallas_call(cols_kernel, out_shape=(jax.ShapeDtypeStruct((2 * SEG, TIL...]
    all_to_all x7, waiting for transfers between devices: 25.5 us -> 16.8 us  [swap(): return lax.all_to_all(x, axis, 0, 0, tiled=True)]
    pallas_call x2, Pallas kernels: 8.39 us -> 16.2 us  [rows_product(): pl.pallas_call(kernel, out_shape=jax.ShapeDtypeStruct((16, CAP * NV + RID...]
    ppermute x0 -> x3, starting transfers between devices: none -> 2.86 us  [per_device(): asked = [ids] + [lax.ppermute(ids, 'x', turned(4, k)) for k in (1, 2, 3)]]
    ppermute x16, starting transfers between devices: 21.3 us -> 18.7 us  [other_core(): return lax.ppermute(x, 'core', turned(2, 1))]
    unnamed x12 -> x2, local copies, waits for them, and re-layouts: 2.24 us -> 0.01 us
  transfers between devices with their start and end apart: 39 -> 42, of which waited for: 20 -> 19; matrix products, arithmetic and copies ran while one was open for 3% -> 2% of each run, Pallas kernels for 11% -> 21%
where the time goes in v3:
time: 176 us; the launch traced here: 174 us
  starting transfers between devices  83.7 us (48%)
  waiting for transfers between devices  43.1 us (24%)
  Pallas kernels  41.8 us (24%)
  local copies, waits for them, and re-layouts  3.19 us (2%)
    all_to_all x7, starting transfers between devices, swap(): return lax.all_to_all(x, axis, 0, 0, tiled=True)  34 us
    ppermute x16, starting transfers between devices, other_core(): return lax.ppermute(x, 'core', turned(2, 1))  18.7 us
    all_to_all x7, waiting for transfers between devices, swap(): return lax.all_to_all(x, axis, 0, 0, tiled=True)  16.8 us
    ppermute x6, waiting for transfers between devices, collect(): both = both + lax.ppermute(met[step], 'y', turned(4, step))  16.4 us
    pallas_call x2, Pallas kernels, rows_product(): pl.pallas_call(kernel, out_shape=jax.ShapeDtypeStruct((16, CAP * NV + RID...  16.2 us
    ppermute x4, starting transfers between devices, other_half(): return lax.ppermute(x, 'zh', turned(2, 1))  13.3 us
    pallas_call x2, Pallas kernels, cols_product(): pl.pallas_call(cols_kernel, out_shape=(jax.ShapeDtypeStruct((2 * SEG, TIL...  12 us
    ppermute x6, starting transfers between devices, collect(): both = both + lax.ppermute(met[step], 'y', turned(4, step))  7.99 us
  transfers between devices with their start and end apart: 42, of which 19 were waited for; matrix products, arithmetic and copies ran while one was open for 2% of the time, Pallas kernels for 21%

profile of v3, /device:TPU:1, one launch (start us, length us, event | category | flops | bytes accessed | tf_op | source)
XLA Modules:
  0.0 174.4 jit_solution(9076708490790639965)
XLA Ops:
  0.6 7.8 %collective-permute-start = (f32[16,1536]{1,0:T(8,128)}, f32[16,1536]{1,0:T(8,128)S(1)}, u32[]{:S(2)}, u32[]{:S(2)}) collective-permute-start(f32[16,1536]{1,0:T(8,128)} %mine.5), channel_id=1, source_target_pairs={{0,32},{32,0},{1,33},{33,1},{2,34},{34,2},{3,35},{35,3},{4,36},{36... | collective-permute-start | bytes 294920 | tf_op jit(solution)/shard_map/ppermute | solution.py:489
  10.2 3.5 %all-to-all-start.1 = ((f32[4,16,1536]{2,1,0:T(8,128)}), f32[4,16,1536]{2,1,0:T(8,128)S(1)}, u32[]{:S(2)}, u32[]{:S(2)}) async-start(f32[4,16,1536]{2,1,0:T(8,128)} %broadcast_in_dim.6), calls=%async_computation.1 | async-start | bytes 786432 | tf_op jit(solution)/shard_map/all_to_all | solution.py:485
  15.0 4.0 %prep.1 = (s32[2,48]{1,0:T(2,128)S(1)}, f32[16,8,256]{2,1,0:T(8,128)S(1)}) custom-call(s32[101]{0:T(128)S(1)} %concatenate.6.facts.refs_0_), custom_call_target="tpu_custom_call" | custom-call | flops 2000000000 | tf_op jit(solution)/shard_map/prep/pallas_call | solution.py:98
  23.2 2.7 %collective-permute-start.1 = (f32[2,16,1536]{2,1,0:T(8,128)S(1)}, f32[2,16,1536]{2,1,0:T(8,128)S(1)}, u32[]{:S(2)}, u32[]{:S(2)}) collective-permute-start(f32[2,16,1536]{2,1,0:T(8,128)S(1)} %get-tuple-element.32.refs_4_), channel_id=1, source_target_pairs={{0,192},{64,0},{128,64},{192,128},{1,193},{65,1},{129,65},{193,129... | collective-permute-start | bytes 589832 | tf_op jit(solution)/shard_map/ppermute | solution.py:497
  29.3 3.5 %all-to-all-start.2 = ((f32[4,4,48,256]{3,2,1,0:T(8,128)}), f32[4,4,48,256]{3,2,1,0:T(8,128)S(1)}, u32[]{:S(2)}, u32[]{:S(2)}) async-start(f32[4,4,48,256]{3,2,1,0:T(8,128)} %pack.1), calls=%async_computation.2 | async-start | bytes 1572864 | tf_op jit(solution)/shard_map/all_to_all | solution.py:485
  32.8 2.7 %collective-permute-start.4 = (f32[2,16,1536]{2,1,0:T(8,128)S(1)}, f32[2,16,1536]{2,1,0:T(8,128)S(1)}, u32[]{:S(2)}, u32[]{:S(2)}) collective-permute-start(f32[2,16,1536]{2,1,0:T(8,128)S(1)} %get-tuple-element.32.refs_4_), channel_id=1, source_target_pairs={{0,16},{16,0},{1,17},{17,1},{2,18},{18,2},{3,19},{19,3},{4,20},{20... | collective-permute-start | bytes 589832 | tf_op jit(solution)/shard_map/ppermute | solution.py:493
  40.0 8.1 %rows_product.2 = f32[16,56,256]{2,1,0:T(8,128)} custom-call(s32[101]{0:T(128)S(1)} %concatenate.6.facts.refs_0_, s32[2,48]{1,0:T(2,128)S(1)} %get-tuple-element.30.refs_1_, f32[16,8,256]{2,1,0:T(8,128)S(1)} %get-tuple-element.31.refs_2_.refs_0_, f32[48,256,256]{2,1,0:T(8,128)} %bitcast.11, f32[2,16,1536]{2,1,0:T(8,128)S(1)} %get-tuple-element.32.refs_4_, ...), custom_call_target="tpu_custom_call" | custom-call | flops 4000000000 | tf_op jit(solution)/shard_map/rows_product/pallas_call | solution.py:252
  48.2 3.6 %all-to-all-start = ((f32[16,56,256]{2,1,0:T(8,128)}), f32[16,56,256]{2,1,0:T(8,128)S(1)}, u32[]{:S(2)}, u32[]{:S(2)}) async-start(f32[16,56,256]{2,1,0:T(8,128)} %rows_product.2), calls=%async_computation | async-start | bytes 1835008 | tf_op jit(solution)/shard_map/all_to_all | solution.py:485
  51.8 6.0 %cols_product.2 = (f32[192,256]{1,0:T(8,128)S(1)}, f32[192,256]{1,0:T(8,128)S(1)}, f32[192,256]{1,0:T(8,128)S(1)}, f32[192,256]{1,0:T(8,128)S(1)}, f32[192,256]{...) custom-call(s32[101]{0:T(128)S(1)} %concatenate.6.facts.refs_0_, ...), custom_call_target="tpu_custom_call" | custom-call | flops 5000000000 | tf_op jit(solution)/shard_map/cols_product/pallas_call | solution.py:266
  59.7 2.4 %collective-permute-start.15 = (f32[192,256]{1,0:T(8,128)S(1)}, f32[192,256]{1,0:T(8,128)S(1)}, u32[]{:S(2)}, u32[]{:S(2)}) collective-permute-start(f32[192,256]{1,0:T(8,128)S(1)} %add.45), channel_id=1, source_target_pairs={{0,128},{64,192},{128,0},{192,64},{1,129},{65,193},{129,1},{193,65... | collective-permute-start | bytes 589832 | tf_op jit(solution)/shard_map/ppermute | solution.py:505
  62.1 2.1 %collective-permute-start.17 = (f32[192,256]{1,0:T(8,128)S(1)}, f32[192,256]{1,0:T(8,128)S(1)}, u32[]{:S(2)}, u32[]{:S(2)}) collective-permute-start(f32[192,256]{1,0:T(8,128)S(1)} %add.47), channel_id=1, source_target_pairs={{0,192},{64,0},{128,64},{192,128},{1,193},{65,1},{129,65},{193,129... | collective-permute-start | bytes 589832 | tf_op jit(solution)/shard_map/ppermute | solution.py:505
  64.2 3.3 %collective-permute-done.13 = f32[192,256]{1,0:T(8,128)S(1)} collective-permute-done((f32[192,256]{1,0:T(8,128)S(1)}, f32[192,256]{1,0:T(8,128)S(1)}, u32[]{:S(2)}, u32[]{:S(2)}) %collective-permute-start.13) | collective-permute-done | bytes 196640 | tf_op jit(solution)/shard_map/ppermute | solution.py:505
  67.5 3.6 %collective-permute-done.15 = f32[192,256]{1,0:T(8,128)S(1)} collective-permute-done((f32[192,256]{1,0:T(8,128)S(1)}, f32[192,256]{1,0:T(8,128)S(1)}, u32[]{:S(2)}, u32[]{:S(2)}) %collective-permute-start.15) | collective-permute-done | bytes 196640 | tf_op jit(solution)/shard_map/ppermute | solution.py:505
  72.0 4.1 %all-to-all-done.from_x = f32[16,56,256]{2,1,0:T(8,128)S(1)} async-done(((f32[16,56,256]{2,1,0:T(8,128)}), f32[16,56,256]{2,1,0:T(8,128)S(1)}, u32[]{:S(2)}, u32[]{:S(2)}) %all-to-all-start) | async-done | bytes 917536 | tf_op jit(solution)/shard_map/all_to_all | solution.py:485
  76.7 3.8 %collective-permute-done.18.far_theirs = f32[96,256]{1,0:T(8,128)S(1)} collective-permute-done((f32[96,256]{1,0:T(8,128)S(1)}, f32[96,256]{1,0:T(8,128)S(1)}, u32[]{:S(2)}, u32[]{:S(2)}) %collective-permute-start.18) | collective-permute-done | bytes 98336 | tf_op jit(solution)/shard_map/ppermute | solution.py:489
  81.8 10.0 %all-to-all-start.4 = ((f32[16,48,256]{2,1,0:T(8,128)}), f32[16,48,256]{2,1,0:T(8,128)S(1)}, u32[]{:S(2)}, u32[]{:S(2)}) async-start(f32[16,48,256]{2,1,0:T(8,128)} %get-tuple-element.45), calls=%async_computation.4 | async-start | bytes 1572864 | tf_op jit(solution)/shard_map/all_to_all | solution.py:485
  92.3 2.5 %collective-permute-start.20 = (f32[200,256]{1,0:T(8,128)S(1)}, f32[200,256]{1,0:T(8,128)S(1)}, u32[]{:S(2)}, u32[]{:S(2)}) collective-permute-start(f32[200,256]{1,0:T(8,128)S(1)} %load.1.refs_4_.pair), channel_id=1, source_target_pairs={{0,192},{64,0},{128,64},{192,128},{1,193},{65,1},{129,65},{193,129... | collective-permute-start | bytes 614408 | tf_op jit(solution)/shard_map/ppermute | solution.py:497
  95.3 3.7 %collective-permute-start.23 = (f32[200,256]{1,0:T(8,128)S(1)}, f32[200,256]{1,0:T(8,128)S(1)}, u32[]{:S(2)}, u32[]{:S(2)}) collective-permute-start(f32[200,256]{1,0:T(8,128)S(1)} %load.1.refs_4_.pair), channel_id=1, source_target_pairs={{0,16},{16,0},{1,17},{17,1},{2,18},{18,2},{3,19},{19,3},{4,20},{20... | collective-permute-start | bytes 614408 | tf_op jit(solution)/shard_map/ppermute | solution.py:493
  100.4 4.1 %collective-permute-start.24 = (f32[200,256]{1,0:T(8,128)S(1)}, f32[200,256]{1,0:T(8,128)S(1)}, u32[]{:S(2)}, u32[]{:S(2)}) collective-permute-start(f32[200,256]{1,0:T(8,128)S(1)} %collective-permute-done.20.refs_5_), channel_id=1, source_target_pairs={{0,16},{16,0},{1,17},{17,1},{2,18},{18,2},{3,19},{19,3},{4,20},{20... | collective-permute-start | bytes 614408 | tf_op jit(solution)/shard_map/ppermute | solution.py:493
  106.1 2.0 %collective-permute-start.26 = (f32[200,256]{1,0:T(8,128)S(1)}, f32[200,256]{1,0:T(8,128)S(1)}, u32[]{:S(2)}, u32[]{:S(2)}) collective-permute-start(f32[200,256]{1,0:T(8,128)S(1)} %collective-permute-done.22.refs_7_), channel_id=1, source_target_pairs={{0,16},{16,0},{1,17},{17,1},{2,18},{18,2},{3,19},{19,3},{4,20},{20... | collective-permute-start | bytes 614408 | tf_op jit(solution)/shard_map/ppermute | solution.py:493
  109.2 8.1 %rows_product.3 = f32[16,56,256]{2,1,0:T(8,128)} custom-call(s32[101]{0:T(128)S(1)} %concatenate.6.facts.refs_0_, s32[2,48]{1,0:T(2,128)S(1)} %get-tuple-element.30.refs_1_, f32[16,8,256]{2,1,0:T(8,128)S(1)} %get-tuple-element.31.refs_2_.refs_0_, f32[48,256,256]{2,1,0:T(8,128)} %bitcast.13, f32[200,256]{1,0:T(8,128)S(1)} %load.1.refs_4_.pair, ...), custom_call_target="tpu_custom_call" | custom-call | flops 5000000000 | tf_op jit(solution)/shard_map/rows_product/pallas_call | solution.py:252
  117.3 3.7 %all-to-all-start.3 = ((f32[16,56,256]{2,1,0:T(8,128)}), f32[16,56,256]{2,1,0:T(8,128)S(1)}, u32[]{:S(2)}, u32[]{:S(2)}) async-start(f32[16,56,256]{2,1,0:T(8,128)} %rows_product.3), calls=%async_computation.3 | async-start | bytes 1835008 | tf_op jit(solution)/shard_map/all_to_all | solution.py:485
  121.0 6.0 %cols_product.3 = (f32[192,256]{1,0:T(8,128)S(1)}, f32[192,256]{1,0:T(8,128)S(1)}, f32[192,256]{1,0:T(8,128)S(1)}, f32[192,256]{1,0:T(8,128)S(1)}, f32[192,256]{...) custom-call(s32[101]{0:T(128)S(1)} %concatenate.6.facts.refs_0_, ...), custom_call_target="tpu_custom_call" | custom-call | flops 5000000000 | tf_op jit(solution)/shard_map/cols_product/pallas_call | solution.py:266
  130.1 1.9 %collective-permute-start.33 = (f32[192,256]{1,0:T(8,128)S(1)}, f32[192,256]{1,0:T(8,128)S(1)}, u32[]{:S(2)}, u32[]{:S(2)}) collective-permute-start(f32[192,256]{1,0:T(8,128)S(1)} %add.54), channel_id=1, source_target_pairs={{0,192},{64,0},{128,64},{192,128},{1,193},{65,1},{129,65},{193,129... | collective-permute-start | bytes 589832 | tf_op jit(solution)/shard_map/ppermute | solution.py:505
  132.0 8.4 %collective-permute-done.29 = f32[192,256]{1,0:T(8,128)S(1)} collective-permute-done((f32[192,256]{1,0:T(8,128)S(1)}, f32[192,256]{1,0:T(8,128)S(1)}, u32[]{:S(2)}, u32[]{:S(2)}) %collective-permute-start.29) | collective-permute-done | bytes 196640 | tf_op jit(solution)/shard_map/ppermute | solution.py:505
  140.9 4.2 %all-to-all-done.3.from_x = f32[16,56,256]{2,1,0:T(8,128)S(1)} async-done(((f32[16,56,256]{2,1,0:T(8,128)}), f32[16,56,256]{2,1,0:T(8,128)S(1)}, u32[]{:S(2)}, u32[]{:S(2)}) %all-to-all-start.3) | async-done | bytes 917536 | tf_op jit(solution)/shard_map/all_to_all | solution.py:485
  145.1 3.6 %finish.1 = (f32[16,1536]{1,0:T(8,128)}, f32[16,1536]{1,0:T(8,128)S(1)}, f32[16,8,128]{2,1,0:T(8,128)}) custom-call(f32[16,8,256]{2,1,0:T(8,128)S(1)} %get-tuple-element.33.wanted, f32[16,56,256]{2,1,0:T(8,128)S(1)} %all-to-all-done.3.from_x, f32[192,256]{1,0:T(8,128)S(1)} %add_add_fusion.both, f32[16,1536]{1,0:T(8,128)S(1)} %copy-done, ...), custom_call_target="tpu_custom_call" | custom-call | tf_op jit(solution)/shard_map/finish/pallas_call | solution.py:448
  148.7 6.3 %all-to-all-start.5 = ((f32[16,8,128]{2,1,0:T(8,128)}), f32[16,8,128]{2,1,0:T(8,128)S(1)}, u32[]{:S(2)}, u32[]{:S(2)}) async-start(f32[16,8,128]{2,1,0:T(8,128)} %get-tuple-element.56), calls=%async_computation.5 | async-start | bytes 131072 | tf_op jit(solution)/shard_map/all_to_all | solution.py:485
  155.0 5.4 %collective-permute-start.34 = (f32[96,256]{1,0:T(8,128)S(1)}, f32[96,256]{1,0:T(8,128)S(1)}, u32[]{:S(2)}, u32[]{:S(2)}) collective-permute-start(f32[96,256]{1,0:T(8,128)S(1)} %slice.17), channel_id=1, source_target_pairs={{0,32},{32,0},{1,33},{33,1},{2,34},{34,2},{3,35},{35,3},{4,36},{36... | collective-permute-start | bytes 294920 | tf_op jit(solution)/shard_map/ppermute | solution.py:489
  160.4 2.6 %all-to-all-done.5 = f32[16,8,128]{2,1,0:T(8,128)S(1)} async-done(((f32[16,8,128]{2,1,0:T(8,128)}), f32[16,8,128]{2,1,0:T(8,128)S(1)}, u32[]{:S(2)}, u32[]{:S(2)}) %all-to-all-start.5) | async-done | bytes 65568 | tf_op jit(solution)/shard_map/all_to_all | solution.py:485
  163.7 3.5 %all-to-all-start.6 = ((f32[16,8,128]{2,1,0:T(8,128)}), f32[16,8,128]{2,1,0:T(8,128)S(1)}, u32[]{:S(2)}, u32[]{:S(2)}) async-start(f32[16,8,128]{2,1,0:T(8,128)} %broadcast_in_dim.7), calls=%async_computation.6 | async-start | bytes 131072 | tf_op jit(solution)/shard_map/all_to_all | solution.py:485
  167.8 5.8 %all-to-all-done.6 = f32[16,8,128]{2,1,0:T(8,128)S(1)} async-done(((f32[16,8,128]{2,1,0:T(8,128)}), f32[16,8,128]{2,1,0:T(8,128)S(1)}, u32[]{:S(2)}, u32[]{:S(2)}) %all-to-all-start.6) | async-done | bytes 65568 | tf_op jit(solution)/shard_map/all_to_all | solution.py:485
  (83 shorter events, 29.7 us)
Async XLA Ops:
  0.6 21.3 %collective-permute-start = (f32[16,1536]{1,0:T(8,128)}, f32[16,1536]{1,0:T(8,128)S(1)}, u32[]{:S(2)}, u32[]{:S(2)}) collective-permute-start(f32[16,1536]{1,0:T(8,128)} %mine.5), channel_id=1, source_target_pairs={{0,32},{32,0},{1,33},{33,1},{2,34},{34,2},{3,35},{35,3},{4,36},{36... | collective-permute-start | bytes 294920 | tf_op jit(solution)/shard_map/ppermute | solution.py:489
  10.2 17.3 %all-to-all-start.1 = ((f32[4,16,1536]{2,1,0:T(8,128)}), f32[4,16,1536]{2,1,0:T(8,128)S(1)}, u32[]{:S(2)}, u32[]{:S(2)}) async-start(f32[4,16,1536]{2,1,0:T(8,128)} %broadcast_in_dim.6), calls=%async_computation.1 | async-start | bytes 786432 | tf_op jit(solution)/shard_map/all_to_all | solution.py:485
  19.1 7.2 %collective-permute-start.10 = (f32[16,8,256]{2,1,0:T(8,128)S(1)}, f32[16,8,256]{2,1,0:T(8,128)S(1)}, u32[]{:S(2)}, u32[]{:S(2)}) collective-permute-start(f32[16,8,256]{2,1,0:T(8,128)S(1)} %get-tuple-element.31.refs_2_.refs_0_), channel_id=1, source_target_pairs={{0,12},{4,0},{8,4},{12,8},{1,13},{5,1},{9,5},{13,9},{2,14},{6,2},{... | collective-permute-start | bytes 393224 | tf_op jit(solution)/shard_map/ppermute | solution.py:515
  20.2 7.3 %collective-permute-start.8 = (f32[16,8,256]{2,1,0:T(8,128)S(1)}, f32[16,8,256]{2,1,0:T(8,128)S(1)}, u32[]{:S(2)}, u32[]{:S(2)}) collective-permute-start(f32[16,8,256]{2,1,0:T(8,128)S(1)} %get-tuple-element.31.refs_2_.refs_0_), channel_id=1, source_target_pairs={{0,4},{4,8},{8,12},{12,0},{1,5},{5,9},{9,13},{13,1},{2,6},{6,10},{... | collective-permute-start | bytes 393224 | tf_op jit(solution)/shard_map/ppermute | solution.py:515
  20.6 6.9 %collective-permute-start.9 = (f32[16,8,256]{2,1,0:T(8,128)S(1)}, f32[16,8,256]{2,1,0:T(8,128)S(1)}, u32[]{:S(2)}, u32[]{:S(2)}) collective-permute-start(f32[16,8,256]{2,1,0:T(8,128)S(1)} %get-tuple-element.31.refs_2_.refs_0_), channel_id=1, source_target_pairs={{0,8},{4,12},{8,0},{12,4},{1,9},{5,13},{9,1},{13,5},{2,10},{6,14},... | collective-permute-start | bytes 393224 | tf_op jit(solution)/shard_map/ppermute | solution.py:515
  23.2 12.3 %collective-permute-start.1 = (f32[2,16,1536]{2,1,0:T(8,128)S(1)}, f32[2,16,1536]{2,1,0:T(8,128)S(1)}, u32[]{:S(2)}, u32[]{:S(2)}) collective-permute-start(f32[2,16,1536]{2,1,0:T(8,128)S(1)} %get-tuple-element.32.refs_4_), channel_id=1, source_target_pairs={{0,192},{64,0},{128,64},{192,128},{1,193},{65,1},{129,65},{193,129... | collective-permute-start | bytes 589832 | tf_op jit(solution)/shard_map/ppermute | solution.py:497
  25.9 9.7 %collective-permute-start.2 = (f32[2,16,1536]{2,1,0:T(8,128)S(1)}, f32[2,16,1536]{2,1,0:T(8,128)S(1)}, u32[]{:S(2)}, u32[]{:S(2)}) collective-permute-start(f32[2,16,1536]{2,1,0:T(8,128)S(1)} %get-tuple-element.32.refs_4_), channel_id=1, source_target_pairs={{0,128},{64,192},{128,0},{192,64},{1,129},{65,193},{129,1},{193,65... | collective-permute-start | bytes 589832 | tf_op jit(solution)/shard_map/ppermute | solution.py:497
  26.2 11.7 %collective-permute-start.3 = (f32[2,16,1536]{2,1,0:T(8,128)S(1)}, f32[2,16,1536]{2,1,0:T(8,128)S(1)}, u32[]{:S(2)}, u32[]{:S(2)}) collective-permute-start(f32[2,16,1536]{2,1,0:T(8,128)S(1)} %get-tuple-element.32.refs_4_), channel_id=1, source_target_pairs={{0,64},{64,128},{128,192},{192,0},{1,65},{65,129},{129,193},{193,1... | collective-permute-start | bytes 589832 | tf_op jit(solution)/shard_map/ppermute | solution.py:497
  29.3 18.9 %all-to-all-start.2 = ((f32[4,4,48,256]{3,2,1,0:T(8,128)}), f32[4,4,48,256]{3,2,1,0:T(8,128)S(1)}, u32[]{:S(2)}, u32[]{:S(2)}) async-start(f32[4,4,48,256]{3,2,1,0:T(8,128)} %pack.1), calls=%async_computation.2 | async-start | bytes 1572864 | tf_op jit(solution)/shard_map/all_to_all | solution.py:485
  32.8 6.2 %collective-permute-start.4 = (f32[2,16,1536]{2,1,0:T(8,128)S(1)}, f32[2,16,1536]{2,1,0:T(8,128)S(1)}, u32[]{:S(2)}, u32[]{:S(2)}) collective-permute-start(f32[2,16,1536]{2,1,0:T(8,128)S(1)} %get-tuple-element.32.refs_4_), channel_id=1, source_target_pairs={{0,16},{16,0},{1,17},{17,1},{2,18},{18,2},{3,19},{19,3},{4,20},{20... | collective-permute-start | bytes 589832 | tf_op jit(solution)/shard_map/ppermute | solution.py:493
  48.2 28.0 %all-to-all-start = ((f32[16,56,256]{2,1,0:T(8,128)}), f32[16,56,256]{2,1,0:T(8,128)S(1)}, u32[]{:S(2)}, u32[]{:S(2)}) async-start(f32[16,56,256]{2,1,0:T(8,128)} %rows_product.2), calls=%async_computation | async-start | bytes 1835008 | tf_op jit(solution)/shard_map/all_to_all | solution.py:485
  58.4 3.7 %collective-permute-start.16 = (f32[192,256]{1,0:T(8,128)S(1)}, f32[192,256]{1,0:T(8,128)S(1)}, u32[]{:S(2)}, u32[]{:S(2)}) collective-permute-start(f32[192,256]{1,0:T(8,128)S(1)} %get-tuple-element.42), channel_id=1, source_target_pairs={{0,16},{16,0},{1,17},{17,1},{2,18},{18,2},{3,19},{19,3},{4,20},{20... | collective-permute-start | bytes 589832 | tf_op jit(solution)/shard_map/ppermute | solution.py:493
  58.5 5.7 %collective-permute-start.11 = (f32[192,256]{1,0:T(8,128)S(1)}, f32[192,256]{1,0:T(8,128)S(1)}, u32[]{:S(2)}, u32[]{:S(2)}) collective-permute-start(f32[192,256]{1,0:T(8,128)S(1)} %get-tuple-element.36), channel_id=1, source_target_pairs={{0,16},{16,0},{1,17},{17,1},{2,18},{18,2},{3,19},{19,3},{4,20},{20... | collective-permute-start | bytes 589832 | tf_op jit(solution)/shard_map/ppermute | solution.py:493
  59.4 8.2 %collective-permute-start.13 = (f32[192,256]{1,0:T(8,128)S(1)}, f32[192,256]{1,0:T(8,128)S(1)}, u32[]{:S(2)}, u32[]{:S(2)}) collective-permute-start(f32[192,256]{1,0:T(8,128)S(1)} %add.43), channel_id=1, source_target_pairs={{0,64},{64,128},{128,192},{192,0},{1,65},{65,129},{129,193},{193,1... | collective-permute-start | bytes 589832 | tf_op jit(solution)/shard_map/ppermute | solution.py:505
  59.7 11.4 %collective-permute-start.15 = (f32[192,256]{1,0:T(8,128)S(1)}, f32[192,256]{1,0:T(8,128)S(1)}, u32[]{:S(2)}, u32[]{:S(2)}) collective-permute-start(f32[192,256]{1,0:T(8,128)S(1)} %add.45), channel_id=1, source_target_pairs={{0,128},{64,192},{128,0},{192,64},{1,129},{65,193},{129,1},{193,65... | collective-permute-start | bytes 589832 | tf_op jit(solution)/shard_map/ppermute | solution.py:505
  62.1 9.7 %collective-permute-start.17 = (f32[192,256]{1,0:T(8,128)S(1)}, f32[192,256]{1,0:T(8,128)S(1)}, u32[]{:S(2)}, u32[]{:S(2)}) collective-permute-start(f32[192,256]{1,0:T(8,128)S(1)} %add.47), channel_id=1, source_target_pairs={{0,192},{64,0},{128,64},{192,128},{1,193},{65,1},{129,65},{193,129... | collective-permute-start | bytes 589832 | tf_op jit(solution)/shard_map/ppermute | solution.py:505
  71.9 8.6 %collective-permute-start.18 = (f32[96,256]{1,0:T(8,128)S(1)}, f32[96,256]{1,0:T(8,128)S(1)}, u32[]{:S(2)}, u32[]{:S(2)}) collective-permute-start(f32[96,256]{1,0:T(8,128)S(1)} %slice.16), channel_id=1, source_target_pairs={{0,32},{32,0},{1,33},{33,1},{2,34},{34,2},{3,35},{35,3},{4,36},{36... | collective-permute-start | bytes 294920 | tf_op jit(solution)/shard_map/ppermute | solution.py:489
  81.8 10.0 %collective-permute-start.19 = (f32[96,256]{1,0:T(8,128)S(1)}, f32[96,256]{1,0:T(8,128)S(1)}, u32[]{:S(2)}, u32[]{:S(2)}) collective-permute-start(f32[96,256]{1,0:T(8,128)S(1)} %get-tuple-element.43.product), channel_id=1, source_target_pairs={{0,32},{32,0},{1,33},{33,1},{2,34},{34,2},{3,35},{35,3},{4,36},{36... | collective-permute-start | bytes 294920 | tf_op jit(solution)/shard_map/ppermute | solution.py:489
  81.8 35.5 %all-to-all-start.4 = ((f32[16,48,256]{2,1,0:T(8,128)}), f32[16,48,256]{2,1,0:T(8,128)S(1)}, u32[]{:S(2)}, u32[]{:S(2)}) async-start(f32[16,48,256]{2,1,0:T(8,128)} %get-tuple-element.45), calls=%async_computation.4 | async-start | bytes 1572864 | tf_op jit(solution)/shard_map/all_to_all | solution.py:485
  92.3 8.1 %collective-permute-start.20 = (f32[200,256]{1,0:T(8,128)S(1)}, f32[200,256]{1,0:T(8,128)S(1)}, u32[]{:S(2)}, u32[]{:S(2)}) collective-permute-start(f32[200,256]{1,0:T(8,128)S(1)} %load.1.refs_4_.pair), channel_id=1, source_target_pairs={{0,192},{64,0},{128,64},{192,128},{1,193},{65,1},{129,65},{193,129... | collective-permute-start | bytes 614408 | tf_op jit(solution)/shard_map/ppermute | solution.py:497
  94.7 9.7 %collective-permute-start.21 = (f32[200,256]{1,0:T(8,128)S(1)}, f32[200,256]{1,0:T(8,128)S(1)}, u32[]{:S(2)}, u32[]{:S(2)}) collective-permute-start(f32[200,256]{1,0:T(8,128)S(1)} %load.1.refs_4_.pair), channel_id=1, source_target_pairs={{0,128},{64,192},{128,0},{192,64},{1,129},{65,193},{129,1},{193,65... | collective-permute-start | bytes 614408 | tf_op jit(solution)/shard_map/ppermute | solution.py:497
  95.0 11.1 %collective-permute-start.22 = (f32[200,256]{1,0:T(8,128)S(1)}, f32[200,256]{1,0:T(8,128)S(1)}, u32[]{:S(2)}, u32[]{:S(2)}) collective-permute-start(f32[200,256]{1,0:T(8,128)S(1)} %load.1.refs_4_.pair), channel_id=1, source_target_pairs={{0,64},{64,128},{128,192},{192,0},{1,65},{65,129},{129,193},{193,1... | collective-permute-start | bytes 614408 | tf_op jit(solution)/shard_map/ppermute | solution.py:497
  95.3 12.8 %collective-permute-start.23 = (f32[200,256]{1,0:T(8,128)S(1)}, f32[200,256]{1,0:T(8,128)S(1)}, u32[]{:S(2)}, u32[]{:S(2)}) collective-permute-start(f32[200,256]{1,0:T(8,128)S(1)} %load.1.refs_4_.pair), channel_id=1, source_target_pairs={{0,16},{16,0},{1,17},{17,1},{2,18},{18,2},{3,19},{19,3},{4,20},{20... | collective-permute-start | bytes 614408 | tf_op jit(solution)/shard_map/ppermute | solution.py:493
  100.4 7.7 %collective-permute-start.24 = (f32[200,256]{1,0:T(8,128)S(1)}, f32[200,256]{1,0:T(8,128)S(1)}, u32[]{:S(2)}, u32[]{:S(2)}) collective-permute-start(f32[200,256]{1,0:T(8,128)S(1)} %collective-permute-done.20.refs_5_), channel_id=1, source_target_pairs={{0,16},{16,0},{1,17},{17,1},{2,18},{18,2},{3,19},{19,3},{4,20},{20... | collective-permute-start | bytes 614408 | tf_op jit(solution)/shard_map/ppermute | solution.py:493
  117.3 27.8 %all-to-all-start.3 = ((f32[16,56,256]{2,1,0:T(8,128)}), f32[16,56,256]{2,1,0:T(8,128)S(1)}, u32[]{:S(2)}, u32[]{:S(2)}) async-start(f32[16,56,256]{2,1,0:T(8,128)} %rows_product.3), calls=%async_computation.3 | async-start | bytes 1835008 | tf_op jit(solution)/shard_map/all_to_all | solution.py:485
  127.7 4.3 %collective-permute-start.27 = (f32[192,256]{1,0:T(8,128)S(1)}, f32[192,256]{1,0:T(8,128)S(1)}, u32[]{:S(2)}, u32[]{:S(2)}) collective-permute-start(f32[192,256]{1,0:T(8,128)S(1)} %get-tuple-element.47), channel_id=1, source_target_pairs={{0,16},{16,0},{1,17},{17,1},{2,18},{18,2},{3,19},{19,3},{4,20},{20... | collective-permute-start | bytes 589832 | tf_op jit(solution)/shard_map/ppermute | solution.py:493
  128.5 11.9 %collective-permute-start.29 = (f32[192,256]{1,0:T(8,128)S(1)}, f32[192,256]{1,0:T(8,128)S(1)}, u32[]{:S(2)}, u32[]{:S(2)}) collective-permute-start(f32[192,256]{1,0:T(8,128)S(1)} %add.50), channel_id=1, source_target_pairs={{0,64},{64,128},{128,192},{192,0},{1,65},{65,129},{129,193},{193,1... | collective-permute-start | bytes 589832 | tf_op jit(solution)/shard_map/ppermute | solution.py:505
  128.8 11.6 %collective-permute-start.31 = (f32[192,256]{1,0:T(8,128)S(1)}, f32[192,256]{1,0:T(8,128)S(1)}, u32[]{:S(2)}, u32[]{:S(2)}) collective-permute-start(f32[192,256]{1,0:T(8,128)S(1)} %add.52), channel_id=1, source_target_pairs={{0,128},{64,192},{128,0},{192,64},{1,129},{65,193},{129,1},{193,65... | collective-permute-start | bytes 589832 | tf_op jit(solution)/shard_map/ppermute | solution.py:505
  130.1 10.7 %collective-permute-start.33 = (f32[192,256]{1,0:T(8,128)S(1)}, f32[192,256]{1,0:T(8,128)S(1)}, u32[]{:S(2)}, u32[]{:S(2)}) collective-permute-start(f32[192,256]{1,0:T(8,128)S(1)} %add.54), channel_id=1, source_target_pairs={{0,192},{64,0},{128,64},{192,128},{1,193},{65,1},{129,65},{193,129... | collective-permute-start | bytes 589832 | tf_op jit(solution)/shard_map/ppermute | solution.py:505
  148.7 14.3 %all-to-all-start.5 = ((f32[16,8,128]{2,1,0:T(8,128)}), f32[16,8,128]{2,1,0:T(8,128)S(1)}, u32[]{:S(2)}, u32[]{:S(2)}) async-start(f32[16,8,128]{2,1,0:T(8,128)} %get-tuple-element.56), calls=%async_computation.5 | async-start | bytes 131072 | tf_op jit(solution)/shard_map/all_to_all | solution.py:485
  155.0 12.2 %collective-permute-start.34 = (f32[96,256]{1,0:T(8,128)S(1)}, f32[96,256]{1,0:T(8,128)S(1)}, u32[]{:S(2)}, u32[]{:S(2)}) collective-permute-start(f32[96,256]{1,0:T(8,128)S(1)} %slice.17), channel_id=1, source_target_pairs={{0,32},{32,0},{1,33},{33,1},{2,34},{34,2},{3,35},{35,3},{4,36},{36... | collective-permute-start | bytes 294920 | tf_op jit(solution)/shard_map/ppermute | solution.py:489
  163.7 10.0 %all-to-all-start.6 = ((f32[16,8,128]{2,1,0:T(8,128)}), f32[16,8,128]{2,1,0:T(8,128)S(1)}, u32[]{:S(2)}, u32[]{:S(2)}) async-start(f32[16,8,128]{2,1,0:T(8,128)} %broadcast_in_dim.7), calls=%async_computation.6 | async-start | bytes 131072 | tf_op jit(solution)/shard_map/all_to_all | solution.py:485
  (11 other events, 64.6 us)

commit v4 on v3

--- a/solution.py
+++ b/solution.py
@@ -20,7 +20,7 @@
 MAXT = 48
 COUNT = 2 * MAXT
 PLACE = COUNT + 1
-UNROLL = 4
+UNROLL = 8
 F32 = jnp.float32
 BF16 = jnp.bfloat16
 HIGH = lax.Precision.HIGHEST
@@ -438,10 +438,9 @@
         image[:, cols] = m
         r_other = pair[other, :] - times(back, theirs[:, cols])
         local += cross(r, m) + cross(r_other, both[other, :])
-    for d in range(gram.shape[0]):
-        gram[d] = jnp.zeros(gram.shape[1:], F32)
-        for h in range(2):
-            gram[d, :, h * NV : (h + 1) * NV] = local[h * RID : (h + 1) * RID, :]
+    for h in range(2):
+        for r in range(RID):
+            gram[h : h + 1, r * NV : (r + 1) * NV] = local[h * RID + r : h * RID + r + 1, :]
 
 
 def finish(wanted, from_x, both, mine, theirs, pair):
@@ -450,7 +449,7 @@
         out_shape=(
             jax.ShapeDtypeStruct(mine.shape, F32),
             jax.ShapeDtypeStruct(mine.shape, F32),
-            jax.ShapeDtypeStruct((16, RID, 128), F32),
+            jax.ShapeDtypeStruct((2, 128), F32),
         ),
         in_specs=[vspec()] * 6,
         out_specs=(vspec(),) * 3,
@@ -473,6 +472,7 @@
         in_specs=[vspec()] * 2,
         out_specs=vspec(),
         compiler_params=params(4),
+        cost_estimate=hint(5),
         name="last",
     )(part, far)
 
@@ -537,9 +537,9 @@
     residual, part, local = finish(wanted, from_x, both, vectors, theirs, pair)
     image = last(part, other_half(both[SEG:]))
 
-    some = jnp.sum(swap(local, ("zh", "zl", "core")), axis=0)
-    total = jnp.sum(swap(jnp.broadcast_to(some, local.shape), ("x", "y")), axis=0)
-    gram = jnp.concatenate([total[:, :NV], total[:, NV : 2 * NV]], axis=0) / order_total
+    chip = local + other_core(local)
+    copies = jnp.broadcast_to(chip, (128,) + chip.shape)
+    gram = jnp.sum(swap(copies, ("y", "zh", "x", "zl")), axis=0).reshape(NV, NV) / order_total
     return (residual, image, gram)
 
 

time: 176 us -> 174 us (0.989)
  starting transfers between devices: 83.7 us -> 98.8 us
  Pallas kernels: 41.8 us -> 29 us
  waiting for transfers between devices: 43.1 us -> 39.8 us
    pallas_call x2, Pallas kernels: 16.2 us -> 9.83 us  [rows_product(): pl.pallas_call(kernel, out_shape=jax.ShapeDtypeStruct((16, CAP * NV + RID...]
    all_to_all x7 -> x6, starting transfers between devices: 34 us -> 40.4 us  [swap(): return lax.all_to_all(x, axis, 0, 0, tiled=True)]
    ppermute x6, starting transfers between devices: 7.99 us -> 12.8 us  [collect(): both = both + lax.ppermute(met[step], 'y', turned(4, step))]
    ppermute x16 -> x17, starting transfers between devices: 18.7 us -> 23.5 us  [other_core(): return lax.ppermute(x, 'core', turned(2, 1))]
    pallas_call x2, Pallas kernels: 12 us -> 7.35 us  [cols_product(): pl.pallas_call(cols_kernel, out_shape=(jax.ShapeDtypeStruct((2 * SEG, TIL...]
    ppermute x4, starting transfers between devices: 13.3 us -> 10.1 us  [other_half(): return lax.ppermute(x, 'zh', turned(2, 1))]
    ppermute x6, waiting for transfers between devices: 2.38 us -> 0.02 us  [spread(): lax.ppermute(mine, 'y', turned(4, -step))]
    ppermute x6, waiting for transfers between devices: 16.4 us -> 14.1 us  [collect(): both = both + lax.ppermute(met[step], 'y', turned(4, step))]
  transfers between devices with their start and end apart: 42 -> 42, of which waited for: 19 -> 14; matrix products, arithmetic and copies ran while one was open for 2% -> 2% of each run, Pallas kernels for 21% -> 16%
where the time goes in v4:
time: 174 us; the launch traced here: 173 us
  starting transfers between devices  98.8 us (57%)
  waiting for transfers between devices  39.8 us (23%)
  Pallas kernels  29 us (17%)
  local copies, waits for them, and re-layouts  3.85 us (2%)
    all_to_all x6, starting transfers between devices, swap(): return lax.all_to_all(x, axis, 0, 0, tiled=True)  40.4 us
    ppermute x17, starting transfers between devices, other_core(): return lax.ppermute(x, 'core', turned(2, 1))  23.5 us
    all_to_all x6, waiting for transfers between devices, swap(): return lax.all_to_all(x, axis, 0, 0, tiled=True)  16.9 us
    ppermute x6, waiting for transfers between devices, collect(): both = both + lax.ppermute(met[step], 'y', turned(4, step))  14.1 us
    ppermute x6, starting transfers between devices, collect(): both = both + lax.ppermute(met[step], 'y', turned(4, step))  12.8 us
    ppermute x4, starting transfers between devices, other_half(): return lax.ppermute(x, 'zh', turned(2, 1))  10.1 us
    pallas_call x2, Pallas kernels, rows_product(): pl.pallas_call(kernel, out_shape=jax.ShapeDtypeStruct((16, CAP * NV + RID...  9.83 us
    ppermute x6, starting transfers between devices, spread(): lax.ppermute(mine, 'y', turned(4, -step))  7.74 us
  transfers between devices with their start and end apart: 42, of which 14 were waited for; matrix products, arithmetic and copies ran while one was open for 2% of the time, Pallas kernels for 16%

profile of v4, /device:TPU:1, one launch (start us, length us, event | category | flops | bytes accessed | tf_op | source)
XLA Modules:
  0.0 173.5 jit_solution(488569461181060937)
XLA Ops:
  0.6 7.8 %collective-permute-start = (f32[16,1536]{1,0:T(8,128)}, f32[16,1536]{1,0:T(8,128)S(1)}, u32[]{:S(2)}, u32[]{:S(2)}) collective-permute-start(f32[16,1536]{1,0:T(8,128)} %mine.5), channel_id=1, source_target_pairs={{0,32},{32,0},{1,33},{33,1},{2,34},{34,2},{3,35},{35,3},{4,36},{36... | collective-permute-start | bytes 294920 | tf_op jit(solution)/shard_map/ppermute | solution.py:489
  10.2 3.5 %all-to-all-start.1 = ((f32[4,16,1536]{2,1,0:T(8,128)}), f32[4,16,1536]{2,1,0:T(8,128)S(1)}, u32[]{:S(2)}, u32[]{:S(2)}) async-start(f32[4,16,1536]{2,1,0:T(8,128)} %broadcast_in_dim.6), calls=%async_computation.1 | async-start | bytes 786432 | tf_op jit(solution)/shard_map/all_to_all | solution.py:485
  15.0 2.6 %prep.1 = (s32[2,48]{1,0:T(2,128)S(1)}, f32[16,8,256]{2,1,0:T(8,128)S(1)}) custom-call(s32[101]{0:T(128)S(1)} %concatenate.3.facts.refs_0_), custom_call_target="tpu_custom_call" | custom-call | flops 2000000000 | tf_op jit(solution)/shard_map/prep/pallas_call | solution.py:98
  17.6 2.3 %collective-permute-start.10 = (f32[16,8,256]{2,1,0:T(8,128)S(1)}, f32[16,8,256]{2,1,0:T(8,128)S(1)}, u32[]{:S(2)}, u32[]{:S(2)}) collective-permute-start(f32[16,8,256]{2,1,0:T(8,128)S(1)} %get-tuple-element.31.refs_2_.refs_0_), channel_id=1, source_target_pairs={{0,12},{4,0},{8,4},{12,8},{1,13},{5,1},{9,5},{13,9},{2,14},{6,2},{... | collective-permute-start | bytes 393224 | tf_op jit(solution)/shard_map/ppermute | solution.py:515
  23.1 2.5 %collective-permute-start.1 = (f32[2,16,1536]{2,1,0:T(8,128)S(1)}, f32[2,16,1536]{2,1,0:T(8,128)S(1)}, u32[]{:S(2)}, u32[]{:S(2)}) collective-permute-start(f32[2,16,1536]{2,1,0:T(8,128)S(1)} %get-tuple-element.32.refs_4_), channel_id=1, source_target_pairs={{0,192},{64,0},{128,64},{192,128},{1,193},{65,1},{129,65},{193,129... | collective-permute-start | bytes 589832 | tf_op jit(solution)/shard_map/ppermute | solution.py:497
  29.8 3.5 %all-to-all-start.2 = ((f32[4,4,48,256]{3,2,1,0:T(8,128)}), f32[4,4,48,256]{3,2,1,0:T(8,128)S(1)}, u32[]{:S(2)}, u32[]{:S(2)}) async-start(f32[4,4,48,256]{3,2,1,0:T(8,128)} %pack.1), calls=%async_computation.2 | async-start | bytes 1572864 | tf_op jit(solution)/shard_map/all_to_all | solution.py:485
  33.3 2.5 %collective-permute-start.4 = (f32[2,16,1536]{2,1,0:T(8,128)S(1)}, f32[2,16,1536]{2,1,0:T(8,128)S(1)}, u32[]{:S(2)}, u32[]{:S(2)}) collective-permute-start(f32[2,16,1536]{2,1,0:T(8,128)S(1)} %get-tuple-element.32.refs_4_), channel_id=1, source_target_pairs={{0,16},{16,0},{1,17},{17,1},{2,18},{18,2},{3,19},{19,3},{4,20},{20... | collective-permute-start | bytes 589832 | tf_op jit(solution)/shard_map/ppermute | solution.py:493
  36.8 2.0 %collective-permute-start.7 = (f32[2,16,1536]{2,1,0:T(8,128)S(1)}, f32[2,16,1536]{2,1,0:T(8,128)S(1)}, u32[]{:S(2)}, u32[]{:S(2)}) collective-permute-start(f32[2,16,1536]{2,1,0:T(8,128)S(1)} %collective-permute-done.3.refs_7_), channel_id=1, source_target_pairs={{0,16},{16,0},{1,17},{17,1},{2,18},{18,2},{3,19},{19,3},{4,20},{20... | collective-permute-start | bytes 589832 | tf_op jit(solution)/shard_map/ppermute | solution.py:493
  39.8 4.9 %rows_product.2 = f32[16,56,256]{2,1,0:T(8,128)} custom-call(s32[101]{0:T(128)S(1)} %concatenate.3.facts.refs_0_, s32[2,48]{1,0:T(2,128)S(1)} %get-tuple-element.30.refs_1_, f32[16,8,256]{2,1,0:T(8,128)S(1)} %get-tuple-element.31.refs_2_.refs_0_, f32[48,256,256]{2,1,0:T(8,128)} %bitcast.11, f32[2,16,1536]{2,1,0:T(8,128)S(1)} %get-tuple-element.32.refs_4_, ...), custom_call_target="tpu_custom_call" | custom-call | flops 4000000000 | tf_op jit(solution)/shard_map/rows_product/pallas_call | solution.py:252
  44.8 6.5 %all-to-all-start = ((f32[16,56,256]{2,1,0:T(8,128)}), f32[16,56,256]{2,1,0:T(8,128)S(1)}, u32[]{:S(2)}, u32[]{:S(2)}) async-start(f32[16,56,256]{2,1,0:T(8,128)} %rows_product.2), calls=%async_computation | async-start | bytes 1835008 | tf_op jit(solution)/shard_map/all_to_all | solution.py:485
  51.3 3.7 %cols_product.2 = (f32[192,256]{1,0:T(8,128)S(1)}, f32[192,256]{1,0:T(8,128)S(1)}, f32[192,256]{1,0:T(8,128)S(1)}, f32[192,256]{1,0:T(8,128)S(1)}, f32[192,256]{...) custom-call(s32[101]{0:T(128)S(1)} %concatenate.3.facts.refs_0_, ...), custom_call_target="tpu_custom_call" | custom-call | flops 5000000000 | tf_op jit(solution)/shard_map/cols_product/pallas_call | solution.py:266
  57.7 5.0 %collective-permute-start.15 = (f32[192,256]{1,0:T(8,128)S(1)}, f32[192,256]{1,0:T(8,128)S(1)}, u32[]{:S(2)}, u32[]{:S(2)}) collective-permute-start(f32[192,256]{1,0:T(8,128)S(1)} %add.48), channel_id=1, source_target_pairs={{0,128},{64,192},{128,0},{192,64},{1,129},{65,193},{129,1},{193,65... | collective-permute-start | bytes 589832 | tf_op jit(solution)/shard_map/ppermute | solution.py:505
  62.7 2.0 %collective-permute-start.17 = (f32[192,256]{1,0:T(8,128)S(1)}, f32[192,256]{1,0:T(8,128)S(1)}, u32[]{:S(2)}, u32[]{:S(2)}) collective-permute-start(f32[192,256]{1,0:T(8,128)S(1)} %add.50), channel_id=1, source_target_pairs={{0,192},{64,0},{128,64},{192,128},{1,193},{65,1},{129,65},{193,129... | collective-permute-start | bytes 589832 | tf_op jit(solution)/shard_map/ppermute | solution.py:505
  64.8 7.0 %collective-permute-done.15 = f32[192,256]{1,0:T(8,128)S(1)} collective-permute-done((f32[192,256]{1,0:T(8,128)S(1)}, f32[192,256]{1,0:T(8,128)S(1)}, u32[]{:S(2)}, u32[]{:S(2)}) %collective-permute-start.15) | collective-permute-done | bytes 196640 | tf_op jit(solution)/shard_map/ppermute | solution.py:505
  72.0 3.5 %all-to-all-done.from_x = f32[16,56,256]{2,1,0:T(8,128)S(1)} async-done(((f32[16,56,256]{2,1,0:T(8,128)}), f32[16,56,256]{2,1,0:T(8,128)S(1)}, u32[]{:S(2)}, u32[]{:S(2)}) %all-to-all-start) | async-done | bytes 917536 | tf_op jit(solution)/shard_map/all_to_all | solution.py:485
  76.0 4.4 %collective-permute-done.18.far_theirs = f32[96,256]{1,0:T(8,128)S(1)} collective-permute-done((f32[96,256]{1,0:T(8,128)S(1)}, f32[96,256]{1,0:T(8,128)S(1)}, u32[]{:S(2)}, u32[]{:S(2)}) %collective-permute-start.18) | collective-permute-done | bytes 98336 | tf_op jit(solution)/shard_map/ppermute | solution.py:489
  81.7 9.5 %all-to-all-start.4 = ((f32[16,48,256]{2,1,0:T(8,128)}), f32[16,48,256]{2,1,0:T(8,128)S(1)}, u32[]{:S(2)}, u32[]{:S(2)}) async-start(f32[16,48,256]{2,1,0:T(8,128)} %get-tuple-element.45), calls=%async_computation.4 | async-start | bytes 1572864 | tf_op jit(solution)/shard_map/all_to_all | solution.py:485
  91.7 2.0 %collective-permute-start.20 = (f32[200,256]{1,0:T(8,128)S(1)}, f32[200,256]{1,0:T(8,128)S(1)}, u32[]{:S(2)}, u32[]{:S(2)}) collective-permute-start(f32[200,256]{1,0:T(8,128)S(1)} %load.1.refs_4_.pair), channel_id=1, source_target_pairs={{0,192},{64,0},{128,64},{192,128},{1,193},{65,1},{129,65},{193,129... | collective-permute-start | bytes 614408 | tf_op jit(solution)/shard_map/ppermute | solution.py:497
  94.5 4.5 %collective-permute-start.23 = (f32[200,256]{1,0:T(8,128)S(1)}, f32[200,256]{1,0:T(8,128)S(1)}, u32[]{:S(2)}, u32[]{:S(2)}) collective-permute-start(f32[200,256]{1,0:T(8,128)S(1)} %load.1.refs_4_.pair), channel_id=1, source_target_pairs={{0,16},{16,0},{1,17},{17,1},{2,18},{18,2},{3,19},{19,3},{4,20},{20... | collective-permute-start | bytes 614408 | tf_op jit(solution)/shard_map/ppermute | solution.py:493
  99.0 4.3 %collective-permute-start.24 = (f32[200,256]{1,0:T(8,128)S(1)}, f32[200,256]{1,0:T(8,128)S(1)}, u32[]{:S(2)}, u32[]{:S(2)}) collective-permute-start(f32[200,256]{1,0:T(8,128)S(1)} %collective-permute-done.20.refs_5_), channel_id=1, source_target_pairs={{0,16},{16,0},{1,17},{17,1},{2,18},{18,2},{3,19},{19,3},{4,20},{20... | collective-permute-start | bytes 614408 | tf_op jit(solution)/shard_map/ppermute | solution.py:493
  104.9 2.1 %collective-permute-start.26 = (f32[200,256]{1,0:T(8,128)S(1)}, f32[200,256]{1,0:T(8,128)S(1)}, u32[]{:S(2)}, u32[]{:S(2)}) collective-permute-start(f32[200,256]{1,0:T(8,128)S(1)} %collective-permute-done.22.refs_7_), channel_id=1, source_target_pairs={{0,16},{16,0},{1,17},{17,1},{2,18},{18,2},{3,19},{19,3},{4,20},{20... | collective-permute-start | bytes 614408 | tf_op jit(solution)/shard_map/ppermute | solution.py:493
  108.1 4.9 %rows_product.3 = f32[16,56,256]{2,1,0:T(8,128)} custom-call(s32[101]{0:T(128)S(1)} %concatenate.3.facts.refs_0_, s32[2,48]{1,0:T(2,128)S(1)} %get-tuple-element.30.refs_1_, f32[16,8,256]{2,1,0:T(8,128)S(1)} %get-tuple-element.31.refs_2_.refs_0_, f32[48,256,256]{2,1,0:T(8,128)} %bitcast.13, f32[200,256]{1,0:T(8,128)S(1)} %load.1.refs_4_.pair, ...), custom_call_target="tpu_custom_call" | custom-call | flops 5000000000 | tf_op jit(solution)/shard_map/rows_product/pallas_call | solution.py:252
  113.1 6.9 %all-to-all-start.3 = ((f32[16,56,256]{2,1,0:T(8,128)}), f32[16,56,256]{2,1,0:T(8,128)S(1)}, u32[]{:S(2)}, u32[]{:S(2)}) async-start(f32[16,56,256]{2,1,0:T(8,128)} %rows_product.3), calls=%async_computation.3 | async-start | bytes 1835008 | tf_op jit(solution)/shard_map/all_to_all | solution.py:485
  120.0 3.7 %cols_product.3 = (f32[192,256]{1,0:T(8,128)S(1)}, f32[192,256]{1,0:T(8,128)S(1)}, f32[192,256]{1,0:T(8,128)S(1)}, f32[192,256]{1,0:T(8,128)S(1)}, f32[192,256]{...) custom-call(s32[101]{0:T(128)S(1)} %concatenate.3.facts.refs_0_, ...), custom_call_target="tpu_custom_call" | custom-call | flops 5000000000 | tf_op jit(solution)/shard_map/cols_product/pallas_call | solution.py:266
  126.5 3.8 %collective-permute-start.31 = (f32[192,256]{1,0:T(8,128)S(1)}, f32[192,256]{1,0:T(8,128)S(1)}, u32[]{:S(2)}, u32[]{:S(2)}) collective-permute-start(f32[192,256]{1,0:T(8,128)S(1)} %add.55), channel_id=1, source_target_pairs={{0,128},{64,192},{128,0},{192,64},{1,129},{65,193},{129,1},{193,65... | collective-permute-start | bytes 589832 | tf_op jit(solution)/shard_map/ppermute | solution.py:505
  130.3 2.0 %collective-permute-start.33 = (f32[192,256]{1,0:T(8,128)S(1)}, f32[192,256]{1,0:T(8,128)S(1)}, u32[]{:S(2)}, u32[]{:S(2)}) collective-permute-start(f32[192,256]{1,0:T(8,128)S(1)} %add.57), channel_id=1, source_target_pairs={{0,192},{64,0},{128,64},{192,128},{1,193},{65,1},{129,65},{193,129... | collective-permute-start | bytes 589832 | tf_op jit(solution)/shard_map/ppermute | solution.py:505
  133.5 5.8 %collective-permute-done.31 = f32[192,256]{1,0:T(8,128)S(1)} collective-permute-done((f32[192,256]{1,0:T(8,128)S(1)}, f32[192,256]{1,0:T(8,128)S(1)}, u32[]{:S(2)}, u32[]{:S(2)}) %collective-permute-start.31) | collective-permute-done | bytes 196640 | tf_op jit(solution)/shard_map/ppermute | solution.py:505
  139.4 2.2 %collective-permute-start.34 = (f32[96,256]{1,0:T(8,128)S(1)}, f32[96,256]{1,0:T(8,128)S(1)}, u32[]{:S(2)}, u32[]{:S(2)}) collective-permute-start(f32[96,256]{1,0:T(8,128)S(1)} %slice.9), channel_id=1, source_target_pairs={{0,32},{32,0},{1,33},{33,1},{2,34},{34,2},{3,35},{35,3},{4,36},{36... | collective-permute-start | bytes 294920 | tf_op jit(solution)/shard_map/ppermute | solution.py:489
  141.6 2.6 %all-to-all-done.3.from_x = f32[16,56,256]{2,1,0:T(8,128)S(1)} async-done(((f32[16,56,256]{2,1,0:T(8,128)}), f32[16,56,256]{2,1,0:T(8,128)S(1)}, u32[]{:S(2)}, u32[]{:S(2)}) %all-to-all-start.3) | async-done | bytes 917536 | tf_op jit(solution)/shard_map/all_to_all | solution.py:485
  144.2 3.3 %finish.1 = (f32[16,1536]{1,0:T(8,128)}, f32[16,1536]{1,0:T(8,128)S(1)}, f32[2,128]{1,0:T(2,128)S(1)}) custom-call(f32[16,8,256]{2,1,0:T(8,128)S(1)} %get-tuple-element.33.wanted, f32[16,56,256]{2,1,0:T(8,128)S(1)} %all-to-all-done.3.from_x, f32[192,256]{1,0:T(8,128)S(1)} %add_add_fusion.both, f32[16,1536]{1,0:T(8,128)S(1)} %copy-done, ...), custom_call_target="tpu_custom_call" | custom-call | tf_op jit(solution)/shard_map/finish/pallas_call | solution.py:447
  150.7 10.5 %all-to-all-start.5 = ((f32[128,2,128]{2,1,0:T(2,128)}), f32[128,2,128]{2,1,0:T(2,128)S(1)}, u32[]{:S(2)}, u32[]{:S(2)}) async-start(f32[128,2,128]{2,1,0:T(2,128)} %broadcast_in_dim.7), calls=%async_computation.5 | async-start | bytes 262144 | tf_op jit(solution)/shard_map/all_to_all | solution.py:485
  161.9 10.8 %all-to-all-done.5 = f32[128,2,128]{2,1,0:T(2,128)S(1)} async-done(((f32[128,2,128]{2,1,0:T(2,128)}), f32[128,2,128]{2,1,0:T(2,128)S(1)}, u32[]{:S(2)}, u32[]{:S(2)}) %all-to-all-start.5) | async-done | bytes 131104 | tf_op jit(solution)/shard_map/all_to_all | solution.py:485
  (83 shorter events, 29.5 us)
Async XLA Ops:
  0.6 21.2 %collective-permute-start = (f32[16,1536]{1,0:T(8,128)}, f32[16,1536]{1,0:T(8,128)S(1)}, u32[]{:S(2)}, u32[]{:S(2)}) collective-permute-start(f32[16,1536]{1,0:T(8,128)} %mine.5), channel_id=1, source_target_pairs={{0,32},{32,0},{1,33},{33,1},{2,34},{34,2},{3,35},{35,3},{4,36},{36... | collective-permute-start | bytes 294920 | tf_op jit(solution)/shard_map/ppermute | solution.py:489
  10.2 17.9 %all-to-all-start.1 = ((f32[4,16,1536]{2,1,0:T(8,128)}), f32[4,16,1536]{2,1,0:T(8,128)S(1)}, u32[]{:S(2)}, u32[]{:S(2)}) async-start(f32[4,16,1536]{2,1,0:T(8,128)} %broadcast_in_dim.6), calls=%async_computation.1 | async-start | bytes 786432 | tf_op jit(solution)/shard_map/all_to_all | solution.py:485
  17.6 9.6 %collective-permute-start.10 = (f32[16,8,256]{2,1,0:T(8,128)S(1)}, f32[16,8,256]{2,1,0:T(8,128)S(1)}, u32[]{:S(2)}, u32[]{:S(2)}) collective-permute-start(f32[16,8,256]{2,1,0:T(8,128)S(1)} %get-tuple-element.31.refs_2_.refs_0_), channel_id=1, source_target_pairs={{0,12},{4,0},{8,4},{12,8},{1,13},{5,1},{9,5},{13,9},{2,14},{6,2},{... | collective-permute-start | bytes 393224 | tf_op jit(solution)/shard_map/ppermute | solution.py:515
  19.9 8.1 %collective-permute-start.8 = (f32[16,8,256]{2,1,0:T(8,128)S(1)}, f32[16,8,256]{2,1,0:T(8,128)S(1)}, u32[]{:S(2)}, u32[]{:S(2)}) collective-permute-start(f32[16,8,256]{2,1,0:T(8,128)S(1)} %get-tuple-element.31.refs_2_.refs_0_), channel_id=1, source_target_pairs={{0,4},{4,8},{8,12},{12,0},{1,5},{5,9},{9,13},{13,1},{2,6},{6,10},{... | collective-permute-start | bytes 393224 | tf_op jit(solution)/shard_map/ppermute | solution.py:515
  19.9 8.1 %collective-permute-start.9 = (f32[16,8,256]{2,1,0:T(8,128)S(1)}, f32[16,8,256]{2,1,0:T(8,128)S(1)}, u32[]{:S(2)}, u32[]{:S(2)}) collective-permute-start(f32[16,8,256]{2,1,0:T(8,128)S(1)} %get-tuple-element.31.refs_2_.refs_0_), channel_id=1, source_target_pairs={{0,8},{4,12},{8,0},{12,4},{1,9},{5,13},{9,1},{13,5},{2,10},{6,14},... | collective-permute-start | bytes 393224 | tf_op jit(solution)/shard_map/ppermute | solution.py:515
  23.1 12.7 %collective-permute-start.1 = (f32[2,16,1536]{2,1,0:T(8,128)S(1)}, f32[2,16,1536]{2,1,0:T(8,128)S(1)}, u32[]{:S(2)}, u32[]{:S(2)}) collective-permute-start(f32[2,16,1536]{2,1,0:T(8,128)S(1)} %get-tuple-element.32.refs_4_), channel_id=1, source_target_pairs={{0,192},{64,0},{128,64},{192,128},{1,193},{65,1},{129,65},{193,129... | collective-permute-start | bytes 589832 | tf_op jit(solution)/shard_map/ppermute | solution.py:497
  25.6 10.3 %collective-permute-start.2 = (f32[2,16,1536]{2,1,0:T(8,128)S(1)}, f32[2,16,1536]{2,1,0:T(8,128)S(1)}, u32[]{:S(2)}, u32[]{:S(2)}) collective-permute-start(f32[2,16,1536]{2,1,0:T(8,128)S(1)} %get-tuple-element.32.refs_4_), channel_id=1, source_target_pairs={{0,128},{64,192},{128,0},{192,64},{1,129},{65,193},{129,1},{193,65... | collective-permute-start | bytes 589832 | tf_op jit(solution)/shard_map/ppermute | solution.py:497
  27.2 9.5 %collective-permute-start.3 = (f32[2,16,1536]{2,1,0:T(8,128)S(1)}, f32[2,16,1536]{2,1,0:T(8,128)S(1)}, u32[]{:S(2)}, u32[]{:S(2)}) collective-permute-start(f32[2,16,1536]{2,1,0:T(8,128)S(1)} %get-tuple-element.32.refs_4_), channel_id=1, source_target_pairs={{0,64},{64,128},{128,192},{192,0},{1,65},{65,129},{129,193},{193,1... | collective-permute-start | bytes 589832 | tf_op jit(solution)/shard_map/ppermute | solution.py:497
  29.8 14.9 %all-to-all-start.2 = ((f32[4,4,48,256]{3,2,1,0:T(8,128)}), f32[4,4,48,256]{3,2,1,0:T(8,128)S(1)}, u32[]{:S(2)}, u32[]{:S(2)}) async-start(f32[4,4,48,256]{3,2,1,0:T(8,128)} %pack.1), calls=%async_computation.2 | async-start | bytes 1572864 | tf_op jit(solution)/shard_map/all_to_all | solution.py:485
  33.3 5.4 %collective-permute-start.4 = (f32[2,16,1536]{2,1,0:T(8,128)S(1)}, f32[2,16,1536]{2,1,0:T(8,128)S(1)}, u32[]{:S(2)}, u32[]{:S(2)}) collective-permute-start(f32[2,16,1536]{2,1,0:T(8,128)S(1)} %get-tuple-element.32.refs_4_), channel_id=1, source_target_pairs={{0,16},{16,0},{1,17},{17,1},{2,18},{18,2},{3,19},{19,3},{4,20},{20... | collective-permute-start | bytes 589832 | tf_op jit(solution)/shard_map/ppermute | solution.py:493
  44.8 30.7 %all-to-all-start = ((f32[16,56,256]{2,1,0:T(8,128)}), f32[16,56,256]{2,1,0:T(8,128)S(1)}, u32[]{:S(2)}, u32[]{:S(2)}) async-start(f32[16,56,256]{2,1,0:T(8,128)} %rows_product.2), calls=%async_computation | async-start | bytes 1835008 | tf_op jit(solution)/shard_map/all_to_all | solution.py:485
  56.4 6.3 %collective-permute-start.16 = (f32[192,256]{1,0:T(8,128)S(1)}, f32[192,256]{1,0:T(8,128)S(1)}, u32[]{:S(2)}, u32[]{:S(2)}) collective-permute-start(f32[192,256]{1,0:T(8,128)S(1)} %get-tuple-element.42), channel_id=1, source_target_pairs={{0,16},{16,0},{1,17},{17,1},{2,18},{18,2},{3,19},{19,3},{4,20},{20... | collective-permute-start | bytes 589832 | tf_op jit(solution)/shard_map/ppermute | solution.py:493
  56.8 7.9 %collective-permute-start.11 = (f32[192,256]{1,0:T(8,128)S(1)}, f32[192,256]{1,0:T(8,128)S(1)}, u32[]{:S(2)}, u32[]{:S(2)}) collective-permute-start(f32[192,256]{1,0:T(8,128)S(1)} %get-tuple-element.36), channel_id=1, source_target_pairs={{0,16},{16,0},{1,17},{17,1},{2,18},{18,2},{3,19},{19,3},{4,20},{20... | collective-permute-start | bytes 589832 | tf_op jit(solution)/shard_map/ppermute | solution.py:493
  57.4 7.4 %collective-permute-start.13 = (f32[192,256]{1,0:T(8,128)S(1)}, f32[192,256]{1,0:T(8,128)S(1)}, u32[]{:S(2)}, u32[]{:S(2)}) collective-permute-start(f32[192,256]{1,0:T(8,128)S(1)} %add.46), channel_id=1, source_target_pairs={{0,64},{64,128},{128,192},{192,0},{1,65},{65,129},{129,193},{193,1... | collective-permute-start | bytes 589832 | tf_op jit(solution)/shard_map/ppermute | solution.py:505
  57.7 14.0 %collective-permute-start.15 = (f32[192,256]{1,0:T(8,128)S(1)}, f32[192,256]{1,0:T(8,128)S(1)}, u32[]{:S(2)}, u32[]{:S(2)}) collective-permute-start(f32[192,256]{1,0:T(8,128)S(1)} %add.48), channel_id=1, source_target_pairs={{0,128},{64,192},{128,0},{192,64},{1,129},{65,193},{129,1},{193,65... | collective-permute-start | bytes 589832 | tf_op jit(solution)/shard_map/ppermute | solution.py:505
  62.7 9.0 %collective-permute-start.17 = (f32[192,256]{1,0:T(8,128)S(1)}, f32[192,256]{1,0:T(8,128)S(1)}, u32[]{:S(2)}, u32[]{:S(2)}) collective-permute-start(f32[192,256]{1,0:T(8,128)S(1)} %add.50), channel_id=1, source_target_pairs={{0,192},{64,0},{128,64},{192,128},{1,193},{65,1},{129,65},{193,129... | collective-permute-start | bytes 589832 | tf_op jit(solution)/shard_map/ppermute | solution.py:505
  71.9 8.6 %collective-permute-start.18 = (f32[96,256]{1,0:T(8,128)S(1)}, f32[96,256]{1,0:T(8,128)S(1)}, u32[]{:S(2)}, u32[]{:S(2)}) collective-permute-start(f32[96,256]{1,0:T(8,128)S(1)} %slice.8), channel_id=1, source_target_pairs={{0,32},{32,0},{1,33},{33,1},{2,34},{34,2},{3,35},{35,3},{4,36},{36... | collective-permute-start | bytes 294920 | tf_op jit(solution)/shard_map/ppermute | solution.py:489
  81.7 9.5 %collective-permute-start.19 = (f32[96,256]{1,0:T(8,128)S(1)}, f32[96,256]{1,0:T(8,128)S(1)}, u32[]{:S(2)}, u32[]{:S(2)}) collective-permute-start(f32[96,256]{1,0:T(8,128)S(1)} %get-tuple-element.43.product), channel_id=1, source_target_pairs={{0,32},{32,0},{1,33},{33,1},{2,34},{34,2},{3,35},{35,3},{4,36},{36... | collective-permute-start | bytes 294920 | tf_op jit(solution)/shard_map/ppermute | solution.py:489
  81.7 31.3 %all-to-all-start.4 = ((f32[16,48,256]{2,1,0:T(8,128)}), f32[16,48,256]{2,1,0:T(8,128)S(1)}, u32[]{:S(2)}, u32[]{:S(2)}) async-start(f32[16,48,256]{2,1,0:T(8,128)} %get-tuple-element.45), calls=%async_computation.4 | async-start | bytes 1572864 | tf_op jit(solution)/shard_map/all_to_all | solution.py:485
  91.7 7.3 %collective-permute-start.20 = (f32[200,256]{1,0:T(8,128)S(1)}, f32[200,256]{1,0:T(8,128)S(1)}, u32[]{:S(2)}, u32[]{:S(2)}) collective-permute-start(f32[200,256]{1,0:T(8,128)S(1)} %load.1.refs_4_.pair), channel_id=1, source_target_pairs={{0,192},{64,0},{128,64},{192,128},{1,193},{65,1},{129,65},{193,129... | collective-permute-start | bytes 614408 | tf_op jit(solution)/shard_map/ppermute | solution.py:497
  93.7 9.7 %collective-permute-start.21 = (f32[200,256]{1,0:T(8,128)S(1)}, f32[200,256]{1,0:T(8,128)S(1)}, u32[]{:S(2)}, u32[]{:S(2)}) collective-permute-start(f32[200,256]{1,0:T(8,128)S(1)} %load.1.refs_4_.pair), channel_id=1, source_target_pairs={{0,128},{64,192},{128,0},{192,64},{1,129},{65,193},{129,1},{193,65... | collective-permute-start | bytes 614408 | tf_op jit(solution)/shard_map/ppermute | solution.py:497
  94.5 10.4 %collective-permute-start.22 = (f32[200,256]{1,0:T(8,128)S(1)}, f32[200,256]{1,0:T(8,128)S(1)}, u32[]{:S(2)}, u32[]{:S(2)}) collective-permute-start(f32[200,256]{1,0:T(8,128)S(1)} %load.1.refs_4_.pair), channel_id=1, source_target_pairs={{0,64},{64,128},{128,192},{192,0},{1,65},{65,129},{129,193},{193,1... | collective-permute-start | bytes 614408 | tf_op jit(solution)/shard_map/ppermute | solution.py:497
  94.5 12.5 %collective-permute-start.23 = (f32[200,256]{1,0:T(8,128)S(1)}, f32[200,256]{1,0:T(8,128)S(1)}, u32[]{:S(2)}, u32[]{:S(2)}) collective-permute-start(f32[200,256]{1,0:T(8,128)S(1)} %load.1.refs_4_.pair), channel_id=1, source_target_pairs={{0,16},{16,0},{1,17},{17,1},{2,18},{18,2},{3,19},{19,3},{4,20},{20... | collective-permute-start | bytes 614408 | tf_op jit(solution)/shard_map/ppermute | solution.py:493
  99.0 8.0 %collective-permute-start.24 = (f32[200,256]{1,0:T(8,128)S(1)}, f32[200,256]{1,0:T(8,128)S(1)}, u32[]{:S(2)}, u32[]{:S(2)}) collective-permute-start(f32[200,256]{1,0:T(8,128)S(1)} %collective-permute-done.20.refs_5_), channel_id=1, source_target_pairs={{0,16},{16,0},{1,17},{17,1},{2,18},{18,2},{3,19},{19,3},{4,20},{20... | collective-permute-start | bytes 614408 | tf_op jit(solution)/shard_map/ppermute | solution.py:493
  113.1 31.1 %all-to-all-start.3 = ((f32[16,56,256]{2,1,0:T(8,128)}), f32[16,56,256]{2,1,0:T(8,128)S(1)}, u32[]{:S(2)}, u32[]{:S(2)}) async-start(f32[16,56,256]{2,1,0:T(8,128)} %rows_product.3), calls=%async_computation.3 | async-start | bytes 1835008 | tf_op jit(solution)/shard_map/all_to_all | solution.py:485
  125.1 5.1 %collective-permute-start.32 = (f32[192,256]{1,0:T(8,128)S(1)}, f32[192,256]{1,0:T(8,128)S(1)}, u32[]{:S(2)}, u32[]{:S(2)}) collective-permute-start(f32[192,256]{1,0:T(8,128)S(1)} %get-tuple-element.53), channel_id=1, source_target_pairs={{0,16},{16,0},{1,17},{17,1},{2,18},{18,2},{3,19},{19,3},{4,20},{20... | collective-permute-start | bytes 589832 | tf_op jit(solution)/shard_map/ppermute | solution.py:493
  125.5 6.7 %collective-permute-start.27 = (f32[192,256]{1,0:T(8,128)S(1)}, f32[192,256]{1,0:T(8,128)S(1)}, u32[]{:S(2)}, u32[]{:S(2)}) collective-permute-start(f32[192,256]{1,0:T(8,128)S(1)} %get-tuple-element.47), channel_id=1, source_target_pairs={{0,16},{16,0},{1,17},{17,1},{2,18},{18,2},{3,19},{19,3},{4,20},{20... | collective-permute-start | bytes 589832 | tf_op jit(solution)/shard_map/ppermute | solution.py:493
  126.1 7.4 %collective-permute-start.29 = (f32[192,256]{1,0:T(8,128)S(1)}, f32[192,256]{1,0:T(8,128)S(1)}, u32[]{:S(2)}, u32[]{:S(2)}) collective-permute-start(f32[192,256]{1,0:T(8,128)S(1)} %add.53), channel_id=1, source_target_pairs={{0,64},{64,128},{128,192},{192,0},{1,65},{65,129},{129,193},{193,1... | collective-permute-start | bytes 589832 | tf_op jit(solution)/shard_map/ppermute | solution.py:505
  126.5 12.8 %collective-permute-start.31 = (f32[192,256]{1,0:T(8,128)S(1)}, f32[192,256]{1,0:T(8,128)S(1)}, u32[]{:S(2)}, u32[]{:S(2)}) collective-permute-start(f32[192,256]{1,0:T(8,128)S(1)} %add.55), channel_id=1, source_target_pairs={{0,128},{64,192},{128,0},{192,64},{1,129},{65,193},{129,1},{193,65... | collective-permute-start | bytes 589832 | tf_op jit(solution)/shard_map/ppermute | solution.py:505
  130.3 9.0 %collective-permute-start.33 = (f32[192,256]{1,0:T(8,128)S(1)}, f32[192,256]{1,0:T(8,128)S(1)}, u32[]{:S(2)}, u32[]{:S(2)}) collective-permute-start(f32[192,256]{1,0:T(8,128)S(1)} %add.57), channel_id=1, source_target_pairs={{0,192},{64,0},{128,64},{192,128},{1,193},{65,1},{129,65},{193,129... | collective-permute-start | bytes 589832 | tf_op jit(solution)/shard_map/ppermute | solution.py:505
  139.4 21.8 %collective-permute-start.34 = (f32[96,256]{1,0:T(8,128)S(1)}, f32[96,256]{1,0:T(8,128)S(1)}, u32[]{:S(2)}, u32[]{:S(2)}) collective-permute-start(f32[96,256]{1,0:T(8,128)S(1)} %slice.9), channel_id=1, source_target_pairs={{0,32},{32,0},{1,33},{33,1},{2,34},{34,2},{3,35},{35,3},{4,36},{36... | collective-permute-start | bytes 294920 | tf_op jit(solution)/shard_map/ppermute | solution.py:489
  150.7 21.9 %all-to-all-start.5 = ((f32[128,2,128]{2,1,0:T(2,128)}), f32[128,2,128]{2,1,0:T(2,128)S(1)}, u32[]{:S(2)}, u32[]{:S(2)}) async-start(f32[128,2,128]{2,1,0:T(2,128)} %broadcast_in_dim.7), calls=%async_computation.5 | async-start | bytes 262144 | tf_op jit(solution)/shard_map/all_to_all | solution.py:485
  (11 other events, 65.9 us)

commit v5 on v4

--- a/solution.py
+++ b/solution.py
@@ -20,7 +20,7 @@
 MAXT = 48
 COUNT = 2 * MAXT
 PLACE = COUNT + 1
-UNROLL = 8
+UNROLL = 4
 F32 = jnp.float32
 BF16 = jnp.bfloat16
 HIGH = lax.Precision.HIGHEST
@@ -472,7 +472,6 @@
         in_specs=[vspec()] * 2,
         out_specs=vspec(),
         compiler_params=params(4),
-        cost_estimate=hint(5),
         name="last",
     )(part, far)
 

time: 174 us -> 175 us (level)
  waiting for transfers between devices: 39.8 us -> 42.2 us
  Pallas kernels: 29 us -> 26.9 us
    all_to_all x6, waiting for transfers between devices: 16.9 us -> 9.44 us  [swap(): return lax.all_to_all(x, axis, 0, 0, tiled=True)]
    ppermute x4, waiting for transfers between devices: 4.4 us -> 10 us  [other_half(): return lax.ppermute(x, 'zh', turned(2, 1))]
    ppermute x6, waiting for transfers between devices: 0.02 us -> 5.17 us  [spread(): lax.ppermute(mine, 'y', turned(4, -step))]
    ppermute x4, starting transfers between devices: 10.1 us -> 14.1 us  [other_half(): return lax.ppermute(x, 'zh', turned(2, 1))]
    ppermute x17, starting transfers between devices: 23.5 us -> 20.4 us  [other_core(): return lax.ppermute(x, 'core', turned(2, 1))]
  transfers between devices with their start and end apart: 42 -> 42, of which waited for: 14 -> 18; matrix products, arithmetic and copies ran while one was open for 2% -> 2% of each run, Pallas kernels for 16% -> 13%
where the time goes in v5:
time: 175 us
  starting transfers between devices  99.9 us (57%)
  waiting for transfers between devices  42.2 us (24%)
  Pallas kernels  26.9 us (15%)
  local copies, waits for them, and re-layouts  3.85 us (2%)
    all_to_all x6, starting transfers between devices, swap(): return lax.all_to_all(x, axis, 0, 0, tiled=True)  40 us
    ppermute x17, starting transfers between devices, other_core(): return lax.ppermute(x, 'core', turned(2, 1))  20.4 us
    ppermute x4, starting transfers between devices, other_half(): return lax.ppermute(x, 'zh', turned(2, 1))  14.1 us
    ppermute x6, waiting for transfers between devices, collect(): both = both + lax.ppermute(met[step], 'y', turned(4, step))  13.7 us
    ppermute x6, starting transfers between devices, collect(): both = both + lax.ppermute(met[step], 'y', turned(4, step))  13 us
    ppermute x4, waiting for transfers between devices, other_half(): return lax.ppermute(x, 'zh', turned(2, 1))  10 us
    all_to_all x6, waiting for transfers between devices, swap(): return lax.all_to_all(x, axis, 0, 0, tiled=True)  9.44 us
    pallas_call x2, Pallas kernels, rows_product(): pl.pallas_call(kernel, out_shape=jax.ShapeDtypeStruct((16, CAP * NV + RID...  8.86 us
  transfers between devices with their start and end apart: 42, of which 18 were waited for; matrix products, arithmetic and copies ran while one was open for 2% of the time, Pallas kernels for 13%

profile of v5, /device:TPU:1, one launch (start us, length us, event | category | flops | bytes accessed | tf_op | source)
XLA Modules:
  0.0 174.9 jit_solution(8133017086791280691)
XLA Ops:
  0.6 7.8 %collective-permute-start = (f32[16,1536]{1,0:T(8,128)}, f32[16,1536]{1,0:T(8,128)S(1)}, u32[]{:S(2)}, u32[]{:S(2)}) collective-permute-start(f32[16,1536]{1,0:T(8,128)} %mine.5), channel_id=1, source_target_pairs={{0,32},{32,0},{1,33},{33,1},{2,34},{34,2},{3,35},{35,3},{4,36},{36... | collective-permute-start | bytes 294920 | tf_op jit(solution)/shard_map/ppermute | solution.py:488
  10.2 3.5 %all-to-all-start.1 = ((f32[4,16,1536]{2,1,0:T(8,128)}), f32[4,16,1536]{2,1,0:T(8,128)S(1)}, u32[]{:S(2)}, u32[]{:S(2)}) async-start(f32[4,16,1536]{2,1,0:T(8,128)} %broadcast_in_dim.6), calls=%async_computation.1 | async-start | bytes 786432 | tf_op jit(solution)/shard_map/all_to_all | solution.py:484
  15.0 2.4 %prep.1 = (s32[2,48]{1,0:T(2,128)S(1)}, f32[16,8,256]{2,1,0:T(8,128)S(1)}) custom-call(s32[101]{0:T(128)S(1)} %concatenate.3.facts.refs_0_), custom_call_target="tpu_custom_call" | custom-call | flops 2000000000 | tf_op jit(solution)/shard_map/prep/pallas_call | solution.py:98
  17.5 2.3 %collective-permute-start.10 = (f32[16,8,256]{2,1,0:T(8,128)S(1)}, f32[16,8,256]{2,1,0:T(8,128)S(1)}, u32[]{:S(2)}, u32[]{:S(2)}) collective-permute-start(f32[16,8,256]{2,1,0:T(8,128)S(1)} %get-tuple-element.31.refs_2_.refs_0_), channel_id=1, source_target_pairs={{0,12},{4,0},{8,4},{12,8},{1,13},{5,1},{9,5},{13,9},{2,14},{6,2},{... | collective-permute-start | bytes 393224 | tf_op jit(solution)/shard_map/ppermute | solution.py:514
  19.8 2.1 %collective-permute-start.9 = (f32[16,8,256]{2,1,0:T(8,128)S(1)}, f32[16,8,256]{2,1,0:T(8,128)S(1)}, u32[]{:S(2)}, u32[]{:S(2)}) collective-permute-start(f32[16,8,256]{2,1,0:T(8,128)S(1)} %get-tuple-element.31.refs_2_.refs_0_), channel_id=1, source_target_pairs={{0,8},{4,12},{8,0},{12,4},{1,9},{5,13},{9,1},{13,5},{2,10},{6,14},... | collective-permute-start | bytes 393224 | tf_op jit(solution)/shard_map/ppermute | solution.py:514
  23.2 4.2 %collective-permute-start.1 = (f32[2,16,1536]{2,1,0:T(8,128)S(1)}, f32[2,16,1536]{2,1,0:T(8,128)S(1)}, u32[]{:S(2)}, u32[]{:S(2)}) collective-permute-start(f32[2,16,1536]{2,1,0:T(8,128)S(1)} %get-tuple-element.32.refs_4_), channel_id=1, source_target_pairs={{0,192},{64,0},{128,64},{192,128},{1,193},{65,1},{129,65},{193,129... | collective-permute-start | bytes 589832 | tf_op jit(solution)/shard_map/ppermute | solution.py:496
  29.9 3.5 %all-to-all-start.2 = ((f32[4,4,48,256]{3,2,1,0:T(8,128)}), f32[4,4,48,256]{3,2,1,0:T(8,128)S(1)}, u32[]{:S(2)}, u32[]{:S(2)}) async-start(f32[4,4,48,256]{3,2,1,0:T(8,128)} %pack.1), calls=%async_computation.2 | async-start | bytes 1572864 | tf_op jit(solution)/shard_map/all_to_all | solution.py:484
  37.2 2.1 %collective-permute-done.3.refs_7_ = f32[2,16,1536]{2,1,0:T(8,128)S(1)} collective-permute-done((f32[2,16,1536]{2,1,0:T(8,128)S(1)}, f32[2,16,1536]{2,1,0:T(8,128)S(1)}, u32[]{:S(2)}, u32[]{:S(2)}) %collective-permute-start.3) | collective-permute-done | bytes 196640 | tf_op jit(solution)/shard_map/ppermute | solution.py:496
  41.2 4.4 %rows_product.2 = f32[16,56,256]{2,1,0:T(8,128)} custom-call(s32[101]{0:T(128)S(1)} %concatenate.3.facts.refs_0_, s32[2,48]{1,0:T(2,128)S(1)} %get-tuple-element.30.refs_1_, f32[16,8,256]{2,1,0:T(8,128)S(1)} %get-tuple-element.31.refs_2_.refs_0_, f32[48,256,256]{2,1,0:T(8,128)} %bitcast.11, f32[2,16,1536]{2,1,0:T(8,128)S(1)} %get-tuple-element.32.refs_4_, ...), custom_call_target="tpu_custom_call" | custom-call | flops 4000000000 | tf_op jit(solution)/shard_map/rows_product/pallas_call | solution.py:252
  45.7 4.6 %all-to-all-start = ((f32[16,56,256]{2,1,0:T(8,128)}), f32[16,56,256]{2,1,0:T(8,128)S(1)}, u32[]{:S(2)}, u32[]{:S(2)}) async-start(f32[16,56,256]{2,1,0:T(8,128)} %rows_product.2), calls=%async_computation | async-start | bytes 1835008 | tf_op jit(solution)/shard_map/all_to_all | solution.py:484
  50.3 3.2 %cols_product.2 = (f32[192,256]{1,0:T(8,128)S(1)}, f32[192,256]{1,0:T(8,128)S(1)}, f32[192,256]{1,0:T(8,128)S(1)}, f32[192,256]{1,0:T(8,128)S(1)}, f32[192,256]{...) custom-call(s32[101]{0:T(128)S(1)} %concatenate.3.facts.refs_0_, ...), custom_call_target="tpu_custom_call" | custom-call | flops 5000000000 | tf_op jit(solution)/shard_map/cols_product/pallas_call | solution.py:266
  53.5 2.4 %collective-permute-start.12 = (f32[192,256]{1,0:T(8,128)S(1)}, f32[192,256]{1,0:T(8,128)S(1)}, u32[]{:S(2)}, u32[]{:S(2)}) collective-permute-start(f32[192,256]{1,0:T(8,128)S(1)} %get-tuple-element.38), channel_id=1, source_target_pairs={{0,16},{16,0},{1,17},{17,1},{2,18},{18,2},{3,19},{19,3},{4,20},{20... | collective-permute-start | bytes 589832 | tf_op jit(solution)/shard_map/ppermute | solution.py:492
  57.8 4.5 %collective-permute-start.15 = (f32[192,256]{1,0:T(8,128)S(1)}, f32[192,256]{1,0:T(8,128)S(1)}, u32[]{:S(2)}, u32[]{:S(2)}) collective-permute-start(f32[192,256]{1,0:T(8,128)S(1)} %add.48), channel_id=1, source_target_pairs={{0,128},{64,192},{128,0},{192,64},{1,129},{65,193},{129,1},{193,65... | collective-permute-start | bytes 589832 | tf_op jit(solution)/shard_map/ppermute | solution.py:504
  63.9 2.0 %collective-permute-done.13 = f32[192,256]{1,0:T(8,128)S(1)} collective-permute-done((f32[192,256]{1,0:T(8,128)S(1)}, f32[192,256]{1,0:T(8,128)S(1)}, u32[]{:S(2)}, u32[]{:S(2)}) %collective-permute-start.13) | collective-permute-done | bytes 196640 | tf_op jit(solution)/shard_map/ppermute | solution.py:504
  65.9 5.1 %collective-permute-done.15 = f32[192,256]{1,0:T(8,128)S(1)} collective-permute-done((f32[192,256]{1,0:T(8,128)S(1)}, f32[192,256]{1,0:T(8,128)S(1)}, u32[]{:S(2)}, u32[]{:S(2)}) %collective-permute-start.15) | collective-permute-done | bytes 196640 | tf_op jit(solution)/shard_map/ppermute | solution.py:504
  72.0 2.5 %all-to-all-done.from_x = f32[16,56,256]{2,1,0:T(8,128)S(1)} async-done(((f32[16,56,256]{2,1,0:T(8,128)}), f32[16,56,256]{2,1,0:T(8,128)S(1)}, u32[]{:S(2)}, u32[]{:S(2)}) %all-to-all-start) | async-done | bytes 917536 | tf_op jit(solution)/shard_map/all_to_all | solution.py:484
  75.0 3.6 %collective-permute-done.18.far_theirs = f32[96,256]{1,0:T(8,128)S(1)} collective-permute-done((f32[96,256]{1,0:T(8,128)S(1)}, f32[96,256]{1,0:T(8,128)S(1)}, u32[]{:S(2)}, u32[]{:S(2)}) %collective-permute-start.18) | collective-permute-done | bytes 98336 | tf_op jit(solution)/shard_map/ppermute | solution.py:488
  80.7 10.2 %all-to-all-start.4 = ((f32[16,48,256]{2,1,0:T(8,128)}), f32[16,48,256]{2,1,0:T(8,128)S(1)}, u32[]{:S(2)}, u32[]{:S(2)}) async-start(f32[16,48,256]{2,1,0:T(8,128)} %get-tuple-element.45), calls=%async_computation.4 | async-start | bytes 1572864 | tf_op jit(solution)/shard_map/all_to_all | solution.py:484
  91.3 2.6 %collective-permute-start.20 = (f32[200,256]{1,0:T(8,128)S(1)}, f32[200,256]{1,0:T(8,128)S(1)}, u32[]{:S(2)}, u32[]{:S(2)}) collective-permute-start(f32[200,256]{1,0:T(8,128)S(1)} %load.1.refs_4_.pair), channel_id=1, source_target_pairs={{0,192},{64,0},{128,64},{192,128},{1,193},{65,1},{129,65},{193,129... | collective-permute-start | bytes 614408 | tf_op jit(solution)/shard_map/ppermute | solution.py:496
  94.5 3.6 %collective-permute-start.23 = (f32[200,256]{1,0:T(8,128)S(1)}, f32[200,256]{1,0:T(8,128)S(1)}, u32[]{:S(2)}, u32[]{:S(2)}) collective-permute-start(f32[200,256]{1,0:T(8,128)S(1)} %load.1.refs_4_.pair), channel_id=1, source_target_pairs={{0,16},{16,0},{1,17},{17,1},{2,18},{18,2},{3,19},{19,3},{4,20},{20... | collective-permute-start | bytes 614408 | tf_op jit(solution)/shard_map/ppermute | solution.py:492
  100.0 3.7 %collective-permute-start.24 = (f32[200,256]{1,0:T(8,128)S(1)}, f32[200,256]{1,0:T(8,128)S(1)}, u32[]{:S(2)}, u32[]{:S(2)}) collective-permute-start(f32[200,256]{1,0:T(8,128)S(1)} %collective-permute-done.20.refs_5_), channel_id=1, source_target_pairs={{0,16},{16,0},{1,17},{17,1},{2,18},{18,2},{3,19},{19,3},{4,20},{20... | collective-permute-start | bytes 614408 | tf_op jit(solution)/shard_map/ppermute | solution.py:492
  108.2 4.4 %rows_product.3 = f32[16,56,256]{2,1,0:T(8,128)} custom-call(s32[101]{0:T(128)S(1)} %concatenate.3.facts.refs_0_, s32[2,48]{1,0:T(2,128)S(1)} %get-tuple-element.30.refs_1_, f32[16,8,256]{2,1,0:T(8,128)S(1)} %get-tuple-element.31.refs_2_.refs_0_, f32[48,256,256]{2,1,0:T(8,128)} %bitcast.13, f32[200,256]{1,0:T(8,128)S(1)} %load.1.refs_4_.pair, ...), custom_call_target="tpu_custom_call" | custom-call | flops 5000000000 | tf_op jit(solution)/shard_map/rows_product/pallas_call | solution.py:252
  113.4 6.2 %all-to-all-start.3 = ((f32[16,56,256]{2,1,0:T(8,128)}), f32[16,56,256]{2,1,0:T(8,128)S(1)}, u32[]{:S(2)}, u32[]{:S(2)}) async-start(f32[16,56,256]{2,1,0:T(8,128)} %rows_product.3), calls=%async_computation.3 | async-start | bytes 1835008 | tf_op jit(solution)/shard_map/all_to_all | solution.py:484
  119.6 3.2 %cols_product.3 = (f32[192,256]{1,0:T(8,128)S(1)}, f32[192,256]{1,0:T(8,128)S(1)}, f32[192,256]{1,0:T(8,128)S(1)}, f32[192,256]{1,0:T(8,128)S(1)}, f32[192,256]{...) custom-call(s32[101]{0:T(128)S(1)} %concatenate.3.facts.refs_0_, ...), custom_call_target="tpu_custom_call" | custom-call | flops 5000000000 | tf_op jit(solution)/shard_map/cols_product/pallas_call | solution.py:266
  125.1 3.9 %collective-permute-start.31 = (f32[192,256]{1,0:T(8,128)S(1)}, f32[192,256]{1,0:T(8,128)S(1)}, u32[]{:S(2)}, u32[]{:S(2)}) collective-permute-start(f32[192,256]{1,0:T(8,128)S(1)} %add.55), channel_id=1, source_target_pairs={{0,128},{64,192},{128,0},{192,64},{1,129},{65,193},{129,1},{193,65... | collective-permute-start | bytes 589832 | tf_op jit(solution)/shard_map/ppermute | solution.py:504
  129.1 1.9 %collective-permute-start.33 = (f32[192,256]{1,0:T(8,128)S(1)}, f32[192,256]{1,0:T(8,128)S(1)}, u32[]{:S(2)}, u32[]{:S(2)}) collective-permute-start(f32[192,256]{1,0:T(8,128)S(1)} %add.57), channel_id=1, source_target_pairs={{0,192},{64,0},{128,64},{192,128},{1,193},{65,1},{129,65},{193,129... | collective-permute-start | bytes 589832 | tf_op jit(solution)/shard_map/ppermute | solution.py:504
  132.2 5.4 %collective-permute-done.31 = f32[192,256]{1,0:T(8,128)S(1)} collective-permute-done((f32[192,256]{1,0:T(8,128)S(1)}, f32[192,256]{1,0:T(8,128)S(1)}, u32[]{:S(2)}, u32[]{:S(2)}) %collective-permute-start.31) | collective-permute-done | bytes 196640 | tf_op jit(solution)/shard_map/ppermute | solution.py:504
  137.6 6.2 %all-to-all-done.3.from_x = f32[16,56,256]{2,1,0:T(8,128)S(1)} async-done(((f32[16,56,256]{2,1,0:T(8,128)}), f32[16,56,256]{2,1,0:T(8,128)S(1)}, u32[]{:S(2)}, u32[]{:S(2)}) %all-to-all-start.3) | async-done | bytes 917536 | tf_op jit(solution)/shard_map/all_to_all | solution.py:484
  143.8 3.3 %finish.1 = (f32[16,1536]{1,0:T(8,128)}, f32[16,1536]{1,0:T(8,128)S(1)}, f32[2,128]{1,0:T(2,128)S(1)}) custom-call(f32[16,8,256]{2,1,0:T(8,128)S(1)} %get-tuple-element.33.wanted, f32[16,56,256]{2,1,0:T(8,128)S(1)} %all-to-all-done.3.from_x, f32[192,256]{1,0:T(8,128)S(1)} %add_add_fusion.both, f32[16,1536]{1,0:T(8,128)S(1)} %copy-done, ...), custom_call_target="tpu_custom_call" | custom-call | tf_op jit(solution)/shard_map/finish/pallas_call | solution.py:447
  150.3 12.0 %all-to-all-start.5 = ((f32[128,2,128]{2,1,0:T(2,128)}), f32[128,2,128]{2,1,0:T(2,128)S(1)}, u32[]{:S(2)}, u32[]{:S(2)}) async-start(f32[128,2,128]{2,1,0:T(2,128)} %broadcast_in_dim.7), calls=%async_computation.5 | async-start | bytes 262144 | tf_op jit(solution)/shard_map/all_to_all | solution.py:484
  162.3 4.6 %collective-permute-start.34 = (f32[96,256]{1,0:T(8,128)S(1)}, f32[96,256]{1,0:T(8,128)S(1)}, u32[]{:S(2)}, u32[]{:S(2)}) collective-permute-start(f32[96,256]{1,0:T(8,128)S(1)} %slice.9), channel_id=1, source_target_pairs={{0,32},{32,0},{1,33},{33,1},{2,34},{34,2},{3,35},{35,3},{4,36},{36... | collective-permute-start | bytes 294920 | tf_op jit(solution)/shard_map/ppermute | solution.py:488
  166.9 6.5 %collective-permute-done.34.far = f32[96,256]{1,0:T(8,128)S(1)} collective-permute-done((f32[96,256]{1,0:T(8,128)S(1)}, f32[96,256]{1,0:T(8,128)S(1)}, u32[]{:S(2)}, u32[]{:S(2)}) %collective-permute-start.34) | collective-permute-done | bytes 98336 | tf_op jit(solution)/shard_map/ppermute | solution.py:488
  (83 shorter events, 35.5 us)
Async XLA Ops:
  0.6 21.3 %collective-permute-start = (f32[16,1536]{1,0:T(8,128)}, f32[16,1536]{1,0:T(8,128)S(1)}, u32[]{:S(2)}, u32[]{:S(2)}) collective-permute-start(f32[16,1536]{1,0:T(8,128)} %mine.5), channel_id=1, source_target_pairs={{0,32},{32,0},{1,33},{33,1},{2,34},{34,2},{3,35},{35,3},{4,36},{36... | collective-permute-start | bytes 294920 | tf_op jit(solution)/shard_map/ppermute | solution.py:488
  10.2 17.9 %all-to-all-start.1 = ((f32[4,16,1536]{2,1,0:T(8,128)}), f32[4,16,1536]{2,1,0:T(8,128)S(1)}, u32[]{:S(2)}, u32[]{:S(2)}) async-start(f32[4,16,1536]{2,1,0:T(8,128)} %broadcast_in_dim.6), calls=%async_computation.1 | async-start | bytes 786432 | tf_op jit(solution)/shard_map/all_to_all | solution.py:484
  17.5 9.9 %collective-permute-start.10 = (f32[16,8,256]{2,1,0:T(8,128)S(1)}, f32[16,8,256]{2,1,0:T(8,128)S(1)}, u32[]{:S(2)}, u32[]{:S(2)}) collective-permute-start(f32[16,8,256]{2,1,0:T(8,128)S(1)} %get-tuple-element.31.refs_2_.refs_0_), channel_id=1, source_target_pairs={{0,12},{4,0},{8,4},{12,8},{1,13},{5,1},{9,5},{13,9},{2,14},{6,2},{... | collective-permute-start | bytes 393224 | tf_op jit(solution)/shard_map/ppermute | solution.py:514
  19.8 8.3 %collective-permute-start.8 = (f32[16,8,256]{2,1,0:T(8,128)S(1)}, f32[16,8,256]{2,1,0:T(8,128)S(1)}, u32[]{:S(2)}, u32[]{:S(2)}) collective-permute-start(f32[16,8,256]{2,1,0:T(8,128)S(1)} %get-tuple-element.31.refs_2_.refs_0_), channel_id=1, source_target_pairs={{0,4},{4,8},{8,12},{12,0},{1,5},{5,9},{9,13},{13,1},{2,6},{6,10},{... | collective-permute-start | bytes 393224 | tf_op jit(solution)/shard_map/ppermute | solution.py:514
  19.8 8.3 %collective-permute-start.9 = (f32[16,8,256]{2,1,0:T(8,128)S(1)}, f32[16,8,256]{2,1,0:T(8,128)S(1)}, u32[]{:S(2)}, u32[]{:S(2)}) collective-permute-start(f32[16,8,256]{2,1,0:T(8,128)S(1)} %get-tuple-element.31.refs_2_.refs_0_), channel_id=1, source_target_pairs={{0,8},{4,12},{8,0},{12,4},{1,9},{5,13},{9,1},{13,5},{2,10},{6,14},... | collective-permute-start | bytes 393224 | tf_op jit(solution)/shard_map/ppermute | solution.py:514
  23.2 12.7 %collective-permute-start.1 = (f32[2,16,1536]{2,1,0:T(8,128)S(1)}, f32[2,16,1536]{2,1,0:T(8,128)S(1)}, u32[]{:S(2)}, u32[]{:S(2)}) collective-permute-start(f32[2,16,1536]{2,1,0:T(8,128)S(1)} %get-tuple-element.32.refs_4_), channel_id=1, source_target_pairs={{0,192},{64,0},{128,64},{192,128},{1,193},{65,1},{129,65},{193,129... | collective-permute-start | bytes 589832 | tf_op jit(solution)/shard_map/ppermute | solution.py:496
  27.4 9.3 %collective-permute-start.2 = (f32[2,16,1536]{2,1,0:T(8,128)S(1)}, f32[2,16,1536]{2,1,0:T(8,128)S(1)}, u32[]{:S(2)}, u32[]{:S(2)}) collective-permute-start(f32[2,16,1536]{2,1,0:T(8,128)S(1)} %get-tuple-element.32.refs_4_), channel_id=1, source_target_pairs={{0,128},{64,192},{128,0},{192,64},{1,129},{65,193},{129,1},{193,65... | collective-permute-start | bytes 589832 | tf_op jit(solution)/shard_map/ppermute | solution.py:496
  27.4 11.9 %collective-permute-start.3 = (f32[2,16,1536]{2,1,0:T(8,128)S(1)}, f32[2,16,1536]{2,1,0:T(8,128)S(1)}, u32[]{:S(2)}, u32[]{:S(2)}) collective-permute-start(f32[2,16,1536]{2,1,0:T(8,128)S(1)} %get-tuple-element.32.refs_4_), channel_id=1, source_target_pairs={{0,64},{64,128},{128,192},{192,0},{1,65},{65,129},{129,193},{193,1... | collective-permute-start | bytes 589832 | tf_op jit(solution)/shard_map/ppermute | solution.py:496
  29.9 15.8 %all-to-all-start.2 = ((f32[4,4,48,256]{3,2,1,0:T(8,128)}), f32[4,4,48,256]{3,2,1,0:T(8,128)S(1)}, u32[]{:S(2)}, u32[]{:S(2)}) async-start(f32[4,4,48,256]{3,2,1,0:T(8,128)} %pack.1), calls=%async_computation.2 | async-start | bytes 1572864 | tf_op jit(solution)/shard_map/all_to_all | solution.py:484
  33.4 6.8 %collective-permute-start.4 = (f32[2,16,1536]{2,1,0:T(8,128)S(1)}, f32[2,16,1536]{2,1,0:T(8,128)S(1)}, u32[]{:S(2)}, u32[]{:S(2)}) collective-permute-start(f32[2,16,1536]{2,1,0:T(8,128)S(1)} %get-tuple-element.32.refs_4_), channel_id=1, source_target_pairs={{0,16},{16,0},{1,17},{17,1},{2,18},{18,2},{3,19},{19,3},{4,20},{20... | collective-permute-start | bytes 589832 | tf_op jit(solution)/shard_map/ppermute | solution.py:492
  45.7 28.8 %all-to-all-start = ((f32[16,56,256]{2,1,0:T(8,128)}), f32[16,56,256]{2,1,0:T(8,128)S(1)}, u32[]{:S(2)}, u32[]{:S(2)}) async-start(f32[16,56,256]{2,1,0:T(8,128)} %rows_product.2), calls=%async_computation | async-start | bytes 1835008 | tf_op jit(solution)/shard_map/all_to_all | solution.py:484
  56.1 6.2 %collective-permute-start.16 = (f32[192,256]{1,0:T(8,128)S(1)}, f32[192,256]{1,0:T(8,128)S(1)}, u32[]{:S(2)}, u32[]{:S(2)}) collective-permute-start(f32[192,256]{1,0:T(8,128)S(1)} %get-tuple-element.42), channel_id=1, source_target_pairs={{0,16},{16,0},{1,17},{17,1},{2,18},{18,2},{3,19},{19,3},{4,20},{20... | collective-permute-start | bytes 589832 | tf_op jit(solution)/shard_map/ppermute | solution.py:492
  56.5 7.4 %collective-permute-start.11 = (f32[192,256]{1,0:T(8,128)S(1)}, f32[192,256]{1,0:T(8,128)S(1)}, u32[]{:S(2)}, u32[]{:S(2)}) collective-permute-start(f32[192,256]{1,0:T(8,128)S(1)} %get-tuple-element.36), channel_id=1, source_target_pairs={{0,16},{16,0},{1,17},{17,1},{2,18},{18,2},{3,19},{19,3},{4,20},{20... | collective-permute-start | bytes 589832 | tf_op jit(solution)/shard_map/ppermute | solution.py:492
  57.1 8.9 %collective-permute-start.13 = (f32[192,256]{1,0:T(8,128)S(1)}, f32[192,256]{1,0:T(8,128)S(1)}, u32[]{:S(2)}, u32[]{:S(2)}) collective-permute-start(f32[192,256]{1,0:T(8,128)S(1)} %add.46), channel_id=1, source_target_pairs={{0,64},{64,128},{128,192},{192,0},{1,65},{65,129},{129,193},{193,1... | collective-permute-start | bytes 589832 | tf_op jit(solution)/shard_map/ppermute | solution.py:504
  57.8 13.2 %collective-permute-start.15 = (f32[192,256]{1,0:T(8,128)S(1)}, f32[192,256]{1,0:T(8,128)S(1)}, u32[]{:S(2)}, u32[]{:S(2)}) collective-permute-start(f32[192,256]{1,0:T(8,128)S(1)} %add.48), channel_id=1, source_target_pairs={{0,128},{64,192},{128,0},{192,64},{1,129},{65,193},{129,1},{193,65... | collective-permute-start | bytes 589832 | tf_op jit(solution)/shard_map/ppermute | solution.py:504
  62.3 8.7 %collective-permute-start.17 = (f32[192,256]{1,0:T(8,128)S(1)}, f32[192,256]{1,0:T(8,128)S(1)}, u32[]{:S(2)}, u32[]{:S(2)}) collective-permute-start(f32[192,256]{1,0:T(8,128)S(1)} %add.50), channel_id=1, source_target_pairs={{0,192},{64,0},{128,64},{192,128},{1,193},{65,1},{129,65},{193,129... | collective-permute-start | bytes 589832 | tf_op jit(solution)/shard_map/ppermute | solution.py:504
  71.1 7.5 %collective-permute-start.18 = (f32[96,256]{1,0:T(8,128)S(1)}, f32[96,256]{1,0:T(8,128)S(1)}, u32[]{:S(2)}, u32[]{:S(2)}) collective-permute-start(f32[96,256]{1,0:T(8,128)S(1)} %slice.8), channel_id=1, source_target_pairs={{0,32},{32,0},{1,33},{33,1},{2,34},{34,2},{3,35},{35,3},{4,36},{36... | collective-permute-start | bytes 294920 | tf_op jit(solution)/shard_map/ppermute | solution.py:488
  79.9 11.0 %collective-permute-start.19 = (f32[96,256]{1,0:T(8,128)S(1)}, f32[96,256]{1,0:T(8,128)S(1)}, u32[]{:S(2)}, u32[]{:S(2)}) collective-permute-start(f32[96,256]{1,0:T(8,128)S(1)} %get-tuple-element.43.product), channel_id=1, source_target_pairs={{0,32},{32,0},{1,33},{33,1},{2,34},{34,2},{3,35},{35,3},{4,36},{36... | collective-permute-start | bytes 294920 | tf_op jit(solution)/shard_map/ppermute | solution.py:488
  80.7 32.7 %all-to-all-start.4 = ((f32[16,48,256]{2,1,0:T(8,128)}), f32[16,48,256]{2,1,0:T(8,128)S(1)}, u32[]{:S(2)}, u32[]{:S(2)}) async-start(f32[16,48,256]{2,1,0:T(8,128)} %get-tuple-element.45), calls=%async_computation.4 | async-start | bytes 1572864 | tf_op jit(solution)/shard_map/all_to_all | solution.py:484
  91.3 8.6 %collective-permute-start.20 = (f32[200,256]{1,0:T(8,128)S(1)}, f32[200,256]{1,0:T(8,128)S(1)}, u32[]{:S(2)}, u32[]{:S(2)}) collective-permute-start(f32[200,256]{1,0:T(8,128)S(1)} %load.1.refs_4_.pair), channel_id=1, source_target_pairs={{0,192},{64,0},{128,64},{192,128},{1,193},{65,1},{129,65},{193,129... | collective-permute-start | bytes 614408 | tf_op jit(solution)/shard_map/ppermute | solution.py:496
  93.9 9.7 %collective-permute-start.21 = (f32[200,256]{1,0:T(8,128)S(1)}, f32[200,256]{1,0:T(8,128)S(1)}, u32[]{:S(2)}, u32[]{:S(2)}) collective-permute-start(f32[200,256]{1,0:T(8,128)S(1)} %load.1.refs_4_.pair), channel_id=1, source_target_pairs={{0,128},{64,192},{128,0},{192,64},{1,129},{65,193},{129,1},{193,65... | collective-permute-start | bytes 614408 | tf_op jit(solution)/shard_map/ppermute | solution.py:496
  94.0 11.7 %collective-permute-start.22 = (f32[200,256]{1,0:T(8,128)S(1)}, f32[200,256]{1,0:T(8,128)S(1)}, u32[]{:S(2)}, u32[]{:S(2)}) collective-permute-start(f32[200,256]{1,0:T(8,128)S(1)} %load.1.refs_4_.pair), channel_id=1, source_target_pairs={{0,64},{64,128},{128,192},{192,0},{1,65},{65,129},{129,193},{193,1... | collective-permute-start | bytes 614408 | tf_op jit(solution)/shard_map/ppermute | solution.py:496
  94.5 12.6 %collective-permute-start.23 = (f32[200,256]{1,0:T(8,128)S(1)}, f32[200,256]{1,0:T(8,128)S(1)}, u32[]{:S(2)}, u32[]{:S(2)}) collective-permute-start(f32[200,256]{1,0:T(8,128)S(1)} %load.1.refs_4_.pair), channel_id=1, source_target_pairs={{0,16},{16,0},{1,17},{17,1},{2,18},{18,2},{3,19},{19,3},{4,20},{20... | collective-permute-start | bytes 614408 | tf_op jit(solution)/shard_map/ppermute | solution.py:492
  100.0 7.2 %collective-permute-start.24 = (f32[200,256]{1,0:T(8,128)S(1)}, f32[200,256]{1,0:T(8,128)S(1)}, u32[]{:S(2)}, u32[]{:S(2)}) collective-permute-start(f32[200,256]{1,0:T(8,128)S(1)} %collective-permute-done.20.refs_5_), channel_id=1, source_target_pairs={{0,16},{16,0},{1,17},{17,1},{2,18},{18,2},{3,19},{19,3},{4,20},{20... | collective-permute-start | bytes 614408 | tf_op jit(solution)/shard_map/ppermute | solution.py:492
  113.4 30.4 %all-to-all-start.3 = ((f32[16,56,256]{2,1,0:T(8,128)}), f32[16,56,256]{2,1,0:T(8,128)S(1)}, u32[]{:S(2)}, u32[]{:S(2)}) async-start(f32[16,56,256]{2,1,0:T(8,128)} %rows_product.3), calls=%async_computation.3 | async-start | bytes 1835008 | tf_op jit(solution)/shard_map/all_to_all | solution.py:484
  123.7 5.3 %collective-permute-start.32 = (f32[192,256]{1,0:T(8,128)S(1)}, f32[192,256]{1,0:T(8,128)S(1)}, u32[]{:S(2)}, u32[]{:S(2)}) collective-permute-start(f32[192,256]{1,0:T(8,128)S(1)} %get-tuple-element.53), channel_id=1, source_target_pairs={{0,16},{16,0},{1,17},{17,1},{2,18},{18,2},{3,19},{19,3},{4,20},{20... | collective-permute-start | bytes 589832 | tf_op jit(solution)/shard_map/ppermute | solution.py:492
  124.1 6.9 %collective-permute-start.27 = (f32[192,256]{1,0:T(8,128)S(1)}, f32[192,256]{1,0:T(8,128)S(1)}, u32[]{:S(2)}, u32[]{:S(2)}) collective-permute-start(f32[192,256]{1,0:T(8,128)S(1)} %get-tuple-element.47), channel_id=1, source_target_pairs={{0,16},{16,0},{1,17},{17,1},{2,18},{18,2},{3,19},{19,3},{4,20},{20... | collective-permute-start | bytes 589832 | tf_op jit(solution)/shard_map/ppermute | solution.py:492
  124.7 7.5 %collective-permute-start.29 = (f32[192,256]{1,0:T(8,128)S(1)}, f32[192,256]{1,0:T(8,128)S(1)}, u32[]{:S(2)}, u32[]{:S(2)}) collective-permute-start(f32[192,256]{1,0:T(8,128)S(1)} %add.53), channel_id=1, source_target_pairs={{0,64},{64,128},{128,192},{192,0},{1,65},{65,129},{129,193},{193,1... | collective-permute-start | bytes 589832 | tf_op jit(solution)/shard_map/ppermute | solution.py:504
  125.1 12.4 %collective-permute-start.31 = (f32[192,256]{1,0:T(8,128)S(1)}, f32[192,256]{1,0:T(8,128)S(1)}, u32[]{:S(2)}, u32[]{:S(2)}) collective-permute-start(f32[192,256]{1,0:T(8,128)S(1)} %add.55), channel_id=1, source_target_pairs={{0,128},{64,192},{128,0},{192,64},{1,129},{65,193},{129,1},{193,65... | collective-permute-start | bytes 589832 | tf_op jit(solution)/shard_map/ppermute | solution.py:504
  129.1 8.5 %collective-permute-start.33 = (f32[192,256]{1,0:T(8,128)S(1)}, f32[192,256]{1,0:T(8,128)S(1)}, u32[]{:S(2)}, u32[]{:S(2)}) collective-permute-start(f32[192,256]{1,0:T(8,128)S(1)} %add.57), channel_id=1, source_target_pairs={{0,192},{64,0},{128,64},{192,128},{1,193},{65,1},{129,65},{193,129... | collective-permute-start | bytes 589832 | tf_op jit(solution)/shard_map/ppermute | solution.py:504
  150.3 23.7 %all-to-all-start.5 = ((f32[128,2,128]{2,1,0:T(2,128)}), f32[128,2,128]{2,1,0:T(2,128)S(1)}, u32[]{:S(2)}, u32[]{:S(2)}) async-start(f32[128,2,128]{2,1,0:T(2,128)} %broadcast_in_dim.7), calls=%async_computation.5 | async-start | bytes 262144 | tf_op jit(solution)/shard_map/all_to_all | solution.py:484
  162.3 11.0 %collective-permute-start.34 = (f32[96,256]{1,0:T(8,128)S(1)}, f32[96,256]{1,0:T(8,128)S(1)}, u32[]{:S(2)}, u32[]{:S(2)}) collective-permute-start(f32[96,256]{1,0:T(8,128)S(1)} %slice.9), channel_id=1, source_target_pairs={{0,32},{32,0},{1,33},{33,1},{2,34},{34,2},{3,35},{35,3},{4,36},{36... | collective-permute-start | bytes 294920 | tf_op jit(solution)/shard_map/ppermute | solution.py:488
  (11 other events, 67.4 us)
